TPU v7x, 128 devices: a whole 4x4x4 slice. The times are simulated.
128 devices in a mesh: dp: 16 (over x, z_hi, core), expert: 8 (over y, z_lo).
Axes of the slice: x: 4, y: 4, z: 4 (z_hi: 2, z_lo: 2; z = z_hi * 2 + z_lo), core: 2. Of those that a mesh axis runs over, the one named last changes fastest.
Arguments:
- tokens: bfloat16 [16384, 2880], P(('dp', 'expert')), may hold values from -6 to 6
- expert_ids: int32 [16384, 4], P(('dp', 'expert')), may hold values from 0 to 63, all different within a row
- gate_raw: float32 [16384, 4], P(('dp', 'expert')), may hold values from 0.1 to 1
- overflow_shift: int32 [16384, 4], P(('dp', 'expert')), may hold values from 1 to 63
- limits: int32 [64], replicated, may hold values from 6 to 12, as said below
- gate_w: bfloat16 [128, 2880, 768], P(('dp', 'expert')), may hold values from -0.109375 to 0.109375
- up_w: bfloat16 [128, 2880, 768], P(('dp', 'expert')), may hold values from -0.109375 to 0.109375
- down_w: bfloat16 [128, 768, 2880], P(('dp', 'expert')), may hold values from -0.15625 to 0.15625
- context: bfloat16 [16384, 4096], P('dp', 'expert'), may hold values from -6 to 6
- out_grad: bfloat16 [16384, 2880], P(('dp', 'expert')), may hold values from -0.059814453 to 0.059814453
Outputs:
- mixed: bfloat16 [16384, 2880], P(('dp', 'expert'))
- proj_grad: float32 [4096, 2880], P('expert')
Inputs may be any that keep to these rules, and one draw needn't show every extreme that they name: `limits`: each expert has between 6 and 12 first-choice slots.
All inputs are finite; a program needn't handle non-finite values.
Results may differ from a plain program's by a relative error of at most 0.023.
Values may be sent and summed in bfloat16 or wider, within the bound.
No kernel may reach another device: no remote copies, remote signals or barrier semaphores. Data moves between devices by JAX's collectives and lax.ppermute only.
A program may use at most 192 MiB of HBM per device.

v0:
```python
import jax
import jax.numpy as jnp
from jax import lax
from jax.sharding import PartitionSpec as P


def place_slots(expert_ids, overflow_shift, limits, capacity):
    experts = limits.shape[0]
    flat_ids = expert_ids.reshape(-1)
    shifts = overflow_shift.reshape(-1)
    labels = jnp.arange(experts, dtype=jnp.int32)
    first_hot = (flat_ids[:, None] == labels[None, :]).astype(jnp.int32)
    first_before = jnp.cumsum(first_hot, axis=0, dtype=jnp.int32) - first_hot
    first_rank = jnp.sum(first_before * first_hot, axis=1, dtype=jnp.int32)
    first_limit = jnp.sum(first_hot * limits[None, :], axis=1, dtype=jnp.int32)
    spilled = first_rank >= first_limit
    second = (flat_ids + shifts) % experts
    second_any = (second[:, None] == labels[None, :]).astype(jnp.int32)
    second_hot = second_any * spilled.astype(jnp.int32)[:, None]
    second_before = jnp.cumsum(second_hot, axis=0, dtype=jnp.int32) - second_hot
    second_rank = jnp.sum(second_before * second_hot, axis=1, dtype=jnp.int32)
    second_limit = jnp.sum(second_any * limits[None, :], axis=1, dtype=jnp.int32)
    target = jnp.where(spilled, second, flat_ids)
    slot_index = jnp.where(spilled, second_limit + second_rank, first_rank)
    return (target, slot_index, slot_index < capacity)


def expert_part(token_rows, gate_half, up_half, down_half):
    gating = jnp.dot(token_rows, gate_half, preferred_element_type=jnp.float32)
    upward = jnp.dot(token_rows, up_half, preferred_element_type=jnp.float32)
    active = ((upward + 1.0) * gating * jax.nn.sigmoid(1.702 * gating)).astype(jnp.bfloat16)
    return jnp.dot(active, down_half, preferred_element_type=jnp.float32).astype(jnp.bfloat16)


def local(
    tokens, expert_ids, gate_raw, overflow_shift, limits, gate_w, up_w, down_w, context, out_grad
):
    tok_count, width = tokens.shape
    top_count = expert_ids.shape[1]
    expert_count = limits.shape[0]
    capacity = max(2, 3 * tok_count * top_count // (2 * expert_count))
    target, slot_index, is_kept = place_slots(expert_ids, overflow_shift, limits, capacity)
    where_to = jnp.where(is_kept, target * capacity + slot_index, expert_count * capacity)
    repeated = jnp.repeat(tokens, top_count, axis=0)
    buffer = (
        jnp.zeros((expert_count * capacity, width), tokens.dtype)
        .at[where_to]
        .set(repeated, mode="drop")
    )
    outgoing = jnp.repeat(buffer.reshape(expert_count, capacity, width), 2, axis=0)
    incoming = lax.all_to_all(outgoing, ("dp", "expert"), split_axis=0, concat_axis=0, tiled=True)
    sources, slot_count, _ = incoming.shape
    partial_value = expert_part(
        incoming.reshape(sources * slot_count, width), gate_w[0], up_w[0], down_w[0]
    )
    returned = lax.all_to_all(
        partial_value.reshape(sources, slot_count, width),
        ("dp", "expert"),
        split_axis=0,
        concat_axis=0,
        tiled=True,
    )
    pair_parts = returned.reshape(expert_count, 2, capacity, width).astype(jnp.float32)
    expert_out = (pair_parts[:, 0] + pair_parts[:, 1]).reshape(expert_count * capacity, width)
    gate_share = gate_raw / jnp.sum(gate_raw, axis=1, keepdims=True)
    weight = jnp.where(is_kept, gate_share.reshape(-1), 0.0)
    fetched = expert_out[jnp.minimum(where_to, expert_count * capacity - 1)]
    mixed = jnp.sum(
        (weight[:, None] * fetched).reshape(tok_count, top_count, width), axis=1
    ).astype(jnp.bfloat16)
    local_grad = lax.dot_general(
        context,
        lax.all_gather(out_grad, "expert", axis=0, tiled=True),
        (((0,), (0,)), ((), ())),
        preferred_element_type=jnp.float32,
    )
    proj_grad = lax.psum(local_grad.astype(jnp.bfloat16), "dp").astype(jnp.float32)
    return (mixed, proj_grad)


def solution(mesh):
    in_specs = (
        P(("dp", "expert"), None),
        P(("dp", "expert"), None),
        P(("dp", "expert"), None),
        P(("dp", "expert"), None),
        P(),
        P(("dp", "expert"), None, None),
        P(("dp", "expert"), None, None),
        P(("dp", "expert"), None, None),
        P("dp", "expert"),
        P(("dp", "expert"), None),
    )
    out_specs = (P(("dp", "expert"), None), P("expert", None))
    return jax.shard_map(local, mesh=mesh, in_specs=in_specs, out_specs=out_specs, check_vma=False)
```

profile of v0, /device:TPU:5, one launch (start us, length us, event | category | flops | bytes accessed | tf_op | source)
XLA Modules:
  0.0 659.2 jit_solution(663156621871088890)
XLA Ops:
  9.5 1.2 reduce-window.14
  14.2 1.5 copy.62
  15.6 2.4 broadcast_in_dim.30
  18.0 5.6 reshape.290
  23.6 8.8 %scatter_custom_fusion = bf16[768,2880]{1,0:T(8,128)(2,1)} fusion(s32[512]{0:T(512)S(1)} %bitcast.72, bf16[512,2880]{1,0:T(8,128)(2,1)} %reshape.290, bf16[]{:T(256)} %constant.35.clone.1), kind=kCustom, calls=%fused_computation.16 | custom fusion | bytes 4424192 | tf_op jit(solution)/shard_map/scatter | solution.py:48
  32.4 7.3 %reshape.272 = bf16[64,12,2880]{2,1,0:T(8,128)(2,1)} reshape(bf16[768,2880]{1,0:T(8,128)(2,1)} %scatter_custom_fusion) | data formatting | bytes 8847360 | tf_op jit(solution)/shard_map/reshape | solution.py:50
  39.8 8.0 %broadcast_in_dim.31 = bf16[64,2,12,2880]{3,2,1,0:T(8,128)(2,1)} broadcast(bf16[64,12,2880]{2,1,0:T(8,128)(2,1)} %reshape.272), dimensions={0,2,3} | broadcast | bytes 13271040 | tf_op jit(solution)/shard_map/broadcast_in_dim | solution.py:50
  47.7 11.2 %all-to-all-start = ((bf16[128,12,2880]{2,1,0:T(8,128)(2,1)}), bf16[128,12,2880]{2,1,0:T(8,128)(2,1)}, u32[]{:S(2)}, u32[]{:S(2)}) async-start(bf16[128,12,2880]{2,1,0:T(8,128)(2,1)} %bitcast.66), calls=%async_computation | async-start | bytes 24117248 | tf_op jit(solution)/shard_map/all_to_all | solution.py:51
  59.7 170.5 %all-to-all-done = bf16[128,12,2880]{2,1,0:T(8,128)(2,1)} async-done(((bf16[128,12,2880]{2,1,0:T(8,128)(2,1)}), bf16[128,12,2880]{2,1,0:T(8,128)(2,1)}, u32[]{:S(2)}, u32[]{:S(2)}) %all-to-all-start) | async-done | bytes 8847392 | tf_op jit(solution)/shard_map/all_to_all | solution.py:51
  230.2 14.6 %reshape.274 = bf16[1536,2880]{1,0:T(8,128)(2,1)} reshape(bf16[128,12,2880]{2,1,0:T(8,128)(2,1)} %all-to-all-done) | data formatting | bytes 17694720 | tf_op jit(solution)/shard_map/reshape | solution.py:54
  244.8 12.7 %fusion.2 = f32[1536,768]{1,0:T(8,128)} fusion(bf16[1536,2880]{1,0:T(8,128)(2,1)} %reshape.274, bf16[1,2880,768]{2,1,0:T(8,128)(2,1)} %param.15), kind=kOutput, calls=%fused_computation.10 | convolution fusion | flops 6794772480 | bytes 17989632 | tf_op jit(solution)/shard_map/dot_general | solution.py:29
  257.4 23.7 %convolution_convert_fusion = bf16[1536,2880]{0,1:T(8,128)(2,1)} fusion(bf16[1,768,2880]{1,2,0:T(8,128)(2,1)} %param.17, f32[1536,768]{1,0:T(8,128)} %fusion.2, bf16[1536,2880]{1,0:T(8,128)(2,1)} %reshape.274, bf16[1,2880,768]{2,1,0:T(8,128)(2,1)} %param.16), kind=kOutput, calls=%fused_computation.5 | convolution fusion | flops 13603405824 | bytes 31260672 | tf_op jit(solution)/shard_map/dot_general | solution.py:32
  281.2 12.5 %copy.63 = bf16[1536,2880]{1,0:T(8,128)(2,1)} copy(bf16[1536,2880]{0,1:T(8,128)(2,1)} %convolution_convert_fusion) | data formatting | bytes 17694720 | tf_op jit(solution)/shard_map/convert_element_type | solution.py:32
  293.6 13.5 %reshape.275 = bf16[128,12,2880]{2,1,0:T(8,128)(2,1)} reshape(bf16[1536,2880]{1,0:T(8,128)(2,1)} %copy.63) | data formatting | bytes 17694720 | tf_op jit(solution)/shard_map/reshape | solution.py:57
  307.1 19.7 %all-to-all-start.1 = ((bf16[128,12,2880]{2,1,0:T(8,128)(2,1)}), bf16[128,12,2880]{2,1,0:T(8,128)(2,1)}, u32[]{:S(2)}, u32[]{:S(2)}) async-start(bf16[128,12,2880]{2,1,0:T(8,128)(2,1)} %reshape.275), calls=%async_computation.1 | async-start | bytes 24117248 | tf_op jit(solution)/shard_map/all_to_all | solution.py:56
  327.2 7.2 %convolution_convert_fusion.1 = bf16[512,2880]{0,1:T(8,128)(2,1)} fusion(bf16[1024,2880]{0,1:T(8,128)(2,1)} %all-gather.2.cloned.1.call-done, bf16[1024,512]{1,0:T(8,128)(2,1)S(1)} %copy-done), kind=kOutput, calls=%fused_computation.8 | convolution fusion | flops 3021373440 | bytes 9895936 | tf_op jit(solution)/shard_map/dot_general | solution.py:71
  335.1 263.7 %all-reduce.2.cloned.1.call-done = bf16[512,2880]{0,1:T(8,128)(2,1)} async-done(((bf16[512,2880]{0,1:T(8,128)(2,1)}), bf16[512,2880]{0,1:T(8,128)(2,1)}) %all-reduce.2.cloned.1.call-update) | async-done | bytes 2949136 | tf_op jit(solution)/shard_map/psum | solution.py:77
  598.8 5.2 convert_element_type.53
  604.1 6.7 %convert.2 = f32[64,2,12,2880]{3,2,1,0:T(8,128)S(1)} convert(bf16[64,2,12,2880]{3,2,1,0:T(8,128)(2,1)} %bitcast.12) | non-fusion elementwise | flops 4423680 | bytes 26542080 | tf_op jit(solution)/shard_map/convert_element_type | solution.py:63
  610.8 4.9 fusion
  615.8 10.2 %add.133 = f32[768,2880]{1,0:T(8,128)} reshape(f32[64,1,12,2880]{3,2,0,1:T(8,128)} %fusion) | data formatting | bytes 17694720 | tf_op jit(solution)/shard_map/add | solution.py:64
  625.9 10.6 %gather_fusion = f32[512,2880]{1,0:T(8,128)} fusion(f32[768,2880]{1,0:T(8,128)} %add.133, s32[1024]{0:T(1024)S(1)} %pad_clamp_fusion), kind=kCustom, calls=%fused_computation | custom fusion | bytes 11798528 | tf_op jit(solution)/shard_map/gather | solution.py:67
  636.5 7.6 %gather.6 = f32[128,4,2880]{2,1,0:T(4,128)} reshape(f32[512,2880]{1,0:T(8,128)} %gather_fusion) | data formatting | bytes 11796480 | tf_op jit(solution)/shard_map/gather | solution.py:67
  644.1 7.1 %multiply_reduce_fusion = bf16[128,2880]{1,0:T(8,128)(2,1)S(1)} fusion(f32[128,4,2880]{2,1,0:T(4,128)} %gather.6, f32[128,4]{1,0:T(8,128)S(1)} %copy.59), kind=kLoop, calls=%fused_computation.6 | loop fusion | flops 2580480 | bytes 6637568 | tf_op jit(solution)/shard_map/reduce_sum | solution.py:68
  (46 shorter events, 8.6 us)
Async XLA Ops:
  7.2 320.0 %copy-start = (bf16[1024,512]{1,0:T(8,128)(2,1)S(1)}, bf16[1024,512]{1,0:T(8,128)(2,1)}, u32[]{:S(2)}) copy-start(bf16[1024,512]{1,0:T(8,128)(2,1)} %param.18) | copy-start | bytes 3145732
  47.7 182.4 %all-to-all-start = ((bf16[128,12,2880]{2,1,0:T(8,128)(2,1)}), bf16[128,12,2880]{2,1,0:T(8,128)(2,1)}, u32[]{:S(2)}, u32[]{:S(2)}) async-start(bf16[128,12,2880]{2,1,0:T(8,128)(2,1)} %bitcast.66), calls=%async_computation | async-start | bytes 24117248 | tf_op jit(solution)/shard_map/all_to_all | solution.py:51
  59.0 268.2 %all-gather.2.cloned.1.call-start = ((), (), s32[]{:S(2)}) async-start(), calls=%async_computation.2 | async-start | bytes 6635520 | tf_op jit(solution)/shard_map/all_gather | solution.py:73
  307.1 297.0 %all-to-all-start.1 = ((bf16[128,12,2880]{2,1,0:T(8,128)(2,1)}), bf16[128,12,2880]{2,1,0:T(8,128)(2,1)}, u32[]{:S(2)}, u32[]{:S(2)}) async-start(bf16[128,12,2880]{2,1,0:T(8,128)(2,1)} %reshape.275), calls=%async_computation.1 | async-start | bytes 24117248 | tf_op jit(solution)/shard_map/all_to_all | solution.py:56
  326.8 8.1 %copy-start.1 = (f32[128,4]{0,1:T(4,128)S(1)}, f32[128,4]{0,1:T(4,128)}, u32[]{:S(2)}) copy-start(f32[128,4]{0,1:T(4,128)} %param.12) | copy-start | bytes 6148
  326.9 272.0 %all-reduce.2.cloned.1.call-start = ((), (), s32[]{:S(2)}) async-start(), calls=%async_computation.3 | async-start | bytes 5898240 | tf_op jit(solution)/shard_map/psum | solution.py:77
Sparse Core Ops, SparseCore 0:
  61.4 251.3 all-gather.1
  334.5 264.2 all-reduce.1
where the time goes:
time: 670 us; the launch traced here: 659 us
  waiting for transfers between devices  435 us (65%)
  local copies, waits for them, and re-layouts  107 us (16%)
  matrix products  43.6 us (7%)
  starting transfers between devices  31.4 us (5%)
  other arithmetic  28.2 us (4%)
  between operations  14.2 us (2%)
    psum x1, waiting for transfers between devices, local(): lax.psum(local_grad.astype(jnp.bfloat16), 'dp').astype(jnp.float32)  264 us
    all_to_all x1, waiting for transfers between devices, local(): lax.all_to_all(outgoing, ('dp', 'expert'), split_axis=0, concat_axis=0, t...  170 us
    dot_general x1, matrix products, expert_part(): jnp.dot(active, down_half, preferred_element_type=jnp.float32)  23.7 us
    all_to_all x1, starting transfers between devices, local(): lax.all_to_all(partial_value.reshape(sources, slot_count, width), ('dp',...  19.7 us
    gather x2, local copies, waits for them, and re-layouts, local(): fetched = expert_out[jnp.minimum(where_to, expert_count * capacity - 1)]  18.2 us
    reshape x1, local copies, waits for them, and re-layouts, local(): incoming.reshape(sources * slot_count, width)  14.6 us
    reshape x1, local copies, waits for them, and re-layouts, local(): partial_value.reshape(sources, slot_count, width)  13.5 us
  transfers between devices with their start and end apart: 4, of which 2 were waited for; matrix products, arithmetic and copies ran while one was open for 14% of the time, Pallas kernels for 0%

commit v1 on v0

v1 whole, which is shorter than its diff:
```python
import functools

import jax
import jax.numpy as jnp
from jax import lax
from jax.experimental import pallas as pl
from jax.experimental.pallas import tpu as pltpu
from jax.sharding import Mesh, PartitionSpec as P

CAP = 12
BF = jnp.bfloat16
F32 = jnp.float32
NT = (((1,), (1,)), ((), ()))


def place(ids, shifts, lim):
    label = lax.broadcasted_iota(jnp.int32, (64, 128), 0)
    earlier = (
        lax.broadcasted_iota(jnp.int32, (128, 128), 0)
        < lax.broadcasted_iota(jnp.int32, (128, 128), 1)
    ).astype(F32).astype(BF)
    rows = [ids[k : k + 1, :] for k in range(4)]
    hots = [(r == label).astype(F32) for r in rows]
    hot = hots[0] + hots[1] + hots[2] + hots[3]
    before = jnp.dot(hot.astype(BF), earlier, preferred_element_type=F32)
    spilled, seconds, second_hots, first_ranks = [], [], [], []
    for k in range(4):
        rank = jnp.sum(before * hots[k], axis=0, keepdims=True)
        limit = jnp.sum(lim * hots[k], axis=0, keepdims=True)
        spill = rank >= limit
        second = (rows[k] + shifts[k : k + 1, :]) & 63
        first_ranks.append(rank)
        spilled.append(spill)
        seconds.append(second)
        second_hots.append((second == label).astype(F32))
    spill_hots = [h * s.astype(F32) for h, s in zip(second_hots, spilled)]
    total = spill_hots[0] + spill_hots[1] + spill_hots[2] + spill_hots[3]
    run = jnp.dot(total.astype(BF), earlier, preferred_element_type=F32)
    out = []
    for k in range(4):
        rank = jnp.sum(run * second_hots[k], axis=0, keepdims=True)
        run = run + spill_hots[k]
        limit = jnp.sum(lim * second_hots[k], axis=0, keepdims=True)
        slot = jnp.where(spilled[k], limit + rank, first_ranks[k]).astype(jnp.int32)
        target = jnp.where(spilled[k], seconds[k], rows[k])
        out.append((target, slot, slot < CAP))
    return out


def local_rows(places, core, side):
    out = []
    for target, slot, kept in places:
        mine = kept & (((target >> 2) & 1) == core)
        index = (target >> 3) * 4 + (target & 3)
        out.append(jnp.where(mine, index * 24 + slot + side * CAP, -1))
    return out


def dispatch_kernel(own_ref, sib_ref, mo_ref, ms_ref, lim_ref, core_ref, out_ref, rows_ref, hot_ref, tok_ref):
    step = pl.program_id(0)

    @pl.when(step == 0)
    def _():
        core = core_ref[0]
        tok_ref[:, :128] = own_ref[...]
        tok_ref[:, 128:] = sib_ref[...]
        slot_of = lax.broadcasted_iota(jnp.int32, (768, 128), 0)
        for side, m_ref in enumerate((mo_ref, ms_ref)):
            m = m_ref[...]
            ids = m[0:4].astype(jnp.int32)
            shifts = m[4:8].astype(jnp.int32)
            rows = local_rows(place(ids, shifts, lim_ref[...]), core, side)
            hot = (rows[0] == slot_of) | (rows[1] == slot_of) | (rows[2] == slot_of) | (rows[3] == slot_of)
            hot_ref[:, 128 * side : 128 * side + 128] = hot.astype(F32).astype(BF)
            for k in range(4):
                rows_ref[4 * side + k : 4 * side + k + 1, :] = rows[k]

    part = hot_ref[pl.ds(pl.multiple_of(step * 192, 192), 192), :]
    got = lax.dot_general(part, tok_ref[...], NT, preferred_element_type=F32).astype(BF)
    out_ref[0] = got
    out_ref[1] = got


def dispatch(tok, sib_tok, meta, sib_meta, lim, core):
    vm = pl.BlockSpec(memory_space=pltpu.VMEM)
    return pl.pallas_call(
        dispatch_kernel,
        grid=(4,),
        in_specs=[vm, vm, vm, vm, vm, pl.BlockSpec(memory_space=pltpu.SMEM)],
        out_specs=[
            pl.BlockSpec((2, 192, 2880), lambda i: (0, i, 0)),
            pl.BlockSpec((8, 128), lambda i: (0, 0)),
        ],
        out_shape=[
            jax.ShapeDtypeStruct((2, 768, 2880), BF),
            jax.ShapeDtypeStruct((8, 128), jnp.int32),
        ],
        scratch_shapes=[pltpu.VMEM((768, 256), BF), pltpu.VMEM((2880, 256), BF)],
        compiler_params=pltpu.CompilerParams(vmem_limit_bytes=40 << 20),
        cost_estimate=pl.CostEstimate(flops=2 * 768 * 256 * 2880, bytes_accessed=11_000_000, transcendentals=0),
        name="dispatch",
    )(tok, sib_tok, meta, sib_meta, lim, core)


def ffn_kernel(x_ref, g_hbm, u_hbm, d_hbm, out_ref, g_ref, u_ref, d_ref, sems):
    step = pl.program_id(0)
    copies = [
        pltpu.make_async_copy(g_hbm.at[0], g_ref, sems.at[0]),
        pltpu.make_async_copy(u_hbm.at[0], u_ref, sems.at[1]),
        pltpu.make_async_copy(d_hbm, d_ref, sems.at[2]),
    ]

    @pl.when(step == 0)
    def _():
        for c in copies:
            c.start()
        copies[0].wait()

    x = x_ref[...]
    gating = jnp.dot(x, g_ref[...], preferred_element_type=F32)

    @pl.when(step == 0)
    def _():
        copies[1].wait()

    upward = jnp.dot(x, u_ref[...], preferred_element_type=F32)
    active = ((upward + 1.0) * gating * jax.nn.sigmoid(1.702 * gating)).astype(BF)

    @pl.when(step == 0)
    def _():
        copies[2].wait()

    out_ref[...] = lax.dot_general(active, d_ref[...], NT, preferred_element_type=F32).astype(BF)


def ffn(x, g, u, d_t, rows=384):
    count = x.shape[0]
    hbm = pl.BlockSpec(memory_space=pl.ANY)
    return pl.pallas_call(
        ffn_kernel,
        grid=(count // rows,),
        in_specs=[pl.BlockSpec((rows, 2880), lambda i: (i, 0)), hbm, hbm, hbm],
        out_specs=pl.BlockSpec((rows, 2880), lambda i: (i, 0)),
        out_shape=jax.ShapeDtypeStruct((count, 2880), BF),
        scratch_shapes=[
            pltpu.VMEM((2880, 768), BF),
            pltpu.VMEM((2880, 768), BF),
            pltpu.VMEM((2880, 768), BF),
            pltpu.SemaphoreType.DMA((3,)),
        ],
        compiler_params=pltpu.CompilerParams(vmem_limit_bytes=48 << 20),
        cost_estimate=pl.CostEstimate(
            flops=6 * count * 2880 * 768, bytes_accessed=13_300_000 + count * 2880 * 4, transcendentals=count * 768
        ),
        name="ffn",
    )(x, g, u, d_t)


def combine_kernel(y_ref, rows_ref, mo_ref, ms_ref, own_ref, sib_ref, w_ref, acc_ref):
    step = pl.program_id(0)

    @pl.when(step == 0)
    def _():
        slot_of = lax.broadcasted_iota(jnp.int32, (768, 128), 0)
        for side, m_ref in enumerate((mo_ref, ms_ref)):
            raw = m_ref[8:12]
            share = raw / jnp.sum(raw, axis=0, keepdims=True)
            w = jnp.zeros((768, 128), F32)
            for k in range(4):
                w = w + jnp.where(rows_ref[4 * side + k : 4 * side + k + 1, :] == slot_of, share[k : k + 1], 0.0)
            wt = w.T.astype(BF)
            for b in range(4):
                w_ref[b, 128 * side : 128 * side + 128, :] = wt[:, 192 * b : 192 * b + 192]
        acc_ref[...] = jnp.zeros_like(acc_ref)

    w = w_ref[step]
    acc_ref[...] += jnp.dot(w, y_ref[0], preferred_element_type=F32) + jnp.dot(
        w, y_ref[1], preferred_element_type=F32
    )

    @pl.when(step == 3)
    def _():
        own_ref[...] = acc_ref[:128, :].T
        sib_ref[...] = acc_ref[128:, :].T.astype(BF)


def combine(y, rows, meta, sib_meta):
    vm = pl.BlockSpec(memory_space=pltpu.VMEM)
    return pl.pallas_call(
        combine_kernel,
        grid=(4,),
        in_specs=[pl.BlockSpec((2, 192, 2880), lambda i: (0, i, 0)), vm, vm, vm],
        out_specs=[pl.BlockSpec((2880, 128), lambda i: (0, 0))] * 2,
        out_shape=[jax.ShapeDtypeStruct((2880, 128), F32), jax.ShapeDtypeStruct((2880, 128), BF)],
        scratch_shapes=[pltpu.VMEM((4, 256, 192), BF), pltpu.VMEM((256, 2880), F32)],
        compiler_params=pltpu.CompilerParams(vmem_limit_bytes=48 << 20),
        cost_estimate=pl.CostEstimate(flops=4 * 768 * 256 * 2880, bytes_accessed=12_000_000, transcendentals=0),
        name="combine",
    )(y, rows, meta, sib_meta)


def ring(axis, shift, n):
    return functools.partial(lax.ppermute, axis_name=axis, perm=[(i, (i + shift) % n) for i in range(n)])


def gather_ring4(block, axis):
    half = block.shape[0] // 2
    below = ring(axis, 1, 4)(block)
    above = ring(axis, -1, 4)(block)
    far = jnp.concatenate([ring(axis, 1, 4)(below[:half]), ring(axis, -1, 4)(above[half:])], axis=0)
    return block, below, above, far


def projection(context, og_t):
    y, zl = lax.axis_index("y"), lax.axis_index("zl")
    x, core, zh = lax.axis_index("x"), lax.axis_index("core"), lax.axis_index("zh")
    other = ring("zl", 1, 2)(og_t)
    pair = jnp.stack([jnp.where(zl == 0, og_t, other), jnp.where(zl == 0, other, og_t)])
    ctx = context.reshape(4, 2, 128, 512)
    grad = None
    for at, block in zip((0, 3, 1, 2), gather_ring4(pair, "y")):
        own_ctx = lax.dynamic_index_in_dim(ctx, (y + at) % 4, 0, keepdims=False)
        term = lax.dot_general(block, own_ctx, (((0, 2), (0, 1)), ((), ())), preferred_element_type=F32)
        grad = term if grad is None else grad + term
    grad = grad.astype(BF)
    halves = grad.reshape(2, 1440, 512)
    mine = lax.dynamic_index_in_dim(halves, core, 0, keepdims=False)
    sent = lax.dynamic_index_in_dim(halves, 1 - core, 0, keepdims=False)
    part = mine.astype(F32) + ring("core", 1, 2)(sent).astype(F32)
    cols = part.reshape(1440, 4, 128).swapaxes(0, 1)

    def block_of(offset):
        return lax.dynamic_index_in_dim(cols, (x + offset) % 4, 0, keepdims=False)

    far = block_of(2).astype(BF)
    from_below = ring("x", 1, 4)(far[:720])
    from_above = ring("x", -1, 4)(far[720:])
    up, down = block_of(1), block_of(3)
    up = jnp.concatenate([up[:720] + from_below.astype(F32), up[720:]]).astype(BF)
    down = jnp.concatenate([down[:720], down[720:] + from_above.astype(F32)]).astype(BF)
    block = block_of(0) + ring("x", 1, 4)(up).astype(F32) + ring("x", -1, 4)(down).astype(F32)
    rows = block.reshape(2, 720, 128)
    kept = lax.dynamic_index_in_dim(rows, zh, 0, keepdims=False)
    gone = lax.dynamic_index_in_dim(rows, 1 - zh, 0, keepdims=False).astype(BF)
    total = (kept + ring("zh", 1, 2)(gone).astype(F32)).astype(BF)
    back = ring("zh", 1, 2)(total)
    block = jnp.concatenate([jnp.where(zh == 0, total, back), jnp.where(zh == 0, back, total)])
    ordered = jnp.stack(gather_ring4(block, "x"))
    at = jnp.array([0, 3, 1, 2])
    source = jnp.take(at.argsort(), (jnp.arange(4) - x) % 4)
    full = jnp.take(ordered, source, axis=0)
    full = full.swapaxes(0, 1).reshape(1440, 512)
    opposite = ring("core", 1, 2)(full)
    both = jnp.concatenate([jnp.where(core == 0, full, opposite), jnp.where(core == 0, opposite, full)])
    return both.astype(F32)


def local(tokens, expert_ids, gate_raw, overflow_shift, limits, gate_w, up_w, down_w, context, out_grad):
    tok = tokens.T
    meta = jnp.concatenate([expert_ids.T.astype(F32), overflow_shift.T.astype(F32), gate_raw.T, jnp.zeros((4, 128), F32)])
    swap = ring("core", 1, 2)
    sib_tok, sib_meta = swap(tok), swap(meta)
    lim = jnp.broadcast_to(limits.astype(F32)[:, None], (64, 128))
    core = lax.axis_index("core")
    send, rows = dispatch(tok, sib_tok, meta, sib_meta, lim, core[None])
    over = ("zl", "x", "zh", "y")
    got = lax.all_to_all(send.reshape(64, 24, 2880), over, split_axis=0, concat_axis=0, tiled=True)
    partial_out = ffn(got.reshape(1536, 2880), gate_w, up_w, down_w[0].T)
    back = lax.all_to_all(partial_out.reshape(64, 24, 2880), over, split_axis=0, concat_axis=0, tiled=True)
    own, sib = combine(back.reshape(2, 768, 2880), rows, meta, sib_meta)
    mixed = (own + swap(sib).astype(F32)).astype(BF)
    grad = projection(context, out_grad.T)
    return mixed.T, grad.T


def solution(mesh):
    fine = Mesh(mesh.devices.reshape(4, 2, 2, 4, 2), ("x", "zh", "core", "y", "zl"))
    every = ("x", "zh", "core", "y", "zl")
    two, three = P(every, None), P(every, None, None)
    in_specs = (two, two, two, two, P(), three, three, three, P(("x", "zh", "core"), ("y", "zl")), two)
    out_specs = (two, P(("y", "zl"), None))
    return jax.shard_map(local, mesh=fine, in_specs=in_specs, out_specs=out_specs, check_vma=False)
```

time: 670 us -> 489 us (0.73)
  waiting for transfers between devices: 435 us -> 342 us
  local copies, waits for them, and re-layouts: 107 us -> 24.2 us
  Pallas kernels: 0 us -> 44.6 us
  matrix products: 43.6 us -> 6.6 us
  starting transfers between devices: 31.4 us -> 46.8 us
  between operations: 14.2 us -> 1.03 us
  other arithmetic: 28.2 us -> 18.5 us
    ppermute x0 -> x20, waiting for transfers between devices: none -> 342 us  [the longest x1 147 us: projection(): from_above = ring('x', -1, 4)(far[720:])]
    psum x1 -> x0, waiting for transfers between devices: 264 us -> none  [local(): lax.psum(local_grad.astype(jnp.bfloat16), 'dp').astype(jnp.float32)]
    all_to_all x2, waiting for transfers between devices: 170 us -> 0.01 us  [the longest x1 0.01 us: local(): lax.all_to_all(partial_out.reshape(64, 24, 2880), over, split_axis=0, con...]
    pallas_call x0 -> x3, Pallas kernels: none -> 44.6 us  [the longest x1 32.5 us: ffn(): pl.pallas_call(ffn_kernel, grid=(count // rows,), in_specs=[pl.BlockSpec(...]
    dot_general x3 -> x4, matrix products: 43.6 us -> 6.6 us  [projection(): lax.dot_general(block, own_ctx, (((0, 2), (0, 1)), ((), ())), preferred_e...]
    reshape x8 -> x1, local copies, waits for them, and re-layouts: 41.4 us -> 4.56 us  [projection(): cols = part.reshape(1440, 4, 128).swapaxes(0, 1)]
    ppermute x0 -> x20, starting transfers between devices: none -> 30.3 us  [the longest x2 9.4 us: gather_ring4(): above = ring(axis, -1, 4)(block)]
    gather x2, local copies, waits for them, and re-layouts: 18.2 us -> 2.84 us  [the longest x1 2.2 us: projection(): full = jnp.take(ordered, source, axis=0)]
  transfers between devices with their start and end apart: 4 -> 22, of which waited for: 2 -> 14; matrix products, arithmetic and copies ran while one was open for 14% -> 8% of each run, Pallas kernels for 0% -> 8%
where the time goes in v1:
time: 489 us; the launch traced here: 484 us
  waiting for transfers between devices  342 us (70%)
  starting transfers between devices  46.8 us (10%)
  Pallas kernels  44.6 us (9%)
  local copies, waits for them, and re-layouts  24.2 us (5%)
  other arithmetic  18.5 us (4%)
  matrix products  6.6 us (1%)
    ppermute x1, waiting for transfers between devices, projection(): from_above = ring('x', -1, 4)(far[720:])  147 us
    ppermute x1, waiting for transfers between devices, projection(): other = ring('zl', 1, 2)(og_t)  106 us
    ppermute x2, waiting for transfers between devices, gather_ring4(): above = ring(axis, -1, 4)(block)  49.8 us
    pallas_call x1, Pallas kernels, ffn(): pl.pallas_call(ffn_kernel, grid=(count // rows,), in_specs=[pl.BlockSpec(...  32.5 us
    ppermute x2, waiting for transfers between devices, gather_ring4(): ring(axis, -1, 4)(above[half:])  13.9 us
    all_to_all x1, starting transfers between devices, local(): lax.all_to_all(send.reshape(64, 24, 2880), over, split_axis=0, concat_axi...  11.2 us
  transfers between devices with their start and end apart: 22, of which 14 were waited for; matrix products, arithmetic and copies ran while one was open for 8% of the time, Pallas kernels for 8%

profile of v1, /device:TPU:5, one launch (start us, length us, event | category | flops | bytes accessed | tf_op | source)
XLA Modules:
  0.0 483.6 jit_solution(4190462012894614465)
XLA Ops:
  5.3 4.3 dispatch.1
  9.6 3.5 copy-done.2
  13.2 11.2 %all-to-all-start = ((bf16[64,24,2880]{2,1,0:T(8,128)(2,1)}), bf16[64,24,2880]{2,1,0:T(8,128)(2,1)}, u32[]{:S(2)}, u32[]{:S(2)}) async-start(bf16[64,24,2880]{2,1,0:T(8,128)(2,1)} %bitcast.121), calls=%async_computation | async-start | bytes 18087936 | tf_op jit(solution)/shard_map/all_to_all | solution.py:267
  25.8 106.1 %collective-permute-done.3 = bf16[2880,128]{1,0:T(8,128)(2,1)} collective-permute-done((bf16[2880,128]{1,0:T(8,128)(2,1)S(1)}, bf16[2880,128]{1,0:T(8,128)(2,1)}, u32[]{:S(2)}, u32[]{:S(2)}) %collective-permute-start.3) | collective-permute-done | bytes 737312 | tf_op jit(solution)/shard_map/ppermute | solution.py:217
  134.5 9.2 %collective-permute-start.5 = (bf16[2,2880,128]{2,1,0:T(8,128)(2,1)}, bf16[2,2880,128]{2,1,0:T(8,128)(2,1)}, u32[]{:S(2)}, u32[]{:S(2)}) collective-permute-start(bf16[2,2880,128]{2,1,0:T(8,128)(2,1)} %pad_maximum_fusion), channel_id=1, source_target_pairs={{0,6},{2,0},{4,2},{6,4},{1,7},{3,1},{5,3},{7,5},{8,14},{10,8},{12,... | collective-permute-start | bytes 4423688 | tf_op jit(solution)/shard_map/ppermute | solution.py:209
  144.6 45.6 %collective-permute-done.5 = bf16[2,2880,128]{2,1,0:T(8,128)(2,1)} collective-permute-done((bf16[2,2880,128]{2,1,0:T(8,128)(2,1)}, bf16[2,2880,128]{2,1,0:T(8,128)(2,1)}, u32[]{:S(2)}, u32[]{:S(2)}) %collective-permute-start.5) | collective-permute-done | bytes 1474592 | tf_op jit(solution)/shard_map/ppermute | solution.py:209
  191.4 3.5 collective-permute-start.7
  200.7 9.5 %collective-permute-done.7 = bf16[1,2880,128]{2,1,0:T(8,128)(2,1)S(1)} collective-permute-done((bf16[1,2880,128]{2,1,0:T(8,128)(2,1)S(1)}, bf16[1,2880,128]{2,1,0:T(8,128)(2,1)S(1)}, u32[]{:S(2)}, u32[]{:S(2)}) %collective-permute-start.7) | collective-permute-done | bytes 737312 | tf_op jit(solution)/shard_map/ppermute | solution.py:210
  210.2 4.3 collective-permute-done.6
  221.1 32.5 %ffn.1 = bf16[1536,2880]{1,0:T(8,128)(2,1)} custom-call(bf16[1536,2880]{1,0:T(8,128)(2,1)} %bitcast.6.x_ref, bf16[1,2880,768]{2,1,0:T(8,128)(2,1)S(1)} %copy-done.3, bf16[1,2880,768]{2,1,0:T(8,128)(2,1)} %u_hbm.1, bf16[2880,768]{1,0:T(8,128)(2,1)} %bitcast.140), custom_call_target="tpu_custom_call" | custom-call | flops 20384317440 | bytes 30994720 | tf_op jit(solution)/shard_map/ffn/pallas_call | solution.py:139
  253.7 5.3 %all-to-all-start.1 = ((bf16[64,24,2880]{2,1,0:T(8,128)(2,1)}), bf16[64,24,2880]{2,1,0:T(8,128)(2,1)}, u32[]{:S(2)}, u32[]{:S(2)}) async-start(bf16[64,24,2880]{2,1,0:T(8,128)(2,1)} %bitcast.126), calls=%async_computation.1 | async-start | bytes 18087936 | tf_op jit(solution)/shard_map/all_to_all | solution.py:269
  259.1 3.9 convert_add_fusion
  262.9 4.6 reshape.142
  267.5 2.3 dynamic-slice_convert_fusion
  274.4 146.7 %collective-permute-done.11 = bf16[720,128]{1,0:T(8,128)(2,1)S(1)} collective-permute-done((bf16[720,128]{1,0:T(8,128)(2,1)S(1)}, bf16[720,128]{1,0:T(8,128)(2,1)S(1)}, u32[]{:S(2)}, u32[]{:S(2)}) %collective-permute-start.11) | collective-permute-done | bytes 184352 | tf_op jit(solution)/shard_map/ppermute | solution.py:237
  422.9 7.4 %collective-permute-done.12 = bf16[1440,128]{1,0:T(8,128)(2,1)S(1)} collective-permute-done((bf16[1440,128]{1,0:T(8,128)(2,1)S(1)}, bf16[1440,128]{1,0:T(8,128)(2,1)S(1)}, u32[]{:S(2)}, u32[]{:S(2)}) %collective-permute-start.12) | collective-permute-done | bytes 368672 | tf_op jit(solution)/shard_map/ppermute | solution.py:241
  430.7 5.9 %collective-permute-done.13 = bf16[720,128]{1,0:T(8,128)(2,1)S(1)} collective-permute-done((bf16[720,128]{1,0:T(8,128)(2,1)S(1)}, bf16[720,128]{1,0:T(8,128)(2,1)S(1)}, u32[]{:S(2)}, u32[]{:S(2)}) %collective-permute-start.13) | collective-permute-done | bytes 184352 | tf_op jit(solution)/shard_map/ppermute | solution.py:245
  436.8 5.9 %collective-permute-done.14 = bf16[720,128]{1,0:T(8,128)(2,1)S(1)} collective-permute-done((bf16[720,128]{1,0:T(8,128)(2,1)S(1)}, bf16[720,128]{1,0:T(8,128)(2,1)S(1)}, u32[]{:S(2)}, u32[]{:S(2)}) %collective-permute-start.14) | collective-permute-done | bytes 184352 | tf_op jit(solution)/shard_map/ppermute | solution.py:246
  445.0 4.2 collective-permute-done.16
  451.8 4.5 collective-permute-done.18
  462.1 6.3 %collective-permute-start.19 = (bf16[1440,512]{1,0:T(8,128)(2,1)}, bf16[1440,512]{1,0:T(8,128)(2,1)}, u32[]{:S(2)}, u32[]{:S(2)}) collective-permute-start(bf16[1440,512]{1,0:T(8,128)(2,1)} %copy_bitcast_fusion), channel_id=1, source_target_pairs={{0,8},{8,0},{1,9},{9,1},{2,10},{10,2},{3,11},{11,3},{4,12},{12,4},... | collective-permute-start | bytes 4423688 | tf_op jit(solution)/shard_map/ppermute | solution.py:253
  468.5 7.8 %combine.1 = (f32[2880,128]{1,0:T(8,128)S(1)}, bf16[2880,128]{1,0:T(8,128)(2,1)S(1)}) custom-call(bf16[2,768,2880]{2,1,0:T(8,128)(2,1)} %bitcast.10.y_ref, s32[8,128]{1,0:T(8,128)S(1)} %get-tuple-element.8.rows_ref, f32[16,128]{1,0:T(8,128)S(1)} %maximum_maximum_fusion.mo_ref, f32[16,128]{1,0:T(8,128)S(1)} %collective-permute-done.1.ms_ref), custom_call_target="tpu_custom_call" | custom-call | flops 2264924160 | bytes 12000000 | tf_op jit(solution)/shard_map/combine/pallas_call | solution.py:189
  476.4 2.3 broadcast_select_fusion.1
  478.7 3.4 convert_bitcast_fusion
  (89 shorter events, 42.4 us)
Async XLA Ops:
  0.6 143.0 %copy-start = (bf16[1024,512]{1,0:T(8,128)(2,1)S(1)}, bf16[1024,512]{1,0:T(8,128)(2,1)}, u32[]{:S(2)}) copy-start(bf16[1024,512]{1,0:T(8,128)(2,1)} %param.19) | copy-start | bytes 3145732
  0.6 3.5 collective-permute-start
  2.9 1.2 collective-permute-start.1
  13.2 205.7 %all-to-all-start = ((bf16[64,24,2880]{2,1,0:T(8,128)(2,1)}), bf16[64,24,2880]{2,1,0:T(8,128)(2,1)}, u32[]{:S(2)}, u32[]{:S(2)}) async-start(bf16[64,24,2880]{2,1,0:T(8,128)(2,1)} %bitcast.121), calls=%async_computation | async-start | bytes 18087936 | tf_op jit(solution)/shard_map/all_to_all | solution.py:267
  24.4 107.6 %collective-permute-start.3 = (bf16[2880,128]{1,0:T(8,128)(2,1)S(1)}, bf16[2880,128]{1,0:T(8,128)(2,1)}, u32[]{:S(2)}, u32[]{:S(2)}) collective-permute-start(bf16[2880,128]{1,0:T(8,128)(2,1)S(1)} %bitcast.136), channel_id=1, source_target_pairs={{0,1},{1,0},{2,3},{3,2},{4,5},{5,4},{6,7},{7,6},{8,9},{9,8},{10,11... | collective-permute-start | bytes 2211848 | tf_op jit(solution)/shard_map/ppermute | solution.py:217
  134.5 55.7 %collective-permute-start.5 = (bf16[2,2880,128]{2,1,0:T(8,128)(2,1)}, bf16[2,2880,128]{2,1,0:T(8,128)(2,1)}, u32[]{:S(2)}, u32[]{:S(2)}) collective-permute-start(bf16[2,2880,128]{2,1,0:T(8,128)(2,1)} %pad_maximum_fusion), channel_id=1, source_target_pairs={{0,6},{2,0},{4,2},{6,4},{1,7},{3,1},{5,3},{7,5},{8,14},{10,8},{12,... | collective-permute-start | bytes 4423688 | tf_op jit(solution)/shard_map/ppermute | solution.py:209
  143.6 51.2 %collective-permute-start.4 = (bf16[2,2880,128]{2,1,0:T(8,128)(2,1)}, bf16[2,2880,128]{2,1,0:T(8,128)(2,1)}, u32[]{:S(2)}, u32[]{:S(2)}) collective-permute-start(bf16[2,2880,128]{2,1,0:T(8,128)(2,1)} %pad_maximum_fusion), channel_id=1, source_target_pairs={{0,2},{2,4},{4,6},{6,0},{1,3},{3,5},{5,7},{7,1},{8,10},{10,12},{12... | collective-permute-start | bytes 4423688 | tf_op jit(solution)/shard_map/ppermute | solution.py:208
  191.4 18.8 %collective-permute-start.7 = (bf16[1,2880,128]{2,1,0:T(8,128)(2,1)S(1)}, bf16[1,2880,128]{2,1,0:T(8,128)(2,1)S(1)}, u32[]{:S(2)}, u32[]{:S(2)}) collective-permute-start(bf16[1,2880,128]{2,1,0:T(8,128)(2,1)S(1)} %slice.71), channel_id=1, source_target_pairs={{0,6},{2,0},{4,2},{6,4},{1,7},{3,1},{5,3},{7,5},{8,14},{10,8},{12,... | collective-permute-start | bytes 2211848 | tf_op jit(solution)/shard_map/ppermute | solution.py:210
  196.0 18.5 %collective-permute-start.6 = (bf16[1,2880,128]{2,1,0:T(8,128)(2,1)S(1)}, bf16[1,2880,128]{2,1,0:T(8,128)(2,1)S(1)}, u32[]{:S(2)}, u32[]{:S(2)}) collective-permute-start(bf16[1,2880,128]{2,1,0:T(8,128)(2,1)S(1)} %slice.70), channel_id=1, source_target_pairs={{0,2},{2,4},{4,6},{6,0},{1,3},{3,5},{5,7},{7,1},{8,10},{10,12},{12... | collective-permute-start | bytes 2211848 | tf_op jit(solution)/shard_map/ppermute | solution.py:210
  217.2 41.9 %collective-permute-start.8 = (bf16[1440,512]{1,0:T(8,128)(2,1)S(1)}, bf16[1440,512]{1,0:T(8,128)(2,1)}, u32[]{:S(2)}, u32[]{:S(2)}) collective-permute-start(bf16[1440,512]{1,0:T(8,128)(2,1)S(1)} %dynamic-slice_bitcast_fusion), channel_id=1, source_target_pairs={{0,8},{8,0},{1,9},{9,1},{2,10},{10,2},{3,11},{11,3},{4,12},{12,4},... | collective-permute-start | bytes 4423688 | tf_op jit(solution)/shard_map/ppermute | solution.py:229
  253.7 214.8 %all-to-all-start.1 = ((bf16[64,24,2880]{2,1,0:T(8,128)(2,1)}), bf16[64,24,2880]{2,1,0:T(8,128)(2,1)}, u32[]{:S(2)}, u32[]{:S(2)}) async-start(bf16[64,24,2880]{2,1,0:T(8,128)(2,1)} %bitcast.126), calls=%async_computation.1 | async-start | bytes 18087936 | tf_op jit(solution)/shard_map/all_to_all | solution.py:269
  270.6 150.5 %collective-permute-start.11 = (bf16[720,128]{1,0:T(8,128)(2,1)S(1)}, bf16[720,128]{1,0:T(8,128)(2,1)S(1)}, u32[]{:S(2)}, u32[]{:S(2)}) collective-permute-start(bf16[720,128]{1,0:T(8,128)(2,1)S(1)} %bitcast.138), channel_id=1, source_target_pairs={{0,96},{32,0},{64,32},{96,64},{1,97},{33,1},{65,33},{97,65},{2,98}... | collective-permute-start | bytes 552968 | tf_op jit(solution)/shard_map/ppermute | solution.py:237
  270.8 150.5 %collective-permute-start.9 = (bf16[720,128]{1,0:T(8,128)(2,1)S(1)}, bf16[720,128]{1,0:T(8,128)(2,1)S(1)}, u32[]{:S(2)}, u32[]{:S(2)}) collective-permute-start(bf16[720,128]{1,0:T(8,128)(2,1)S(1)} %bitcast.137), channel_id=1, source_target_pairs={{0,32},{32,64},{64,96},{96,0},{1,33},{33,65},{65,97},{97,1},{2,34}... | collective-permute-start | bytes 552968 | tf_op jit(solution)/shard_map/ppermute | solution.py:236
  421.2 9.1 %collective-permute-start.12 = (bf16[1440,128]{1,0:T(8,128)(2,1)S(1)}, bf16[1440,128]{1,0:T(8,128)(2,1)S(1)}, u32[]{:S(2)}, u32[]{:S(2)}) collective-permute-start(bf16[1440,128]{1,0:T(8,128)(2,1)S(1)} %pad_maximum_fusion.3), channel_id=1, source_target_pairs={{0,96},{32,0},{64,32},{96,64},{1,97},{33,1},{65,33},{97,65},{2,98}... | collective-permute-start | bytes 1105928 | tf_op jit(solution)/shard_map/ppermute | solution.py:241
  421.4 9.1 %collective-permute-start.10 = (bf16[1440,128]{1,0:T(8,128)(2,1)S(1)}, bf16[1440,128]{1,0:T(8,128)(2,1)S(1)}, u32[]{:S(2)}, u32[]{:S(2)}) collective-permute-start(bf16[1440,128]{1,0:T(8,128)(2,1)S(1)} %pad_maximum_fusion.2), channel_id=1, source_target_pairs={{0,32},{32,64},{64,96},{96,0},{1,33},{33,65},{65,97},{97,1},{2,34}... | collective-permute-start | bytes 1105928 | tf_op jit(solution)/shard_map/ppermute | solution.py:241
  430.6 13.7 %copy-start.5 = (s32[4]{0:T(128)S(1)}, s32[4]{0:T(128)}, u32[]{:S(2)}) copy-start(s32[4]{0:T(128)} %constant.145) | copy-start | bytes 52
  430.6 6.0 %collective-permute-start.13 = (bf16[720,128]{1,0:T(8,128)(2,1)S(1)}, bf16[720,128]{1,0:T(8,128)(2,1)S(1)}, u32[]{:S(2)}, u32[]{:S(2)}) collective-permute-start(bf16[720,128]{1,0:T(8,128)(2,1)S(1)} %fusion.21), channel_id=1, source_target_pairs={{0,16},{16,0},{1,17},{17,1},{2,18},{18,2},{3,19},{19,3},{4,20},{20... | collective-permute-start | bytes 552968 | tf_op jit(solution)/shard_map/ppermute | solution.py:245
  436.7 6.0 %collective-permute-start.14 = (bf16[720,128]{1,0:T(8,128)(2,1)S(1)}, bf16[720,128]{1,0:T(8,128)(2,1)S(1)}, u32[]{:S(2)}, u32[]{:S(2)}) collective-permute-start(bf16[720,128]{1,0:T(8,128)(2,1)S(1)} %fusion.9), channel_id=1, source_target_pairs={{0,16},{16,0},{1,17},{17,1},{2,18},{18,2},{3,19},{19,3},{4,20},{20... | collective-permute-start | bytes 552968 | tf_op jit(solution)/shard_map/ppermute | solution.py:246
  442.7 6.4 %collective-permute-start.16 = (bf16[1440,128]{1,0:T(8,128)(2,1)S(1)}, bf16[1440,128]{1,0:T(8,128)(2,1)S(1)}, u32[]{:S(2)}, u32[]{:S(2)}) collective-permute-start(bf16[1440,128]{1,0:T(8,128)(2,1)S(1)} %get-tuple-element.22), channel_id=1, source_target_pairs={{0,96},{32,0},{64,32},{96,64},{1,97},{33,1},{65,33},{97,65},{2,98}... | collective-permute-start | bytes 1105928 | tf_op jit(solution)/shard_map/ppermute | solution.py:209
  442.9 7.0 %collective-permute-start.15 = (bf16[1440,128]{1,0:T(8,128)(2,1)S(1)}, bf16[1440,128]{1,0:T(8,128)(2,1)S(1)}, u32[]{:S(2)}, u32[]{:S(2)}) collective-permute-start(bf16[1440,128]{1,0:T(8,128)(2,1)S(1)} %get-tuple-element.22), channel_id=1, source_target_pairs={{0,32},{32,64},{64,96},{96,0},{1,33},{33,65},{65,97},{97,1},{2,34}... | collective-permute-start | bytes 1105928 | tf_op jit(solution)/shard_map/ppermute | solution.py:208
  449.2 7.0 %collective-permute-start.18 = (bf16[720,128]{1,0:T(8,128)(2,1)S(1)}, bf16[720,128]{1,0:T(8,128)(2,1)S(1)}, u32[]{:S(2)}, u32[]{:S(2)}) collective-permute-start(bf16[720,128]{1,0:T(8,128)(2,1)S(1)} %slice.79), channel_id=1, source_target_pairs={{0,96},{32,0},{64,32},{96,64},{1,97},{33,1},{65,33},{97,65},{2,98}... | collective-permute-start | bytes 552968 | tf_op jit(solution)/shard_map/ppermute | solution.py:210
  450.0 7.1 %collective-permute-start.17 = (bf16[720,128]{1,0:T(8,128)(2,1)S(1)}, bf16[720,128]{1,0:T(8,128)(2,1)S(1)}, u32[]{:S(2)}, u32[]{:S(2)}) collective-permute-start(bf16[720,128]{1,0:T(8,128)(2,1)S(1)} %slice.78), channel_id=1, source_target_pairs={{0,32},{32,64},{64,96},{96,0},{1,33},{33,65},{65,97},{97,1},{2,34}... | collective-permute-start | bytes 552968 | tf_op jit(solution)/shard_map/ppermute | solution.py:210
  462.1 14.2 %collective-permute-start.19 = (bf16[1440,512]{1,0:T(8,128)(2,1)}, bf16[1440,512]{1,0:T(8,128)(2,1)}, u32[]{:S(2)}, u32[]{:S(2)}) collective-permute-start(bf16[1440,512]{1,0:T(8,128)(2,1)} %copy_bitcast_fusion), channel_id=1, source_target_pairs={{0,8},{8,0},{1,9},{9,1},{2,10},{10,2},{3,11},{11,3},{4,12},{12,4},... | collective-permute-start | bytes 4423688 | tf_op jit(solution)/shard_map/ppermute | solution.py:253
  476.3 5.8 %collective-permute-start.2 = (bf16[2880,128]{1,0:T(8,128)(2,1)S(1)}, bf16[2880,128]{1,0:T(8,128)(2,1)S(1)}, u32[]{:S(2)}, u32[]{:S(2)}) collective-permute-start(bf16[2880,128]{1,0:T(8,128)(2,1)S(1)} %get-tuple-element.10), channel_id=1, source_target_pairs={{0,8},{8,0},{1,9},{9,1},{2,10},{10,2},{3,11},{11,3},{4,12},{12,4},... | collective-permute-start | bytes 2211848 | tf_op jit(solution)/shard_map/ppermute | solution.py:271
  (7 other events, 26.0 us)

commit v2 on v1

v2 whole, which is shorter than its diff:
```python
import functools

import jax
import jax.numpy as jnp
from jax import lax
from jax.experimental import pallas as pl
from jax.experimental.pallas import tpu as pltpu
from jax.sharding import Mesh, PartitionSpec as P

CAP = 12
BF = jnp.bfloat16
F32 = jnp.float32
NT = (((1,), (1,)), ((), ()))


def place(ids, shifts, lim):
    label = lax.broadcasted_iota(jnp.int32, (64, 128), 0)
    earlier = (
        lax.broadcasted_iota(jnp.int32, (128, 128), 0)
        < lax.broadcasted_iota(jnp.int32, (128, 128), 1)
    ).astype(F32).astype(BF)
    rows = [ids[k : k + 1, :] for k in range(4)]
    hots = [(r == label).astype(F32) for r in rows]
    hot = hots[0] + hots[1] + hots[2] + hots[3]
    before = jnp.dot(hot.astype(BF), earlier, preferred_element_type=F32)
    spilled, seconds, second_hots, first_ranks = [], [], [], []
    for k in range(4):
        rank = jnp.sum(before * hots[k], axis=0, keepdims=True)
        limit = jnp.sum(lim * hots[k], axis=0, keepdims=True)
        spill = rank >= limit
        second = (rows[k] + shifts[k : k + 1, :]) & 63
        first_ranks.append(rank)
        spilled.append(spill)
        seconds.append(second)
        second_hots.append((second == label).astype(F32))
    spill_hots = [h * s.astype(F32) for h, s in zip(second_hots, spilled)]
    total = spill_hots[0] + spill_hots[1] + spill_hots[2] + spill_hots[3]
    run = jnp.dot(total.astype(BF), earlier, preferred_element_type=F32)
    out = []
    for k in range(4):
        rank = jnp.sum(run * second_hots[k], axis=0, keepdims=True)
        run = run + spill_hots[k]
        limit = jnp.sum(lim * second_hots[k], axis=0, keepdims=True)
        slot = jnp.where(spilled[k], limit + rank, first_ranks[k]).astype(jnp.int32)
        target = jnp.where(spilled[k], seconds[k], rows[k])
        out.append((target, slot, slot < CAP))
    return out


def place_kernel(tok_ref, ids_ref, shift_ref, raw_ref, lim_ref, out_ref):
    out_ref[:2880, :] = tok_ref[...]
    places = place(ids_ref[...], shift_ref[...], lim_ref[...])
    raw = raw_ref[...]
    share = raw / jnp.sum(raw, axis=0, keepdims=True)
    rows = [t.astype(F32) for t, _, _ in places]
    rows += [jnp.where(k, s, -1).astype(F32) for _, s, k in places]
    rows += [share, jnp.zeros((4, 128), F32)]
    out_ref[2880:, :] = jnp.concatenate(rows, axis=0).astype(BF)


def place_call(tok, ids, shifts, raw, lim):
    vm = pl.BlockSpec(memory_space=pltpu.VMEM)
    return pl.pallas_call(
        place_kernel,
        in_specs=[vm] * 5,
        out_specs=vm,
        out_shape=jax.ShapeDtypeStruct((2896, 128), BF),
        compiler_params=pltpu.CompilerParams(vmem_limit_bytes=16 << 20),
        cost_estimate=pl.CostEstimate(flops=1 << 22, bytes_accessed=1_500_000, transcendentals=0),
        name="place",
    )(tok, ids, shifts, raw, lim)


def row_hot(tail, core, y, side):
    tail = tail.astype(F32)
    at = lax.broadcasted_iota(jnp.int32, (192, 128), 0)
    hot = None
    for k in range(4):
        target = tail[k : k + 1].astype(jnp.int32)
        slot = tail[4 + k : 5 + k].astype(jnp.int32)
        mine = (slot >= 0) & (((target >> 2) & 1) == core) & ((target & 3) == y)
        one = jnp.where(mine, (target >> 3) * 24 + side * CAP + slot, -1) == at
        hot = one if hot is None else hot | one
    return hot.astype(F32).astype(BF)


def picked_rows(own_ref, sib_ref, core, y):
    hot = jnp.concatenate(
        [row_hot(own_ref[2880:, :], core, y, 0), row_hot(sib_ref[2880:, :], core, y, 1)], axis=1
    )
    both = jnp.concatenate([own_ref[:2880, :], sib_ref[:2880, :]], axis=1)
    return lax.dot_general(hot, both, NT, preferred_element_type=F32)


def near_kernel(at_ref, own_ref, sib_ref, out_ref):
    got = picked_rows(own_ref, sib_ref, at_ref[0], at_ref[1]).astype(BF)
    out_ref[0] = got
    out_ref[1] = got


def near_rows(at, own, sib):
    vm = pl.BlockSpec(memory_space=pltpu.VMEM)
    return pl.pallas_call(
        near_kernel,
        in_specs=[pl.BlockSpec(memory_space=pltpu.SMEM), vm, vm],
        out_specs=vm,
        out_shape=jax.ShapeDtypeStruct((2, 192, 2880), BF),
        compiler_params=pltpu.CompilerParams(vmem_limit_bytes=24 << 20),
        cost_estimate=pl.CostEstimate(flops=2 * 192 * 256 * 2880, bytes_accessed=3_700_000, transcendentals=0),
        name="near_rows",
    )(at, own, sib)


def far_kernel(at_ref, *refs):
    out_ref = refs[6]
    for o in range(3):

        @pl.when(pl.program_id(0) == o)
        def _(o=o):
            got = picked_rows(refs[2 * o], refs[2 * o + 1], at_ref[0], at_ref[1])
            got = got.reshape(8, 24, 2880).astype(BF)
            out_ref[0, :, 0] = got
            out_ref[1, :, 0] = got


def far_rows(at, blocks):
    vm = pl.BlockSpec(memory_space=pltpu.VMEM)
    return pl.pallas_call(
        far_kernel,
        grid=(3,),
        in_specs=[pl.BlockSpec(memory_space=pltpu.SMEM)] + [vm] * 6,
        out_specs=pl.BlockSpec((2, 8, 1, 24, 2880), lambda i: (0, 0, i, 0, 0)),
        out_shape=jax.ShapeDtypeStruct((2, 8, 3, 24, 2880), BF),
        compiler_params=pltpu.CompilerParams(vmem_limit_bytes=48 << 20),
        cost_estimate=pl.CostEstimate(flops=6 * 192 * 256 * 2880, bytes_accessed=11_000_000, transcendentals=0),
        name="far_rows",
    )(at, *blocks)


def ffn_kernel(near, at_ref, x_ref, g_ref, u_ref, d_ref, *refs):
    out_ref = refs[-1]
    x = x_ref[...] if near else x_ref[:, 0].reshape(384, 2880)
    gating = jnp.dot(x, g_ref[...], preferred_element_type=F32)
    upward = jnp.dot(x, u_ref[...], preferred_element_type=F32)
    active = ((upward + 1.0) * gating * jax.nn.sigmoid(1.702 * gating)).astype(BF)
    got = lax.dot_general(active, d_ref[...], NT, preferred_element_type=F32)
    out_ref[:, 0] = got.reshape(16, 24, 2880).astype(BF)


def ffn_part(at, o, x, g, u, d_t, into=None):
    vm = pl.BlockSpec(memory_space=pltpu.VMEM)
    if o == 0:
        x_spec = pl.BlockSpec((384, 2880), lambda i, at: (0, 0))
    else:
        x_spec = pl.BlockSpec((16, 1, 24, 2880), lambda i, at: (0, o - 1, 0, 0))
    args = (at, x, g, u, d_t) + (() if into is None else (into,))
    return pl.pallas_call(
        functools.partial(ffn_kernel, o == 0),
        grid_spec=pltpu.PrefetchScalarGridSpec(
            num_scalar_prefetch=1,
            grid=(1,),
            in_specs=[x_spec, vm, vm, vm] + ([] if into is None else [pl.BlockSpec(memory_space=pltpu.HBM)]),
            out_specs=pl.BlockSpec((16, 1, 24, 2880), lambda i, at: (0, (at[1] + o) & 3, 0, 0)),
        ),
        out_shape=pltpu.HBM((16, 4, 24, 2880), BF),
        input_output_aliases={} if into is None else {5: 0},
        compiler_params=pltpu.CompilerParams(vmem_limit_bytes=30 << 20),
        cost_estimate=pl.CostEstimate(
            flops=6 * 384 * 2880 * 768, bytes_accessed=18_000_000, transcendentals=384 * 768
        ),
        name="ffn_part",
    )(*args)


def first_kernel(at_ref, x_ref, g_hbm, u_hbm, d_hbm, out_ref, g_ref, u_ref, d_ref, sems):
    copies = [
        pltpu.make_async_copy(g_hbm.at[0], g_ref, sems.at[0]),
        pltpu.make_async_copy(u_hbm.at[0], u_ref, sems.at[1]),
        pltpu.make_async_copy(d_hbm, d_ref, sems.at[2]),
    ]
    for c in copies:
        c.start()
    x = x_ref[:, 0].reshape(384, 2880)
    copies[0].wait()
    gating = jnp.dot(x, g_ref[...], preferred_element_type=F32)
    copies[1].wait()
    upward = jnp.dot(x, u_ref[...], preferred_element_type=F32)
    active = ((upward + 1.0) * gating * jax.nn.sigmoid(1.702 * gating)).astype(BF)
    copies[2].wait()
    got = lax.dot_general(active, d_ref[...], NT, preferred_element_type=F32)
    out_ref[:, 0] = got.reshape(16, 24, 2880).astype(BF)


def ffn_first(at, x, g, u, d_t):
    hbm = pl.BlockSpec(memory_space=pltpu.HBM)
    return pl.pallas_call(
        first_kernel,
        grid_spec=pltpu.PrefetchScalarGridSpec(
            num_scalar_prefetch=1,
            grid=(1,),
            in_specs=[pl.BlockSpec((16, 1, 24, 2880), lambda i, at: (0, 0, 0, 0)), hbm, hbm, hbm],
            out_specs=[pl.BlockSpec((16, 1, 24, 2880), lambda i, at: (0, (at[1] + 1) & 3, 0, 0))]
            + [pl.BlockSpec(memory_space=pltpu.VMEM)] * 3,
            scratch_shapes=[pltpu.SemaphoreType.DMA((3,))],
        ),
        out_shape=[pltpu.HBM((16, 4, 24, 2880), BF)] + [pltpu.VMEM((2880, 768), BF)] * 3,
        compiler_params=pltpu.CompilerParams(vmem_limit_bytes=47 << 20),
        cost_estimate=pl.CostEstimate(
            flops=6 * 384 * 2880 * 768, bytes_accessed=18_000_000, transcendentals=384 * 768
        ),
        name="ffn_first",
    )(at, x, g, u, d_t)


def combine_kernel(at_ref, y_ref, own_tail_ref, sib_tail_ref, own_ref, sib_ref, w_ref, acc_ref):
    step = pl.program_id(0)

    @pl.when(step == 0)
    def _():
        core = at_ref[0]
        slot_of = lax.broadcasted_iota(jnp.int32, (768, 128), 0)
        for side, ref in enumerate((own_tail_ref, sib_tail_ref)):
            tail = ref[...].astype(F32)
            w = jnp.zeros((768, 128), F32)
            for k in range(4):
                target = tail[k : k + 1].astype(jnp.int32)
                slot = tail[4 + k : 5 + k].astype(jnp.int32)
                mine = (slot >= 0) & (((target >> 2) & 1) == core)
                row = jnp.where(mine, ((target >> 3) * 4 + (target & 3)) * 24 + side * CAP + slot, -1)
                w = w + jnp.where(row == slot_of, tail[8 + k : 9 + k], 0.0)
            wt = w.T.astype(BF)
            for b in range(4):
                w_ref[b, 128 * side : 128 * side + 128, :] = wt[:, 192 * b : 192 * b + 192]
        acc_ref[...] = jnp.zeros_like(acc_ref)

    w = w_ref[step]
    acc_ref[...] += jnp.dot(w, y_ref[0], preferred_element_type=F32) + jnp.dot(
        w, y_ref[1], preferred_element_type=F32
    )

    @pl.when(step == 3)
    def _():
        own_ref[...] = acc_ref[:128, :].T
        sib_ref[...] = acc_ref[128:, :].T.astype(BF)


def combine(at, y, own_tail, sib_tail):
    vm = pl.BlockSpec(memory_space=pltpu.VMEM)
    return pl.pallas_call(
        combine_kernel,
        grid=(4,),
        in_specs=[
            pl.BlockSpec(memory_space=pltpu.SMEM),
            pl.BlockSpec((2, 192, 2880), lambda i: (0, i, 0)),
            vm,
            vm,
        ],
        out_specs=[pl.BlockSpec((2880, 128), lambda i: (0, 0))] * 2,
        out_shape=[jax.ShapeDtypeStruct((2880, 128), F32), jax.ShapeDtypeStruct((2880, 128), BF)],
        scratch_shapes=[pltpu.VMEM((4, 256, 192), BF), pltpu.VMEM((256, 2880), F32)],
        compiler_params=pltpu.CompilerParams(vmem_limit_bytes=48 << 20),
        cost_estimate=pl.CostEstimate(flops=4 * 768 * 256 * 2880, bytes_accessed=12_000_000, transcendentals=0),
        name="combine",
    )(at, y, own_tail, sib_tail)


def grad_kernel(at_ref, p0_ref, p1_ref, p2_ref, p3_ref, ctx_ref, out_ref):
    y, zl, x = at_ref[1], at_ref[2], at_ref[3]
    total = None
    for o, ref in enumerate((p0_ref, p1_ref, p2_ref, p3_ref)):
        base = ((y + o) & 3) * 256
        same = ctx_ref[pl.ds(pl.multiple_of(base + zl * 128, 128), 128), :]
        other = ctx_ref[pl.ds(pl.multiple_of(base + (1 - zl) * 128, 128), 128), :]
        left = jnp.concatenate([ref[0], ref[1]], axis=1)
        term = jnp.dot(left, jnp.concatenate([same, other], axis=0), preferred_element_type=F32)
        total = term if total is None else total + term
    for j in range(4):
        out_ref[0, pl.ds((j - x) & 3, 1)] = total[None, :, 128 * j : 128 * j + 128].astype(BF)


def local_grad(at, pairs, context):
    return pl.pallas_call(
        grad_kernel,
        grid_spec=pltpu.PrefetchScalarGridSpec(
            num_scalar_prefetch=1,
            grid=(4,),
            in_specs=[pl.BlockSpec((2, 720, 128), lambda i, at: (0, i, 0))] * 4
            + [pl.BlockSpec(memory_space=pltpu.VMEM)],
            out_specs=pl.BlockSpec((1, 4, 720, 128), lambda i, at: ((i >> 1) ^ at[0], 0, i & 1, 0)),
        ),
        out_shape=jax.ShapeDtypeStruct((2, 4, 1440, 128), BF),
        compiler_params=pltpu.CompilerParams(vmem_limit_bytes=24 << 20),
        cost_estimate=pl.CostEstimate(flops=2 * 1024 * 512 * 2880, bytes_accessed=10_000_000, transcendentals=0),
        name="local_grad",
    )(at, *pairs, context)


def spread_kernel(at_ref, own_ref, sib_ref, out_ref):
    core = at_ref[0]
    out_ref[pl.ds(core, 1)] = own_ref[...].astype(F32)
    out_ref[pl.ds(1 - core, 1)] = sib_ref[...].astype(F32)


def spread(at, own, sib):
    block = pl.BlockSpec((1, 1440, 128), lambda i, at: (i, 0, 0))
    return pl.pallas_call(
        spread_kernel,
        grid_spec=pltpu.PrefetchScalarGridSpec(
            num_scalar_prefetch=1,
            grid=(4,),
            in_specs=[block, block],
            out_specs=pl.BlockSpec((2, 1440, 128), lambda i, at: (0, 0, (at[3] + i) & 3)),
        ),
        out_shape=jax.ShapeDtypeStruct((2, 1440, 512), F32),
        compiler_params=pltpu.CompilerParams(vmem_limit_bytes=16 << 20),
        cost_estimate=pl.CostEstimate(flops=0, bytes_accessed=9_000_000, transcendentals=0),
        name="spread",
    )(at, own, sib)


def shift(axis, by, n):
    return functools.partial(lax.ppermute, axis_name=axis, perm=[(i, (i + by) % n) for i in range(n)])


def from_others(block, axis):
    return [shift(axis, -o, 4)(block) for o in (1, 2, 3)]


def after(value, *others):
    return lax.optimization_barrier((value,) + others)[0]


def local(tokens, expert_ids, gate_raw, overflow_shift, limits, gate_w, up_w, down_w, context, out_grad):
    at = jnp.stack([lax.axis_index(a) for a in ("core", "y", "zl", "x", "zh")]).astype(jnp.int32)
    zh = lax.axis_index("zh")
    core_swap, zl_swap, zh_swap = shift("core", 1, 2), shift("zl", 1, 2), shift("zh", 1, 2)
    over = ("zl", "x", "zh")

    lim = jnp.broadcast_to(limits.astype(F32)[:, None], (64, 128))
    mine = place_call(tokens.T, expert_ids.T, overflow_shift.T, gate_raw.T, lim)
    og = out_grad.T
    og_other = zl_swap(og)
    sibling = core_swap(mine)
    others = from_others(mine, "y")
    near = near_rows(at, mine, sibling).reshape(16, 24, 2880)
    near = lax.all_to_all(near, over, split_axis=0, concat_axis=0, tiled=True)
    blocks = []
    for block in others:
        blocks += [block, core_swap(block)]
    pair = jnp.stack([og, og_other])
    far = after(far_rows(at, blocks), pair, near).reshape(16, 72, 2880)
    far = lax.all_to_all(far, over, split_axis=0, concat_axis=0, tiled=True)

    pairs = [pair] + from_others(pair, "y")
    grads = local_grad(at, pairs, context)
    part = grads[0].astype(F32) + core_swap(grads[1]).astype(F32)
    total = part[0]
    for o in (1, 2, 3):
        total = total + shift("x", o, 4)(part[o].astype(BF)).astype(F32)
    far = far.reshape(16, 3, 24, 2880)
    rows = total.reshape(2, 720, 128)
    kept = lax.dynamic_index_in_dim(rows, zh, 0, keepdims=False)
    gone = lax.dynamic_index_in_dim(rows, 1 - zh, 0, keepdims=False).astype(BF)
    came = zh_swap(gone)
    out, *weights = ffn_first(at, after(far, gone), gate_w, up_w, down_w[0].T)
    total = (kept + after(came, out).astype(F32)).astype(BF)
    back = zh_swap(total)
    out = ffn_part(at, 2, far, *weights, after(out, total))
    back = after(back, out)
    block = jnp.concatenate([jnp.where(zh == 0, total, back), jnp.where(zh == 0, back, total)])
    blocks = from_others(block, "x")
    out = ffn_part(at, 3, far, *weights, after(out, block))
    out = ffn_part(at, 0, near.reshape(384, 2880), *weights, out)
    out = after(out, *blocks)
    full = jnp.stack([block] + blocks)
    grad = spread(at, full, core_swap(full)).reshape(2880, 512)

    out = lax.all_to_all(out.reshape(64, 24, 2880), over + ("y",), split_axis=0, concat_axis=0, tiled=True)
    own, sib = combine(at, out.reshape(2, 768, 2880), mine[2880:], sibling[2880:])
    mixed = (own + core_swap(sib).astype(F32)).astype(BF)
    return mixed.T, grad.T


def solution(mesh):
    fine = Mesh(mesh.devices.reshape(4, 2, 2, 4, 2), ("x", "zh", "core", "y", "zl"))
    every = ("x", "zh", "core", "y", "zl")
    two, three = P(every, None), P(every, None, None)
    in_specs = (two, two, two, two, P(), three, three, three, P(("x", "zh", "core"), ("y", "zl")), two)
    out_specs = (two, P(("y", "zl"), None))
    return jax.shard_map(local, mesh=fine, in_specs=in_specs, out_specs=out_specs, check_vma=False)
```

time: 489 us -> 414 us (0.85)
  waiting for transfers between devices: 342 us -> 269 us
  Pallas kernels: 44.6 us -> 63.3 us
  starting transfers between devices: 46.8 us -> 60.8 us
  local copies, waits for them, and re-layouts: 24.2 us -> 10.7 us
  other arithmetic: 18.5 us -> 5.99 us
  matrix products: 6.6 us -> 0 us
    ppermute x20 -> x22, waiting for transfers between devices: 342 us -> 142 us  [the longest x9 89.3 us: from_others(): return [shift(axis, -o, 4)(block) for o in (1, 2, 3)]]
    all_to_all x2 -> x3, waiting for transfers between devices: 0.01 us -> 128 us  [the longest x1 128 us: local(): lax.all_to_all(out.reshape(64, 24, 2880), over + ('y',), split_axis=0, co...]
    pallas_call x3 -> x10, Pallas kernels: 44.6 us -> 63.3 us  [the longest x3 26.3 us: ffn_part(): pl.pallas_call(functools.partial(ffn_kernel, o == 0), grid_spec=pltpu.Pre...]
    all_to_all x2 -> x3, starting transfers between devices: 16.5 us -> 24.7 us  [the longest x1 9.2 us: local(): lax.all_to_all(out.reshape(64, 24, 2880), over + ('y',), split_axis=0, co...]
    dot_general x4 -> x0, matrix products: 6.6 us -> none  [projection(): lax.dot_general(block, own_ctx, (((0, 2), (0, 1)), ((), ())), preferred_e...]
    ppermute x20 -> x22, starting transfers between devices: 30.3 us -> 36.1 us  [the longest x9 12 us: from_others(): return [shift(axis, -o, 4)(block) for o in (1, 2, 3)]]
  transfers between devices with their start and end apart: 22 -> 25, of which waited for: 14 -> 12; matrix products, arithmetic and copies ran while one was open for 8% -> 2% of each run, Pallas kernels for 8% -> 15%
where the time goes in v2:
time: 414 us; the launch traced here: 411 us
  waiting for transfers between devices  269 us (65%)
  Pallas kernels  63.3 us (15%)
  starting transfers between devices  60.8 us (15%)
  local copies, waits for them, and re-layouts  10.7 us (3%)
  other arithmetic  5.99 us (1%)
    all_to_all x1, waiting for transfers between devices, local(): lax.all_to_all(out.reshape(64, 24, 2880), over + ('y',), split_axis=0, co...  128 us
    ppermute x9, waiting for transfers between devices, from_others(): return [shift(axis, -o, 4)(block) for o in (1, 2, 3)]  89.3 us
    ppermute x3, waiting for transfers between devices, local(): total = total + shift('x', o, 4)(part[o].astype(BF)).astype(F32)  36.8 us
    pallas_call x3, Pallas kernels, ffn_part(): pl.pallas_call(functools.partial(ffn_kernel, o == 0), grid_spec=pltpu.Pre...  26.3 us
    pallas_call x1, Pallas kernels, ffn_first(): pl.pallas_call(first_kernel, grid_spec=pltpu.PrefetchScalarGridSpec(num_s...  13.3 us
    ppermute x9, starting transfers between devices, from_others(): return [shift(axis, -o, 4)(block) for o in (1, 2, 3)]  12 us
    ppermute x1, waiting for transfers between devices, local(): og_other = zl_swap(og)  10.8 us
    all_to_all x1, starting transfers between devices, local(): lax.all_to_all(out.reshape(64, 24, 2880), over + ('y',), split_axis=0, co...  9.2 us
  transfers between devices with their start and end apart: 25, of which 12 were waited for; matrix products, arithmetic and copies ran while one was open for 2% of the time, Pallas kernels for 15%

profile of v2, /device:TPU:5, one launch (start us, length us, event | category | flops | bytes accessed | tf_op | source)
XLA Modules:
  0.0 410.8 jit_solution(2768138762208772778)
XLA Ops:
  10.0 7.7 %all-to-all-start = ((bf16[16,24,2880]{2,1,0:T(8,128)(2,1)}), bf16[16,24,2880]{2,1,0:T(8,128)(2,1)S(1)}, u32[]{:S(2)}, u32[]{:S(2)}) async-start(bf16[16,24,2880]{2,1,0:T(8,128)(2,1)} %bitcast.9), calls=%async_computation | async-start | bytes 4521984 | tf_op jit(solution)/shard_map/all_to_all | solution.py:346
  23.9 12.3 %collective-permute-done.5.refs_4_ = bf16[2896,128]{1,0:T(8,128)(2,1)S(1)} collective-permute-done((bf16[2896,128]{1,0:T(8,128)(2,1)S(1)}, bf16[2896,128]{1,0:T(8,128)(2,1)S(1)}, u32[]{:S(2)}, u32[]{:S(2)}) %collective-permute-start.5) | collective-permute-done | bytes 741408 | tf_op jit(solution)/shard_map/ppermute | solution.py:326
  38.3 15.0 %collective-permute-done.3.refs_2_ = bf16[2896,128]{1,0:T(8,128)(2,1)S(1)} collective-permute-done((bf16[2896,128]{1,0:T(8,128)(2,1)S(1)}, bf16[2896,128]{1,0:T(8,128)(2,1)S(1)}, u32[]{:S(2)}, u32[]{:S(2)}) %collective-permute-start.3) | collective-permute-done | bytes 741408 | tf_op jit(solution)/shard_map/ppermute | solution.py:326
  55.1 10.8 %collective-permute-done.7 = bf16[2880,128]{1,0:T(8,128)(2,1)S(1)} collective-permute-done((bf16[2880,128]{1,0:T(8,128)(2,1)}, bf16[2880,128]{1,0:T(8,128)(2,1)S(1)}, u32[]{:S(2)}, u32[]{:S(2)}) %collective-permute-start.7) | collective-permute-done | bytes 737312 | tf_op jit(solution)/shard_map/ppermute | solution.py:342
  68.3 4.6 %far_rows.1 = bf16[2,8,3,24,2880]{4,3,2,1,0:T(8,128)(2,1)} custom-call(s32[5]{0:T(128)S(1)} %stack.47.at_ref, bf16[2896,128]{1,0:T(8,128)(2,1)S(1)} %collective-permute-done.1.refs_0_, bf16[2896,128]{1,0:T(8,128)(2,1)S(1)} %collective-permute-done.2.refs_1_, bf16[2896,128]{1,0:T(8,128)(2,1)S(1)} %collective-permute-done.3.refs_2_, ...), custom_call_target="tpu_custom_call" | custom-call | flops 849346560 | bytes 11000000 | tf_op jit(solution)/shard_map/far_rows/pallas_call | solution.py:128
  74.3 7.8 %all-to-all-start.1 = ((bf16[16,72,2880]{2,1,0:T(8,128)(2,1)}), bf16[16,72,2880]{2,1,0:T(8,128)(2,1)}, u32[]{:S(2)}, u32[]{:S(2)}) async-start(bf16[16,72,2880]{2,1,0:T(8,128)(2,1)} %bitcast.68), calls=%async_computation.1 | async-start | bytes 13565952 | tf_op jit(solution)/shard_map/all_to_all | solution.py:352
  83.3 2.6 collective-permute-start.9
  87.0 28.5 %collective-permute-done.10.p3_ref = bf16[2,2880,128]{2,1,0:T(8,128)(2,1)S(1)} collective-permute-done((bf16[2,2880,128]{2,1,0:T(8,128)(2,1)}, bf16[2,2880,128]{2,1,0:T(8,128)(2,1)S(1)}, u32[]{:S(2)}, u32[]{:S(2)}) %collective-permute-start.10) | collective-permute-done | bytes 1474592 | tf_op jit(solution)/shard_map/ppermute | solution.py:326
  115.5 32.7 %collective-permute-done.9.p2_ref = bf16[2,2880,128]{2,1,0:T(8,128)(2,1)S(1)} collective-permute-done((bf16[2,2880,128]{2,1,0:T(8,128)(2,1)}, bf16[2,2880,128]{2,1,0:T(8,128)(2,1)S(1)}, u32[]{:S(2)}, u32[]{:S(2)}) %collective-permute-start.9) | collective-permute-done | bytes 1474592 | tf_op jit(solution)/shard_map/ppermute | solution.py:326
  151.7 5.0 %local_grad.1 = bf16[2,4,1440,128]{3,2,1,0:T(8,128)(2,1)S(1)} custom-call(s32[5]{0:T(128)S(1)} %stack.47.at_ref, bf16[2,2880,128]{2,1,0:T(8,128)(2,1)S(1)} %copy-done.3, bf16[2,2880,128]{2,1,0:T(8,128)(2,1)S(1)} %collective-permute-done.8.p1_ref, bf16[2,2880,128]{2,1,0:T(8,128)(2,1)S(1)} %collective-permute-done.9.p2_ref, ...), custom_call_target="tpu_custom_call" | custom-call | flops 3019898880 | bytes 10000000 | tf_op jit(solution)/shard_map/local_grad/pallas_call | solution.py:282
  158.8 2.9 collective-permute-done.11
  166.0 22.0 %collective-permute-done.12 = bf16[1440,128]{1,0:T(8,128)(2,1)S(1)} collective-permute-done((bf16[1440,128]{1,0:T(8,128)(2,1)}, bf16[1440,128]{1,0:T(8,128)(2,1)S(1)}, u32[]{:S(2)}, u32[]{:S(2)}) %collective-permute-start.12) | collective-permute-done | bytes 368672 | tf_op jit(solution)/shard_map/ppermute | solution.py:359
  188.0 6.5 %collective-permute-done.14 = bf16[1440,128]{1,0:T(8,128)(2,1)} collective-permute-done((bf16[1440,128]{1,0:T(8,128)(2,1)}, bf16[1440,128]{1,0:T(8,128)(2,1)}, u32[]{:S(2)}, u32[]{:S(2)}) %collective-permute-start.14) | collective-permute-done | bytes 368672 | tf_op jit(solution)/shard_map/ppermute | solution.py:359
  194.5 8.3 %collective-permute-done.13 = bf16[1440,128]{1,0:T(8,128)(2,1)} collective-permute-done((bf16[1440,128]{1,0:T(8,128)(2,1)}, bf16[1440,128]{1,0:T(8,128)(2,1)}, u32[]{:S(2)}, u32[]{:S(2)}) %collective-permute-start.13) | collective-permute-done | bytes 368672 | tf_op jit(solution)/shard_map/ppermute | solution.py:359
  206.4 13.3 %ffn_first.1 = (bf16[16,4,24,2880]{3,2,1,0:T(8,128)(2,1)}, bf16[2880,768]{1,0:T(8,128)(2,1)S(1)}, bf16[2880,768]{1,0:T(8,128)(2,1)S(1)}, bf16[2880,768]{1,0:T(8,128)(2,1)S(1)}) custom-call(s32[5]{0:T(128)} %copy-done.6, bf16[16,3,24,2880]{3,2,1,0:T(8,128)(2,1)} %bitcast.15.x_ref, bf16[1,2880,768]{2,1,0:T(8,128)(2,1)} %g_hbm.1, bf16[1,2880,768]{2,1,0:T(8,128)(2,1)} %u_hbm.1, ...), custom_call_target="tpu_custom_call" | custom-call | flops 5096079360 | bytes 18000000 | tf_op jit(solution)/shard_map/ffn_first/pallas_call | solution.py:196
  221.7 9.2 %ffn_part.3.refs_0_ = bf16[16,4,24,2880]{3,2,1,0:T(8,128)(2,1)} custom-call(s32[5]{0:T(128)S(1)} %copy-done.7, bf16[16,3,24,2880]{3,2,1,0:T(8,128)(2,1)} %bitcast.15.x_ref, bf16[2880,768]{1,0:T(8,128)(2,1)S(1)} %get-tuple-element.17.g_ref, bf16[2880,768]{1,0:T(8,128)(2,1)S(1)} %get-tuple-element.18.u_ref, ...), custom_call_target="tpu_custom_call", output_to_operand_aliasing={{}: (5, {})} | custom-call | flops 5096079360 | bytes 18000000 | tf_op jit(solution)/shard_map/ffn_part/pallas_call | solution.py:157
  233.0 9.4 %ffn_part.4.refs_0_ = bf16[16,4,24,2880]{3,2,1,0:T(8,128)(2,1)} custom-call(s32[5]{0:T(128)S(1)} %copy-done.7, bf16[16,3,24,2880]{3,2,1,0:T(8,128)(2,1)} %bitcast.15.x_ref, bf16[2880,768]{1,0:T(8,128)(2,1)S(1)} %get-tuple-element.17.g_ref, bf16[2880,768]{1,0:T(8,128)(2,1)S(1)} %get-tuple-element.18.u_ref, ...), custom_call_target="tpu_custom_call", output_to_operand_aliasing={{}: (5, {})} | custom-call | flops 5096079360 | bytes 18000000 | tf_op jit(solution)/shard_map/ffn_part/pallas_call | solution.py:157
  242.5 7.6 %ffn_part.5 = bf16[16,4,24,2880]{3,2,1,0:T(8,128)(2,1)} custom-call(s32[5]{0:T(128)S(1)} %copy-done.7, bf16[384,2880]{1,0:T(8,128)(2,1)S(1)} %bitcast.62, bf16[2880,768]{1,0:T(8,128)(2,1)S(1)} %get-tuple-element.17.g_ref, bf16[2880,768]{1,0:T(8,128)(2,1)S(1)} %get-tuple-element.18.u_ref, ...), custom_call_target="tpu_custom_call", output_to_operand_aliasing={{}: (5, {})} | custom-call | flops 5096079360 | bytes 18000000 | tf_op jit(solution)/shard_map/ffn_part/pallas_call | solution.py:157
  250.1 9.2 %all-to-all-start.2 = ((bf16[64,24,2880]{2,1,0:T(8,128)(2,1)}), bf16[64,24,2880]{2,1,0:T(8,128)(2,1)}, u32[]{:S(2)}, u32[]{:S(2)}) async-start(bf16[64,24,2880]{2,1,0:T(8,128)(2,1)} %bitcast.67), calls=%async_computation.2 | async-start | bytes 18087936 | tf_op jit(solution)/shard_map/all_to_all | solution.py:378
  259.5 4.6 %collective-permute-start.21 = (bf16[4,1440,128]{2,1,0:T(8,128)(2,1)S(1)}, bf16[4,1440,128]{2,1,0:T(8,128)(2,1)S(1)}, u32[]{:S(2)}, u32[]{:S(2)}) collective-permute-start(bf16[4,1440,128]{2,1,0:T(8,128)(2,1)S(1)} %pad_maximum_fusion.1.own_ref), channel_id=1, source_target_pairs={{0,8},{8,0},{1,9},{9,1},{2,10},{10,2},{3,11},{11,3},{4,12},{12,4},... | collective-permute-start | bytes 4423688 | tf_op jit(solution)/shard_map/ppermute | solution.py:376
  265.5 127.7 %all-to-all-done.2 = bf16[64,24,2880]{2,1,0:T(8,128)(2,1)} async-done(((bf16[64,24,2880]{2,1,0:T(8,128)(2,1)}), bf16[64,24,2880]{2,1,0:T(8,128)(2,1)}, u32[]{:S(2)}, u32[]{:S(2)}) %all-to-all-start.2) | async-done | bytes 8847392 | tf_op jit(solution)/shard_map/all_to_all | solution.py:378
  393.2 7.7 %combine.1 = (f32[2880,128]{1,0:T(8,128)S(1)}, bf16[2880,128]{1,0:T(8,128)(2,1)S(1)}) custom-call(s32[5]{0:T(128)S(1)} %copy-done.7, bf16[2,768,2880]{2,1,0:T(8,128)(2,1)} %bitcast.28.y_ref, bf16[16,128]{1,0:T(8,128)(2,1)S(1)} %slice.41.own_tail_ref, bf16[16,128]{1,0:T(8,128)(2,1)S(1)} %slice.42.sib_tail_ref), custom_call_target="tpu_custom_call" | custom-call | flops 2264924160 | bytes 12000000 | tf_op jit(solution)/shard_map/combine/pallas_call | solution.py:249
  400.9 5.4 %collective-permute-start.20 = (bf16[2880,128]{1,0:T(8,128)(2,1)S(1)}, bf16[2880,128]{1,0:T(8,128)(2,1)S(1)}, u32[]{:S(2)}, u32[]{:S(2)}) collective-permute-start(bf16[2880,128]{1,0:T(8,128)(2,1)S(1)} %get-tuple-element.27), channel_id=1, source_target_pairs={{0,8},{8,0},{1,9},{9,1},{2,10},{10,2},{3,11},{11,3},{4,12},{12,4},... | collective-permute-start | bytes 2211848 | tf_op jit(solution)/shard_map/ppermute | solution.py:380
  406.4 3.5 spread.1
  (80 shorter events, 45.6 us)
Async XLA Ops:
  10.0 62.9 %all-to-all-start = ((bf16[16,24,2880]{2,1,0:T(8,128)(2,1)}), bf16[16,24,2880]{2,1,0:T(8,128)(2,1)S(1)}, u32[]{:S(2)}, u32[]{:S(2)}) async-start(bf16[16,24,2880]{2,1,0:T(8,128)(2,1)} %bitcast.9), calls=%async_computation | async-start | bytes 4521984 | tf_op jit(solution)/shard_map/all_to_all | solution.py:346
  17.8 18.5 %collective-permute-start.5 = (bf16[2896,128]{1,0:T(8,128)(2,1)S(1)}, bf16[2896,128]{1,0:T(8,128)(2,1)S(1)}, u32[]{:S(2)}, u32[]{:S(2)}) collective-permute-start(bf16[2896,128]{1,0:T(8,128)(2,1)S(1)} %place.1.own_ref), channel_id=1, source_target_pairs={{0,2},{2,4},{4,6},{6,0},{1,3},{3,5},{5,7},{7,1},{8,10},{10,12},{12... | collective-permute-start | bytes 2224136 | tf_op jit(solution)/shard_map/ppermute | solution.py:326
  19.1 34.2 %collective-permute-start.3 = (bf16[2896,128]{1,0:T(8,128)(2,1)S(1)}, bf16[2896,128]{1,0:T(8,128)(2,1)S(1)}, u32[]{:S(2)}, u32[]{:S(2)}) collective-permute-start(bf16[2896,128]{1,0:T(8,128)(2,1)S(1)} %place.1.own_ref), channel_id=1, source_target_pairs={{0,4},{2,6},{4,0},{6,2},{1,5},{3,7},{5,1},{7,3},{8,12},{10,14},{12... | collective-permute-start | bytes 2224136 | tf_op jit(solution)/shard_map/ppermute | solution.py:326
  21.7 33.4 %collective-permute-start.1 = (bf16[2896,128]{1,0:T(8,128)(2,1)S(1)}, bf16[2896,128]{1,0:T(8,128)(2,1)S(1)}, u32[]{:S(2)}, u32[]{:S(2)}) collective-permute-start(bf16[2896,128]{1,0:T(8,128)(2,1)S(1)} %place.1.own_ref), channel_id=1, source_target_pairs={{0,6},{2,0},{4,2},{6,4},{1,7},{3,1},{5,3},{7,5},{8,14},{10,8},{12,... | collective-permute-start | bytes 2224136 | tf_op jit(solution)/shard_map/ppermute | solution.py:326
  22.7 43.1 %collective-permute-start.7 = (bf16[2880,128]{1,0:T(8,128)(2,1)}, bf16[2880,128]{1,0:T(8,128)(2,1)S(1)}, u32[]{:S(2)}, u32[]{:S(2)}) collective-permute-start(bf16[2880,128]{1,0:T(8,128)(2,1)} %bitcast.73), channel_id=1, source_target_pairs={{0,1},{1,0},{2,3},{3,2},{4,5},{5,4},{6,7},{7,6},{8,9},{9,8},{10,11... | collective-permute-start | bytes 2211848 | tf_op jit(solution)/shard_map/ppermute | solution.py:342
  36.2 32.0 %collective-permute-start.6 = (bf16[2896,128]{1,0:T(8,128)(2,1)S(1)}, bf16[2896,128]{1,0:T(8,128)(2,1)S(1)}, u32[]{:S(2)}, u32[]{:S(2)}) collective-permute-start(bf16[2896,128]{1,0:T(8,128)(2,1)S(1)} %collective-permute-done.5.refs_4_), channel_id=1, source_target_pairs={{0,8},{8,0},{1,9},{9,1},{2,10},{10,2},{3,11},{11,3},{4,12},{12,4},... | collective-permute-start | bytes 2224136 | tf_op jit(solution)/shard_map/ppermute | solution.py:349
  53.2 15.0 %collective-permute-start.4 = (bf16[2896,128]{1,0:T(8,128)(2,1)S(1)}, bf16[2896,128]{1,0:T(8,128)(2,1)S(1)}, u32[]{:S(2)}, u32[]{:S(2)}) collective-permute-start(bf16[2896,128]{1,0:T(8,128)(2,1)S(1)} %collective-permute-done.3.refs_2_), channel_id=1, source_target_pairs={{0,8},{8,0},{1,9},{9,1},{2,10},{10,2},{3,11},{11,3},{4,12},{12,4},... | collective-permute-start | bytes 2224136 | tf_op jit(solution)/shard_map/ppermute | solution.py:349
  55.1 13.2 %collective-permute-start.2 = (bf16[2896,128]{1,0:T(8,128)(2,1)S(1)}, bf16[2896,128]{1,0:T(8,128)(2,1)S(1)}, u32[]{:S(2)}, u32[]{:S(2)}) collective-permute-start(bf16[2896,128]{1,0:T(8,128)(2,1)S(1)} %collective-permute-done.1.refs_0_), channel_id=1, source_target_pairs={{0,8},{8,0},{1,9},{9,1},{2,10},{10,2},{3,11},{11,3},{4,12},{12,4},... | collective-permute-start | bytes 2224136 | tf_op jit(solution)/shard_map/ppermute | solution.py:349
  74.3 132.1 %all-to-all-start.1 = ((bf16[16,72,2880]{2,1,0:T(8,128)(2,1)}), bf16[16,72,2880]{2,1,0:T(8,128)(2,1)}, u32[]{:S(2)}, u32[]{:S(2)}) async-start(bf16[16,72,2880]{2,1,0:T(8,128)(2,1)} %bitcast.68), calls=%async_computation.1 | async-start | bytes 13565952 | tf_op jit(solution)/shard_map/all_to_all | solution.py:352
  82.0 33.5 %collective-permute-start.10 = (bf16[2,2880,128]{2,1,0:T(8,128)(2,1)}, bf16[2,2880,128]{2,1,0:T(8,128)(2,1)S(1)}, u32[]{:S(2)}, u32[]{:S(2)}) collective-permute-start(bf16[2,2880,128]{2,1,0:T(8,128)(2,1)} %pad_maximum_fusion.p0_ref), channel_id=1, source_target_pairs={{0,2},{2,4},{4,6},{6,0},{1,3},{3,5},{5,7},{7,1},{8,10},{10,12},{12... | collective-permute-start | bytes 4423688 | tf_op jit(solution)/shard_map/ppermute | solution.py:326
  83.3 64.9 %collective-permute-start.9 = (bf16[2,2880,128]{2,1,0:T(8,128)(2,1)}, bf16[2,2880,128]{2,1,0:T(8,128)(2,1)S(1)}, u32[]{:S(2)}, u32[]{:S(2)}) collective-permute-start(bf16[2,2880,128]{2,1,0:T(8,128)(2,1)} %pad_maximum_fusion.p0_ref), channel_id=1, source_target_pairs={{0,4},{2,6},{4,0},{6,2},{1,5},{3,7},{5,1},{7,3},{8,12},{10,14},{12... | collective-permute-start | bytes 4423688 | tf_op jit(solution)/shard_map/ppermute | solution.py:326
  86.0 63.1 %collective-permute-start.8 = (bf16[2,2880,128]{2,1,0:T(8,128)(2,1)}, bf16[2,2880,128]{2,1,0:T(8,128)(2,1)S(1)}, u32[]{:S(2)}, u32[]{:S(2)}) collective-permute-start(bf16[2,2880,128]{2,1,0:T(8,128)(2,1)} %pad_maximum_fusion.p0_ref), channel_id=1, source_target_pairs={{0,6},{2,0},{4,2},{6,4},{1,7},{3,1},{5,3},{7,5},{8,14},{10,8},{12,... | collective-permute-start | bytes 4423688 | tf_op jit(solution)/shard_map/ppermute | solution.py:326
  156.8 4.9 %collective-permute-start.11 = (bf16[4,1440,128]{2,1,0:T(8,128)(2,1)S(1)}, bf16[4,1440,128]{2,1,0:T(8,128)(2,1)S(1)}, u32[]{:S(2)}, u32[]{:S(2)}) collective-permute-start(bf16[4,1440,128]{2,1,0:T(8,128)(2,1)S(1)} %slice_bitcast_fusion), channel_id=1, source_target_pairs={{0,8},{8,0},{1,9},{9,1},{2,10},{10,2},{3,11},{11,3},{4,12},{12,4},... | collective-permute-start | bytes 4423688 | tf_op jit(solution)/shard_map/ppermute | solution.py:356
  163.1 24.9 %collective-permute-start.12 = (bf16[1440,128]{1,0:T(8,128)(2,1)}, bf16[1440,128]{1,0:T(8,128)(2,1)S(1)}, u32[]{:S(2)}, u32[]{:S(2)}) collective-permute-start(bf16[1440,128]{1,0:T(8,128)(2,1)} %get-tuple-element.30), channel_id=1, source_target_pairs={{0,32},{32,64},{64,96},{96,0},{1,33},{33,65},{65,97},{97,1},{2,34}... | collective-permute-start | bytes 1105928 | tf_op jit(solution)/shard_map/ppermute | solution.py:359
  164.0 30.5 %collective-permute-start.14 = (bf16[1440,128]{1,0:T(8,128)(2,1)}, bf16[1440,128]{1,0:T(8,128)(2,1)}, u32[]{:S(2)}, u32[]{:S(2)}) collective-permute-start(bf16[1440,128]{1,0:T(8,128)(2,1)} %get-tuple-element.31), channel_id=1, source_target_pairs={{0,96},{32,0},{64,32},{96,64},{1,97},{33,1},{65,33},{97,65},{2,98}... | collective-permute-start | bytes 1105928 | tf_op jit(solution)/shard_map/ppermute | solution.py:359
  164.6 38.2 %collective-permute-start.13 = (bf16[1440,128]{1,0:T(8,128)(2,1)}, bf16[1440,128]{1,0:T(8,128)(2,1)}, u32[]{:S(2)}, u32[]{:S(2)}) collective-permute-start(bf16[1440,128]{1,0:T(8,128)(2,1)} %get-tuple-element.32), channel_id=1, source_target_pairs={{0,64},{32,96},{64,0},{96,32},{1,65},{33,97},{65,1},{97,33},{2,66}... | collective-permute-start | bytes 1105928 | tf_op jit(solution)/shard_map/ppermute | solution.py:359
  205.0 14.8 %collective-permute-start.15 = (bf16[720,128]{1,0:T(8,128)(2,1)S(1)}, bf16[720,128]{1,0:T(8,128)(2,1)S(1)}, u32[]{:S(2)}, u32[]{:S(2)}) collective-permute-start(bf16[720,128]{1,0:T(8,128)(2,1)S(1)} %fusion.5), channel_id=1, source_target_pairs={{0,16},{16,0},{1,17},{17,1},{2,18},{18,2},{3,19},{19,3},{4,20},{20... | collective-permute-start | bytes 552968 | tf_op jit(solution)/shard_map/ppermute | solution.py:364
  219.8 11.1 %collective-permute-start.16 = (bf16[720,128]{1,0:T(8,128)(2,1)S(1)}, bf16[720,128]{1,0:T(8,128)(2,1)S(1)}, u32[]{:S(2)}, u32[]{:S(2)}) collective-permute-start(bf16[720,128]{1,0:T(8,128)(2,1)S(1)} %fusion.4), channel_id=1, source_target_pairs={{0,16},{16,0},{1,17},{17,1},{2,18},{18,2},{3,19},{19,3},{4,20},{20... | collective-permute-start | bytes 552968 | tf_op jit(solution)/shard_map/ppermute | solution.py:367
  231.0 19.1 %collective-permute-start.19 = (bf16[1440,128]{1,0:T(8,128)(2,1)S(1)}, bf16[1440,128]{1,0:T(8,128)(2,1)S(1)}, u32[]{:S(2)}, u32[]{:S(2)}) collective-permute-start(bf16[1440,128]{1,0:T(8,128)(2,1)S(1)} %get-tuple-element.34), channel_id=1, source_target_pairs={{0,32},{32,64},{64,96},{96,0},{1,33},{33,65},{65,97},{97,1},{2,34}... | collective-permute-start | bytes 1105928 | tf_op jit(solution)/shard_map/ppermute | solution.py:326
  231.1 19.0 %collective-permute-start.18 = (bf16[1440,128]{1,0:T(8,128)(2,1)S(1)}, bf16[1440,128]{1,0:T(8,128)(2,1)S(1)}, u32[]{:S(2)}, u32[]{:S(2)}) collective-permute-start(bf16[1440,128]{1,0:T(8,128)(2,1)S(1)} %get-tuple-element.34), channel_id=1, source_target_pairs={{0,64},{32,96},{64,0},{96,32},{1,65},{33,97},{65,1},{97,33},{2,66}... | collective-permute-start | bytes 1105928 | tf_op jit(solution)/shard_map/ppermute | solution.py:326
  233.0 17.1 %collective-permute-start.17 = (bf16[1440,128]{1,0:T(8,128)(2,1)S(1)}, bf16[1440,128]{1,0:T(8,128)(2,1)S(1)}, u32[]{:S(2)}, u32[]{:S(2)}) collective-permute-start(bf16[1440,128]{1,0:T(8,128)(2,1)S(1)} %get-tuple-element.34), channel_id=1, source_target_pairs={{0,96},{32,0},{64,32},{96,64},{1,97},{33,1},{65,33},{97,65},{2,98}... | collective-permute-start | bytes 1105928 | tf_op jit(solution)/shard_map/ppermute | solution.py:326
  250.1 143.1 %all-to-all-start.2 = ((bf16[64,24,2880]{2,1,0:T(8,128)(2,1)}), bf16[64,24,2880]{2,1,0:T(8,128)(2,1)}, u32[]{:S(2)}, u32[]{:S(2)}) async-start(bf16[64,24,2880]{2,1,0:T(8,128)(2,1)} %bitcast.67), calls=%async_computation.2 | async-start | bytes 18087936 | tf_op jit(solution)/shard_map/all_to_all | solution.py:378
  259.5 146.9 %collective-permute-start.21 = (bf16[4,1440,128]{2,1,0:T(8,128)(2,1)S(1)}, bf16[4,1440,128]{2,1,0:T(8,128)(2,1)S(1)}, u32[]{:S(2)}, u32[]{:S(2)}) collective-permute-start(bf16[4,1440,128]{2,1,0:T(8,128)(2,1)S(1)} %pad_maximum_fusion.1.own_ref), channel_id=1, source_target_pairs={{0,8},{8,0},{1,9},{9,1},{2,10},{10,2},{3,11},{11,3},{4,12},{12,4},... | collective-permute-start | bytes 4423688 | tf_op jit(solution)/shard_map/ppermute | solution.py:376
  400.9 8.9 %collective-permute-start.20 = (bf16[2880,128]{1,0:T(8,128)(2,1)S(1)}, bf16[2880,128]{1,0:T(8,128)(2,1)S(1)}, u32[]{:S(2)}, u32[]{:S(2)}) collective-permute-start(bf16[2880,128]{1,0:T(8,128)(2,1)S(1)} %get-tuple-element.27), channel_id=1, source_target_pairs={{0,8},{8,0},{1,9},{9,1},{2,10},{10,2},{3,11},{11,3},{4,12},{12,4},... | collective-permute-start | bytes 2211848 | tf_op jit(solution)/shard_map/ppermute | solution.py:380
  (15 other events, 211.5 us)

commit v3 on v2

--- a/solution.py
+++ b/solution.py
@@ -137,42 +137,21 @@
     )(at, *blocks)
 
 
-def ffn_kernel(near, at_ref, x_ref, g_ref, u_ref, d_ref, *refs):
-    out_ref = refs[-1]
-    x = x_ref[...] if near else x_ref[:, 0].reshape(384, 2880)
+def ffn_rows(x, g_ref, u_ref, d_ref, copies=(None,) * 3):
+    def ready(i):
+        if copies[i] is not None:
+            copies[i].wait()
+
+    ready(0)
     gating = jnp.dot(x, g_ref[...], preferred_element_type=F32)
+    ready(1)
     upward = jnp.dot(x, u_ref[...], preferred_element_type=F32)
     active = ((upward + 1.0) * gating * jax.nn.sigmoid(1.702 * gating)).astype(BF)
-    got = lax.dot_general(active, d_ref[...], NT, preferred_element_type=F32)
-    out_ref[:, 0] = got.reshape(16, 24, 2880).astype(BF)
-
-
-def ffn_part(at, o, x, g, u, d_t, into=None):
-    vm = pl.BlockSpec(memory_space=pltpu.VMEM)
-    if o == 0:
-        x_spec = pl.BlockSpec((384, 2880), lambda i, at: (0, 0))
-    else:
-        x_spec = pl.BlockSpec((16, 1, 24, 2880), lambda i, at: (0, o - 1, 0, 0))
-    args = (at, x, g, u, d_t) + (() if into is None else (into,))
-    return pl.pallas_call(
-        functools.partial(ffn_kernel, o == 0),
-        grid_spec=pltpu.PrefetchScalarGridSpec(
-            num_scalar_prefetch=1,
-            grid=(1,),
-            in_specs=[x_spec, vm, vm, vm] + ([] if into is None else [pl.BlockSpec(memory_space=pltpu.HBM)]),
-            out_specs=pl.BlockSpec((16, 1, 24, 2880), lambda i, at: (0, (at[1] + o) & 3, 0, 0)),
-        ),
-        out_shape=pltpu.HBM((16, 4, 24, 2880), BF),
-        input_output_aliases={} if into is None else {5: 0},
-        compiler_params=pltpu.CompilerParams(vmem_limit_bytes=30 << 20),
-        cost_estimate=pl.CostEstimate(
-            flops=6 * 384 * 2880 * 768, bytes_accessed=18_000_000, transcendentals=384 * 768
-        ),
-        name="ffn_part",
-    )(*args)
-
-
-def first_kernel(at_ref, x_ref, g_hbm, u_hbm, d_hbm, out_ref, g_ref, u_ref, d_ref, sems):
+    ready(2)
+    return lax.dot_general(active, d_ref[...], NT, preferred_element_type=F32)
+
+
+def started(g_hbm, u_hbm, d_hbm, g_ref, u_ref, d_ref, sems):
     copies = [
         pltpu.make_async_copy(g_hbm.at[0], g_ref, sems.at[0]),
         pltpu.make_async_copy(u_hbm.at[0], u_ref, sems.at[1]),
@@ -180,39 +159,56 @@
     ]
     for c in copies:
         c.start()
-    x = x_ref[:, 0].reshape(384, 2880)
-    copies[0].wait()
-    gating = jnp.dot(x, g_ref[...], preferred_element_type=F32)
-    copies[1].wait()
-    upward = jnp.dot(x, u_ref[...], preferred_element_type=F32)
-    active = ((upward + 1.0) * gating * jax.nn.sigmoid(1.702 * gating)).astype(BF)
-    copies[2].wait()
-    got = lax.dot_general(active, d_ref[...], NT, preferred_element_type=F32)
+    return copies
+
+
+def near_ffn_kernel(at_ref, x_ref, g_hbm, u_hbm, d_hbm, out_ref, g_ref, u_ref, d_ref, sems):
+    copies = started(g_hbm, u_hbm, d_hbm, g_ref, u_ref, d_ref, sems)
+    got = ffn_rows(x_ref[...], g_ref, u_ref, d_ref, copies)
     out_ref[:, 0] = got.reshape(16, 24, 2880).astype(BF)
 
 
-def ffn_first(at, x, g, u, d_t):
-    hbm = pl.BlockSpec(memory_space=pltpu.HBM)
-    return pl.pallas_call(
-        first_kernel,
+def first_kernel(at_ref, x_ref, g_hbm, u_hbm, d_hbm, into_ref, out_ref, g_ref, u_ref, d_ref, sems):
+    copies = started(g_hbm, u_hbm, d_hbm, g_ref, u_ref, d_ref, sems)
+    got = ffn_rows(x_ref[:, 0].reshape(384, 2880), g_ref, u_ref, d_ref, copies)
+    out_ref[:, 0] = got.reshape(16, 24, 2880).astype(BF)
+
+
+def part_kernel(at_ref, x_ref, g_ref, u_ref, d_ref, into_ref, out_ref):
+    got = ffn_rows(x_ref[:, 0].reshape(384, 2880), g_ref, u_ref, d_ref)
+    out_ref[:, 0] = got.reshape(16, 24, 2880).astype(BF)
+
+
+def ffn_part(at, o, x, g, u, d_t, into=None):
+    hbm, vm = pl.BlockSpec(memory_space=pltpu.HBM), pl.BlockSpec(memory_space=pltpu.VMEM)
+    kernel = (near_ffn_kernel, first_kernel, part_kernel, part_kernel)[o]
+    held = [pltpu.VMEM((2880, 768), BF)] * 3
+    sems = [pltpu.SemaphoreType.DMA((3,))]
+    if o == 0:
+        x_spec = pl.BlockSpec((384, 2880), lambda i, at: (0, 0))
+    else:
+        x_spec = pl.BlockSpec((16, 1, 24, 2880), lambda i, at: (0, o - 1, 0, 0))
+    return pl.pallas_call(
+        kernel,
         grid_spec=pltpu.PrefetchScalarGridSpec(
             num_scalar_prefetch=1,
             grid=(1,),
-            in_specs=[pl.BlockSpec((16, 1, 24, 2880), lambda i, at: (0, 0, 0, 0)), hbm, hbm, hbm],
-            out_specs=[pl.BlockSpec((16, 1, 24, 2880), lambda i, at: (0, (at[1] + 1) & 3, 0, 0))]
-            + [pl.BlockSpec(memory_space=pltpu.VMEM)] * 3,
-            scratch_shapes=[pltpu.SemaphoreType.DMA((3,))],
+            in_specs=[x_spec] + [vm if o > 1 else hbm] * 3 + [hbm] * (o > 0),
+            out_specs=[pl.BlockSpec((16, 1, 24, 2880), lambda i, at: (0, (at[1] + o) & 3, 0, 0))]
+            + [vm] * 3 * (o == 1),
+            scratch_shapes=(held + sems, sems, [], [])[o],
         ),
-        out_shape=[pltpu.HBM((16, 4, 24, 2880), BF)] + [pltpu.VMEM((2880, 768), BF)] * 3,
-        compiler_params=pltpu.CompilerParams(vmem_limit_bytes=47 << 20),
+        out_shape=[pltpu.HBM((16, 4, 24, 2880), BF)] + held * (o == 1),
+        input_output_aliases={5: 0} if o else {},
+        compiler_params=pltpu.CompilerParams(vmem_limit_bytes=(60, 47, 30, 30)[o] << 20),
         cost_estimate=pl.CostEstimate(
             flops=6 * 384 * 2880 * 768, bytes_accessed=18_000_000, transcendentals=384 * 768
         ),
-        name="ffn_first",
-    )(at, x, g, u, d_t)
-
-
-def combine_kernel(at_ref, y_ref, own_tail_ref, sib_tail_ref, own_ref, sib_ref, w_ref, acc_ref):
+        name="ffn_part%d" % o,
+    )(at, x, g, u, d_t, *([into] if o else []))
+
+
+def combine_kernel(at_ref, y_ref, own_tail_ref, sib_tail_ref, ahead_ref, own_ref, sib_ref, w_ref, acc_ref):
     step = pl.program_id(0)
 
     @pl.when(step == 0)
@@ -244,7 +240,7 @@
         sib_ref[...] = acc_ref[128:, :].T.astype(BF)
 
 
-def combine(at, y, own_tail, sib_tail):
+def combine(at, y, own_tail, sib_tail, ahead):
     vm = pl.BlockSpec(memory_space=pltpu.VMEM)
     return pl.pallas_call(
         combine_kernel,
@@ -254,6 +250,7 @@
             pl.BlockSpec((2, 192, 2880), lambda i: (0, i, 0)),
             vm,
             vm,
+            pl.BlockSpec(memory_space=pl.ANY),
         ],
         out_specs=[pl.BlockSpec((2880, 128), lambda i: (0, 0))] * 2,
         out_shape=[jax.ShapeDtypeStruct((2880, 128), F32), jax.ShapeDtypeStruct((2880, 128), BF)],
@@ -261,7 +258,7 @@
         compiler_params=pltpu.CompilerParams(vmem_limit_bytes=48 << 20),
         cost_estimate=pl.CostEstimate(flops=4 * 768 * 256 * 2880, bytes_accessed=12_000_000, transcendentals=0),
         name="combine",
-    )(at, y, own_tail, sib_tail)
+    )(at, y, own_tail, sib_tail, ahead)
 
 
 def grad_kernel(at_ref, p0_ref, p1_ref, p2_ref, p3_ref, ctx_ref, out_ref):
@@ -342,7 +339,7 @@
     og_other = zl_swap(og)
     sibling = core_swap(mine)
     others = from_others(mine, "y")
-    near = near_rows(at, mine, sibling).reshape(16, 24, 2880)
+    near = after(near_rows(at, mine, sibling), og_other, others[0], others[2]).reshape(16, 24, 2880)
     near = lax.all_to_all(near, over, split_axis=0, concat_axis=0, tiled=True)
     blocks = []
     for block in others:
@@ -350,33 +347,33 @@
     pair = jnp.stack([og, og_other])
     far = after(far_rows(at, blocks), pair, near).reshape(16, 72, 2880)
     far = lax.all_to_all(far, over, split_axis=0, concat_axis=0, tiled=True)
-
-    pairs = [pair] + from_others(pair, "y")
+    far = far.reshape(16, 3, 24, 2880)
+
+    hbm_weights = gate_w, up_w, down_w[0].T
+    (out,) = ffn_part(at, 0, near.reshape(384, 2880), *hbm_weights)
+    pairs = [after(pair, out)] + from_others(pair, "y")
     grads = local_grad(at, pairs, context)
     part = grads[0].astype(F32) + core_swap(grads[1]).astype(F32)
-    total = part[0]
-    for o in (1, 2, 3):
-        total = total + shift("x", o, 4)(part[o].astype(BF)).astype(F32)
-    far = far.reshape(16, 3, 24, 2880)
+    terms = [shift("x", o, 4)(part[o].astype(BF)) for o in (1, 2, 3)]
+    out, *weights = ffn_part(at, 1, far, *hbm_weights, out)
+    terms = lax.optimization_barrier((*terms, out))[:3]
+    total = part[0] + terms[0].astype(F32) + terms[1].astype(F32) + terms[2].astype(F32)
     rows = total.reshape(2, 720, 128)
     kept = lax.dynamic_index_in_dim(rows, zh, 0, keepdims=False)
     gone = lax.dynamic_index_in_dim(rows, 1 - zh, 0, keepdims=False).astype(BF)
     came = zh_swap(gone)
-    out, *weights = ffn_first(at, after(far, gone), gate_w, up_w, down_w[0].T)
+    (out,) = ffn_part(at, 2, far, *weights, after(out, gone))
     total = (kept + after(came, out).astype(F32)).astype(BF)
     back = zh_swap(total)
-    out = ffn_part(at, 2, far, *weights, after(out, total))
+    (out,) = ffn_part(at, 3, far, *weights, after(out, total))
     back = after(back, out)
     block = jnp.concatenate([jnp.where(zh == 0, total, back), jnp.where(zh == 0, back, total)])
-    blocks = from_others(block, "x")
-    out = ffn_part(at, 3, far, *weights, after(out, block))
-    out = ffn_part(at, 0, near.reshape(384, 2880), *weights, out)
-    out = after(out, *blocks)
-    full = jnp.stack([block] + blocks)
+    full = jnp.stack([block] + from_others(block, "x"))
     grad = spread(at, full, core_swap(full)).reshape(2880, 512)
 
-    out = lax.all_to_all(out.reshape(64, 24, 2880), over + ("y",), split_axis=0, concat_axis=0, tiled=True)
-    own, sib = combine(at, out.reshape(2, 768, 2880), mine[2880:], sibling[2880:])
+    out = after(out, block).reshape(64, 24, 2880)
+    out = lax.all_to_all(out, over + ("y",), split_axis=0, concat_axis=0, tiled=True)
+    own, sib = combine(at, out.reshape(2, 768, 2880), mine[2880:], sibling[2880:], grad)
     mixed = (own + core_swap(sib).astype(F32)).astype(BF)
     return mixed.T, grad.T
 

time: 414 us -> 398 us (0.961)
  starting transfers between devices: 60.8 us -> 47.9 us
  waiting for transfers between devices: 269 us -> 259 us
  Pallas kernels: 63.3 us -> 69.7 us
    ppermute x9, waiting for transfers between devices: 89.3 us -> 218 us  [from_others(): return [shift(axis, -o, 4)(block) for o in (1, 2, 3)]]
    all_to_all x1, waiting for transfers between devices: 128 us -> 0.01 us  [local(): lax.all_to_all(out, over + ('y',), split_axis=0, concat_axis=0, tiled=True)]
    ppermute x3, waiting for transfers between devices: 36.8 us -> 2.02 us  [local(): terms = [shift('x', o, 4)(part[o].astype(BF)) for o in (1, 2, 3)]]
    all_to_all x1, waiting for transfers between devices: 0.01 us -> 10.6 us  [local(): far = lax.all_to_all(far, over, split_axis=0, concat_axis=0, tiled=True)]
    all_to_all x1, waiting for transfers between devices: 0.01 us -> 6.07 us  [local(): near = lax.all_to_all(near, over, split_axis=0, concat_axis=0, tiled=True)]
    pallas_call x4, Pallas kernels: 39.6 us -> 45.1 us  [ffn_part(): pl.pallas_call(kernel, grid_spec=pltpu.PrefetchScalarGridSpec(num_scalar_...]
    ppermute x1, starting transfers between devices: 5.43 us -> 0.46 us  [local(): mixed = (own + core_swap(sib).astype(F32)).astype(BF)]
    ppermute x9, starting transfers between devices: 12 us -> 7.52 us  [from_others(): return [shift(axis, -o, 4)(block) for o in (1, 2, 3)]]
  transfers between devices with their start and end apart: 25 -> 25, of which waited for: 12 -> 17; matrix products, arithmetic and copies ran while one was open for 2% -> 2% of each run, Pallas kernels for 15% -> 16%
where the time goes in v3:
time: 398 us; the launch traced here: 397 us
  waiting for transfers between devices  259 us (65%)
  Pallas kernels  69.7 us (18%)
  starting transfers between devices  47.9 us (12%)
  local copies, waits for them, and re-layouts  11.1 us (3%)
  other arithmetic  8.18 us (2%)
    ppermute x9, waiting for transfers between devices, from_others(): return [shift(axis, -o, 4)(block) for o in (1, 2, 3)]  218 us
    pallas_call x4, Pallas kernels, ffn_part(): pl.pallas_call(kernel, grid_spec=pltpu.PrefetchScalarGridSpec(num_scalar_...  45.1 us
    ppermute x1, waiting for transfers between devices, local(): og_other = zl_swap(og)  14.1 us
    all_to_all x1, waiting for transfers between devices, local(): far = lax.all_to_all(far, over, split_axis=0, concat_axis=0, tiled=True)  10.6 us
    all_to_all x1, starting transfers between devices, local(): lax.all_to_all(out, over + ('y',), split_axis=0, concat_axis=0, tiled=True)  9.39 us
    unnamed x28, local copies, waits for them, and re-layouts  8.27 us
  transfers between devices with their start and end apart: 25, of which 17 were waited for; matrix products, arithmetic and copies ran while one was open for 2% of the time, Pallas kernels for 16%

profile of v3, /device:TPU:5, one launch (start us, length us, event | category | flops | bytes accessed | tf_op | source)
XLA Modules:
  0.0 396.6 jit_solution(11181438549204811532)
XLA Ops:
  5.6 2.7 collective-permute-start
  12.7 14.1 %collective-permute-done.6 = bf16[2880,128]{1,0:T(8,128)(2,1)} collective-permute-done((bf16[2880,128]{1,0:T(8,128)(2,1)}, bf16[2880,128]{1,0:T(8,128)(2,1)}, u32[]{:S(2)}, u32[]{:S(2)}) %collective-permute-start.6) | collective-permute-done | bytes 737312 | tf_op jit(solution)/shard_map/ppermute | solution.py:339
  27.4 7.7 %all-to-all-start = ((bf16[16,24,2880]{2,1,0:T(8,128)(2,1)}), bf16[16,24,2880]{2,1,0:T(8,128)(2,1)}, u32[]{:S(2)}, u32[]{:S(2)}) async-start(bf16[16,24,2880]{2,1,0:T(8,128)(2,1)} %bitcast.12), calls=%async_computation | async-start | bytes 4521984 | tf_op jit(solution)/shard_map/all_to_all | solution.py:343
  37.9 15.2 %collective-permute-done.2.refs_2_ = bf16[2896,128]{1,0:T(8,128)(2,1)S(1)} collective-permute-done((bf16[2896,128]{1,0:T(8,128)(2,1)S(1)}, bf16[2896,128]{1,0:T(8,128)(2,1)S(1)}, u32[]{:S(2)}, u32[]{:S(2)}) %collective-permute-start.2) | collective-permute-done | bytes 741408 | tf_op jit(solution)/shard_map/ppermute | solution.py:323
  58.6 4.7 %far_rows.1 = bf16[2,8,3,24,2880]{4,3,2,1,0:T(8,128)(2,1)} custom-call(s32[5]{0:T(128)S(1)} %stack.47.at_ref, bf16[2896,128]{1,0:T(8,128)(2,1)S(1)} %collective-permute-done.refs_0_, bf16[2896,128]{1,0:T(8,128)(2,1)S(1)} %collective-permute-done.1.refs_1_, bf16[2896,128]{1,0:T(8,128)(2,1)S(1)} %collective-permute-done.2.refs_2_, ...), custom_call_target="tpu_custom_call" | custom-call | flops 849346560 | bytes 11000000 | tf_op jit(solution)/shard_map/far_rows/pallas_call | solution.py:128
  63.3 6.1 %all-to-all-done = bf16[16,24,2880]{2,1,0:T(8,128)(2,1)} async-done(((bf16[16,24,2880]{2,1,0:T(8,128)(2,1)}), bf16[16,24,2880]{2,1,0:T(8,128)(2,1)}, u32[]{:S(2)}, u32[]{:S(2)}) %all-to-all-start) | async-done | bytes 2211872 | tf_op jit(solution)/shard_map/all_to_all | solution.py:343
  69.4 4.9 %all-to-all-start.1 = ((bf16[16,72,2880]{2,1,0:T(8,128)(2,1)}), bf16[16,72,2880]{2,1,0:T(8,128)(2,1)}, u32[]{:S(2)}, u32[]{:S(2)}) async-start(bf16[16,72,2880]{2,1,0:T(8,128)(2,1)} %bitcast.67), calls=%async_computation.1 | async-start | bytes 13565952 | tf_op jit(solution)/shard_map/all_to_all | solution.py:349
  75.9 13.3 %ffn_part0.1.into_ref = bf16[16,4,24,2880]{3,2,1,0:T(8,128)(2,1)} custom-call(s32[5]{0:T(128)} %copy-done.5, bf16[384,2880]{1,0:T(8,128)(2,1)} %bitcast.17.x_ref, bf16[1,2880,768]{2,1,0:T(8,128)(2,1)} %g_hbm.3, bf16[1,2880,768]{2,1,0:T(8,128)(2,1)} %u_hbm.3, bf16[2880,768]{1,0:T(8,128)(2,1)} %bitcast.70), custom_call_target="tpu_custom_call" | custom-call | flops 5096079360 | bytes 18000000 | tf_op jit(solution)/shard_map/ffn_part0/pallas_call | solution.py:191
  89.3 15.9 %collective-permute-done.8.p1_ref = bf16[2,2880,128]{2,1,0:T(8,128)(2,1)S(1)} collective-permute-done((bf16[2,2880,128]{2,1,0:T(8,128)(2,1)S(1)}, bf16[2,2880,128]{2,1,0:T(8,128)(2,1)S(1)}, u32[]{:S(2)}, u32[]{:S(2)}) %collective-permute-start.8) | collective-permute-done | bytes 1474592 | tf_op jit(solution)/shard_map/ppermute | solution.py:323
  107.5 35.0 %collective-permute-done.10.p3_ref = bf16[2,2880,128]{2,1,0:T(8,128)(2,1)} collective-permute-done((bf16[2,2880,128]{2,1,0:T(8,128)(2,1)S(1)}, bf16[2,2880,128]{2,1,0:T(8,128)(2,1)}, u32[]{:S(2)}, u32[]{:S(2)}) %collective-permute-start.10) | collective-permute-done | bytes 1474592 | tf_op jit(solution)/shard_map/ppermute | solution.py:323
  146.5 5.9 %local_grad.1 = bf16[2,4,1440,128]{3,2,1,0:T(8,128)(2,1)S(1)} custom-call(s32[5]{0:T(128)S(1)} %copy-done.6, bf16[2,2880,128]{2,1,0:T(8,128)(2,1)S(1)} %copy-done.2, bf16[2,2880,128]{2,1,0:T(8,128)(2,1)S(1)} %copy-done.12, bf16[2,2880,128]{2,1,0:T(8,128)(2,1)} %collective-permute-done.9.p2_ref, bf16[2,2880,128]{2,1,0:T(8,128)(2,1)} %collective-permute-done.10.p3_ref, ...), custom_call_target="tpu_custom_call" | custom-call | flops 3019898880 | bytes 10000000 | tf_op jit(solution)/shard_map/local_grad/pallas_call | solution.py:279
  154.2 3.2 collective-permute-done.11
  157.5 3.4 fusion.7
  163.3 10.6 %all-to-all-done.1 = bf16[16,72,2880]{2,1,0:T(8,128)(2,1)} async-done(((bf16[16,72,2880]{2,1,0:T(8,128)(2,1)}), bf16[16,72,2880]{2,1,0:T(8,128)(2,1)}, u32[]{:S(2)}, u32[]{:S(2)}) %all-to-all-start.1) | async-done | bytes 6635552 | tf_op jit(solution)/shard_map/all_to_all | solution.py:349
  173.8 13.2 %ffn_part1.1 = (bf16[16,4,24,2880]{3,2,1,0:T(8,128)(2,1)}, bf16[2880,768]{1,0:T(8,128)(2,1)S(1)}, bf16[2880,768]{1,0:T(8,128)(2,1)S(1)}, bf16[2880,768]{1,0:T(8,128)(2,1)S(1)}) custom-call(s32[5]{0:T(128)} %copy-done.5, bf16[16,3,24,2880]{3,2,1,0:T(8,128)(2,1)} %bitcast.14.x_ref, bf16[1,2880,768]{2,1,0:T(8,128)(2,1)} %g_hbm.3, ...), custom_call_target="tpu_custom_call", output_to_operand_aliasing={{0}: (5, {})} | custom-call | flops 5096079360 | bytes 18000000 | tf_op jit(solution)/shard_map/ffn_part1/pallas_call | solution.py:191
  191.7 9.3 %ffn_part2.1.into_ref = bf16[16,4,24,2880]{3,2,1,0:T(8,128)(2,1)} custom-call(s32[5]{0:T(128)S(1)} %copy-done.7, bf16[16,3,24,2880]{3,2,1,0:T(8,128)(2,1)} %bitcast.14.x_ref, bf16[2880,768]{1,0:T(8,128)(2,1)S(1)} %get-tuple-element.21.g_ref, bf16[2880,768]{1,0:T(8,128)(2,1)S(1)} %get-tuple-element.22.u_ref, ...), custom_call_target="tpu_custom_call", output_to_operand_aliasing={{}: (5, {})} | custom-call | flops 5096079360 | bytes 18000000 | tf_op jit(solution)/shard_map/ffn_part2/pallas_call | solution.py:191
  203.1 9.3 %ffn_part3.1 = bf16[16,4,24,2880]{3,2,1,0:T(8,128)(2,1)} custom-call(s32[5]{0:T(128)S(1)} %copy-done.7, bf16[16,3,24,2880]{3,2,1,0:T(8,128)(2,1)} %bitcast.14.x_ref, bf16[2880,768]{1,0:T(8,128)(2,1)S(1)} %get-tuple-element.21.g_ref, bf16[2880,768]{1,0:T(8,128)(2,1)S(1)} %get-tuple-element.22.u_ref, ...), custom_call_target="tpu_custom_call", output_to_operand_aliasing={{}: (5, {})} | custom-call | flops 5096079360 | bytes 18000000 | tf_op jit(solution)/shard_map/ffn_part3/pallas_call | solution.py:191
  212.5 9.4 %all-to-all-start.2 = ((bf16[64,24,2880]{2,1,0:T(8,128)(2,1)}), bf16[64,24,2880]{2,1,0:T(8,128)(2,1)}, u32[]{:S(2)}, u32[]{:S(2)}) async-start(bf16[64,24,2880]{2,1,0:T(8,128)(2,1)} %bitcast.66), calls=%async_computation.2 | async-start | bytes 18087936 | tf_op jit(solution)/shard_map/all_to_all | solution.py:375
  224.6 115.4 %collective-permute-done.19 = bf16[1440,128]{1,0:T(8,128)(2,1)S(1)} collective-permute-done((bf16[1440,128]{1,0:T(8,128)(2,1)S(1)}, bf16[1440,128]{1,0:T(8,128)(2,1)S(1)}, u32[]{:S(2)}, u32[]{:S(2)}) %collective-permute-start.19) | collective-permute-done | bytes 368672 | tf_op jit(solution)/shard_map/ppermute | solution.py:323
  339.9 26.1 %collective-permute-done.18 = bf16[1440,128]{1,0:T(8,128)(2,1)S(1)} collective-permute-done((bf16[1440,128]{1,0:T(8,128)(2,1)S(1)}, bf16[1440,128]{1,0:T(8,128)(2,1)S(1)}, u32[]{:S(2)}, u32[]{:S(2)}) %collective-permute-start.18) | collective-permute-done | bytes 368672 | tf_op jit(solution)/shard_map/ppermute | solution.py:323
  366.0 8.7 %collective-permute-done.17 = bf16[1440,128]{1,0:T(8,128)(2,1)S(1)} collective-permute-done((bf16[1440,128]{1,0:T(8,128)(2,1)S(1)}, bf16[1440,128]{1,0:T(8,128)(2,1)S(1)}, u32[]{:S(2)}, u32[]{:S(2)}) %collective-permute-start.17) | collective-permute-done | bytes 368672 | tf_op jit(solution)/shard_map/ppermute | solution.py:323
  374.9 4.3 %collective-permute-start.20 = (bf16[4,1440,128]{2,1,0:T(8,128)(2,1)S(1)}, bf16[4,1440,128]{2,1,0:T(8,128)(2,1)S(1)}, u32[]{:S(2)}, u32[]{:S(2)}) collective-permute-start(bf16[4,1440,128]{2,1,0:T(8,128)(2,1)S(1)} %pad_maximum_fusion.1.own_ref), channel_id=1, source_target_pairs={{0,8},{8,0},{1,9},{9,1},{2,10},{10,2},{3,11},{11,3},{4,12},{12,4},... | collective-permute-start | bytes 4423688 | tf_op jit(solution)/shard_map/ppermute | solution.py:372
  382.0 3.5 spread.1
  385.5 7.7 %combine.1 = (f32[2880,128]{1,0:T(8,128)S(1)}, bf16[2880,128]{1,0:T(8,128)(2,1)S(1)}) custom-call(s32[5]{0:T(128)S(1)} %copy-done.7, bf16[2,768,2880]{2,1,0:T(8,128)(2,1)} %bitcast.29.y_ref, bf16[16,128]{1,0:T(8,128)(2,1)S(1)} %slice.41.own_tail_ref, bf16[16,128]{1,0:T(8,128)(2,1)S(1)} %slice.42.sib_tail_ref, f32[2880,512]{1,0:T(8,128)} %bitcast.68), custom_call_target="tpu_custom_call" | custom-call | flops 2264924160 | bytes 12000000 | tf_op jit(solution)/shard_map/combine/pallas_call | solution.py:245
  (80 shorter events, 46.3 us)
Async XLA Ops:
  4.8 5.2 %collective-permute-start.7 = (bf16[2896,128]{1,0:T(8,128)(2,1)S(1)}, bf16[2896,128]{1,0:T(8,128)(2,1)S(1)}, u32[]{:S(2)}, u32[]{:S(2)}) collective-permute-start(bf16[2896,128]{1,0:T(8,128)(2,1)S(1)} %place.1.own_ref), channel_id=1, source_target_pairs={{0,8},{8,0},{1,9},{9,1},{2,10},{10,2},{3,11},{11,3},{4,12},{12,4},... | collective-permute-start | bytes 2224136 | tf_op jit(solution)/shard_map/ppermute | solution.py:340
  5.6 21.2 %collective-permute-start = (bf16[2896,128]{1,0:T(8,128)(2,1)S(1)}, bf16[2896,128]{1,0:T(8,128)(2,1)S(1)}, u32[]{:S(2)}, u32[]{:S(2)}) collective-permute-start(bf16[2896,128]{1,0:T(8,128)(2,1)S(1)} %place.1.own_ref), channel_id=1, source_target_pairs={{0,6},{2,0},{4,2},{6,4},{1,7},{3,1},{5,3},{7,5},{8,14},{10,8},{12,... | collective-permute-start | bytes 2224136 | tf_op jit(solution)/shard_map/ppermute | solution.py:323
  8.4 19.0 %collective-permute-start.4 = (bf16[2896,128]{1,0:T(8,128)(2,1)S(1)}, bf16[2896,128]{1,0:T(8,128)(2,1)S(1)}, u32[]{:S(2)}, u32[]{:S(2)}) collective-permute-start(bf16[2896,128]{1,0:T(8,128)(2,1)S(1)} %place.1.own_ref), channel_id=1, source_target_pairs={{0,2},{2,4},{4,6},{6,0},{1,3},{3,5},{5,7},{7,1},{8,10},{10,12},{12... | collective-permute-start | bytes 2224136 | tf_op jit(solution)/shard_map/ppermute | solution.py:323
  8.4 18.4 %collective-permute-start.6 = (bf16[2880,128]{1,0:T(8,128)(2,1)}, bf16[2880,128]{1,0:T(8,128)(2,1)}, u32[]{:S(2)}, u32[]{:S(2)}) collective-permute-start(bf16[2880,128]{1,0:T(8,128)(2,1)} %bitcast.9), channel_id=1, source_target_pairs={{0,1},{1,0},{2,3},{3,2},{4,5},{5,4},{6,7},{7,6},{8,9},{9,8},{10,11... | collective-permute-start | bytes 2211848 | tf_op jit(solution)/shard_map/ppermute | solution.py:339
  27.4 42.0 %all-to-all-start = ((bf16[16,24,2880]{2,1,0:T(8,128)(2,1)}), bf16[16,24,2880]{2,1,0:T(8,128)(2,1)}, u32[]{:S(2)}, u32[]{:S(2)}) async-start(bf16[16,24,2880]{2,1,0:T(8,128)(2,1)} %bitcast.12), calls=%async_computation | async-start | bytes 4521984 | tf_op jit(solution)/shard_map/all_to_all | solution.py:343
  35.1 18.0 %collective-permute-start.2 = (bf16[2896,128]{1,0:T(8,128)(2,1)S(1)}, bf16[2896,128]{1,0:T(8,128)(2,1)S(1)}, u32[]{:S(2)}, u32[]{:S(2)}) collective-permute-start(bf16[2896,128]{1,0:T(8,128)(2,1)S(1)} %place.1.own_ref), channel_id=1, source_target_pairs={{0,4},{2,6},{4,0},{6,2},{1,5},{3,7},{5,1},{7,3},{8,12},{10,14},{12... | collective-permute-start | bytes 2224136 | tf_op jit(solution)/shard_map/ppermute | solution.py:323
  35.5 21.6 %collective-permute-start.1 = (bf16[2896,128]{1,0:T(8,128)(2,1)S(1)}, bf16[2896,128]{1,0:T(8,128)(2,1)S(1)}, u32[]{:S(2)}, u32[]{:S(2)}) collective-permute-start(bf16[2896,128]{1,0:T(8,128)(2,1)S(1)} %collective-permute-done.refs_0_), channel_id=1, source_target_pairs={{0,8},{8,0},{1,9},{9,1},{2,10},{10,2},{3,11},{11,3},{4,12},{12,4},... | collective-permute-start | bytes 2224136 | tf_op jit(solution)/shard_map/ppermute | solution.py:346
  53.1 4.4 %collective-permute-start.3 = (bf16[2896,128]{1,0:T(8,128)(2,1)S(1)}, bf16[2896,128]{1,0:T(8,128)(2,1)S(1)}, u32[]{:S(2)}, u32[]{:S(2)}) collective-permute-start(bf16[2896,128]{1,0:T(8,128)(2,1)S(1)} %collective-permute-done.2.refs_2_), channel_id=1, source_target_pairs={{0,8},{8,0},{1,9},{9,1},{2,10},{10,2},{3,11},{11,3},{4,12},{12,4},... | collective-permute-start | bytes 2224136 | tf_op jit(solution)/shard_map/ppermute | solution.py:346
  55.7 2.9 collective-permute-start.5
  69.4 104.5 %all-to-all-start.1 = ((bf16[16,72,2880]{2,1,0:T(8,128)(2,1)}), bf16[16,72,2880]{2,1,0:T(8,128)(2,1)}, u32[]{:S(2)}, u32[]{:S(2)}) async-start(bf16[16,72,2880]{2,1,0:T(8,128)(2,1)} %bitcast.67), calls=%async_computation.1 | async-start | bytes 13565952 | tf_op jit(solution)/shard_map/all_to_all | solution.py:349
  74.2 31.0 %collective-permute-start.8 = (bf16[2,2880,128]{2,1,0:T(8,128)(2,1)S(1)}, bf16[2,2880,128]{2,1,0:T(8,128)(2,1)S(1)}, u32[]{:S(2)}, u32[]{:S(2)}) collective-permute-start(bf16[2,2880,128]{2,1,0:T(8,128)(2,1)S(1)} %pad_maximum_fusion.p0_ref), channel_id=1, source_target_pairs={{0,6},{2,0},{4,2},{6,4},{1,7},{3,1},{5,3},{7,5},{8,14},{10,8},{12,... | collective-permute-start | bytes 4423688 | tf_op jit(solution)/shard_map/ppermute | solution.py:323
  75.3 32.3 %collective-permute-start.9 = (bf16[2,2880,128]{2,1,0:T(8,128)(2,1)S(1)}, bf16[2,2880,128]{2,1,0:T(8,128)(2,1)}, u32[]{:S(2)}, u32[]{:S(2)}) collective-permute-start(bf16[2,2880,128]{2,1,0:T(8,128)(2,1)S(1)} %pad_maximum_fusion.p0_ref), channel_id=1, source_target_pairs={{0,4},{2,6},{4,0},{6,2},{1,5},{3,7},{5,1},{7,3},{8,12},{10,14},{12... | collective-permute-start | bytes 4423688 | tf_op jit(solution)/shard_map/ppermute | solution.py:323
  75.5 67.0 %collective-permute-start.10 = (bf16[2,2880,128]{2,1,0:T(8,128)(2,1)S(1)}, bf16[2,2880,128]{2,1,0:T(8,128)(2,1)}, u32[]{:S(2)}, u32[]{:S(2)}) collective-permute-start(bf16[2,2880,128]{2,1,0:T(8,128)(2,1)S(1)} %pad_maximum_fusion.p0_ref), channel_id=1, source_target_pairs={{0,2},{2,4},{4,6},{6,0},{1,3},{3,5},{5,7},{7,1},{8,10},{10,12},{12... | collective-permute-start | bytes 4423688 | tf_op jit(solution)/shard_map/ppermute | solution.py:323
  153.7 3.8 collective-permute-start.11
  160.9 26.1 %collective-permute-start.12 = (bf16[1440,128]{1,0:T(8,128)(2,1)S(1)}, bf16[1440,128]{1,0:T(8,128)(2,1)S(1)}, u32[]{:S(2)}, u32[]{:S(2)}) collective-permute-start(bf16[1440,128]{1,0:T(8,128)(2,1)S(1)} %get-tuple-element.40), channel_id=1, source_target_pairs={{0,32},{32,64},{64,96},{96,0},{1,33},{33,65},{65,97},{97,1},{2,34}... | collective-permute-start | bytes 1105928 | tf_op jit(solution)/shard_map/ppermute | solution.py:357
  161.9 27.2 %collective-permute-start.13 = (bf16[1440,128]{1,0:T(8,128)(2,1)S(1)}, bf16[1440,128]{1,0:T(8,128)(2,1)S(1)}, u32[]{:S(2)}, u32[]{:S(2)}) collective-permute-start(bf16[1440,128]{1,0:T(8,128)(2,1)S(1)} %get-tuple-element.39), channel_id=1, source_target_pairs={{0,64},{32,96},{64,0},{96,32},{1,65},{33,97},{65,1},{97,33},{2,66}... | collective-permute-start | bytes 1105928 | tf_op jit(solution)/shard_map/ppermute | solution.py:357
  162.8 26.2 %collective-permute-start.14 = (bf16[1440,128]{1,0:T(8,128)(2,1)S(1)}, bf16[1440,128]{1,0:T(8,128)(2,1)S(1)}, u32[]{:S(2)}, u32[]{:S(2)}) collective-permute-start(bf16[1440,128]{1,0:T(8,128)(2,1)S(1)} %get-tuple-element.38), channel_id=1, source_target_pairs={{0,96},{32,0},{64,32},{96,64},{1,97},{33,1},{65,33},{97,65},{2,98}... | collective-permute-start | bytes 1105928 | tf_op jit(solution)/shard_map/ppermute | solution.py:357
  190.4 10.6 %collective-permute-start.15 = (bf16[720,128]{1,0:T(8,128)(2,1)S(1)}, bf16[720,128]{1,0:T(8,128)(2,1)S(1)}, u32[]{:S(2)}, u32[]{:S(2)}) collective-permute-start(bf16[720,128]{1,0:T(8,128)(2,1)S(1)} %fusion.5), channel_id=1, source_target_pairs={{0,16},{16,0},{1,17},{17,1},{2,18},{18,2},{3,19},{19,3},{4,20},{20... | collective-permute-start | bytes 552968 | tf_op jit(solution)/shard_map/ppermute | solution.py:364
  201.0 11.4 %collective-permute-start.16 = (bf16[720,128]{1,0:T(8,128)(2,1)S(1)}, bf16[720,128]{1,0:T(8,128)(2,1)S(1)}, u32[]{:S(2)}, u32[]{:S(2)}) collective-permute-start(bf16[720,128]{1,0:T(8,128)(2,1)S(1)} %fusion.4), channel_id=1, source_target_pairs={{0,16},{16,0},{1,17},{17,1},{2,18},{18,2},{3,19},{19,3},{4,20},{20... | collective-permute-start | bytes 552968 | tf_op jit(solution)/shard_map/ppermute | solution.py:367
  212.5 173.0 %all-to-all-start.2 = ((bf16[64,24,2880]{2,1,0:T(8,128)(2,1)}), bf16[64,24,2880]{2,1,0:T(8,128)(2,1)}, u32[]{:S(2)}, u32[]{:S(2)}) async-start(bf16[64,24,2880]{2,1,0:T(8,128)(2,1)} %bitcast.66), calls=%async_computation.2 | async-start | bytes 18087936 | tf_op jit(solution)/shard_map/all_to_all | solution.py:375
  221.9 118.0 %collective-permute-start.19 = (bf16[1440,128]{1,0:T(8,128)(2,1)S(1)}, bf16[1440,128]{1,0:T(8,128)(2,1)S(1)}, u32[]{:S(2)}, u32[]{:S(2)}) collective-permute-start(bf16[1440,128]{1,0:T(8,128)(2,1)S(1)} %get-tuple-element.42), channel_id=1, source_target_pairs={{0,32},{32,64},{64,96},{96,0},{1,33},{33,65},{65,97},{97,1},{2,34}... | collective-permute-start | bytes 1105928 | tf_op jit(solution)/shard_map/ppermute | solution.py:323
  222.9 143.1 %collective-permute-start.18 = (bf16[1440,128]{1,0:T(8,128)(2,1)S(1)}, bf16[1440,128]{1,0:T(8,128)(2,1)S(1)}, u32[]{:S(2)}, u32[]{:S(2)}) collective-permute-start(bf16[1440,128]{1,0:T(8,128)(2,1)S(1)} %get-tuple-element.42), channel_id=1, source_target_pairs={{0,64},{32,96},{64,0},{96,32},{1,65},{33,97},{65,1},{97,33},{2,66}... | collective-permute-start | bytes 1105928 | tf_op jit(solution)/shard_map/ppermute | solution.py:323
  223.4 151.3 %collective-permute-start.17 = (bf16[1440,128]{1,0:T(8,128)(2,1)S(1)}, bf16[1440,128]{1,0:T(8,128)(2,1)S(1)}, u32[]{:S(2)}, u32[]{:S(2)}) collective-permute-start(bf16[1440,128]{1,0:T(8,128)(2,1)S(1)} %get-tuple-element.42), channel_id=1, source_target_pairs={{0,96},{32,0},{64,32},{96,64},{1,97},{33,1},{65,33},{97,65},{2,98}... | collective-permute-start | bytes 1105928 | tf_op jit(solution)/shard_map/ppermute | solution.py:323
  374.9 7.2 %collective-permute-start.20 = (bf16[4,1440,128]{2,1,0:T(8,128)(2,1)S(1)}, bf16[4,1440,128]{2,1,0:T(8,128)(2,1)S(1)}, u32[]{:S(2)}, u32[]{:S(2)}) collective-permute-start(bf16[4,1440,128]{2,1,0:T(8,128)(2,1)S(1)} %pad_maximum_fusion.1.own_ref), channel_id=1, source_target_pairs={{0,8},{8,0},{1,9},{9,1},{2,10},{10,2},{3,11},{11,3},{4,12},{12,4},... | collective-permute-start | bytes 4423688 | tf_op jit(solution)/shard_map/ppermute | solution.py:372
  (15 other events, 179.5 us)

commit v4 on v2

v4 whole, which is shorter than its diff:
```python
import functools

import jax
import jax.numpy as jnp
from jax import lax
from jax.experimental import pallas as pl
from jax.experimental.pallas import tpu as pltpu
from jax.sharding import Mesh, PartitionSpec as P

CAP = 12
BF = jnp.bfloat16
F32 = jnp.float32
NT = (((1,), (1,)), ((), ()))


def place(ids, shifts, lim):
    label = lax.broadcasted_iota(jnp.int32, (64, 128), 0)
    earlier = (
        lax.broadcasted_iota(jnp.int32, (128, 128), 0)
        < lax.broadcasted_iota(jnp.int32, (128, 128), 1)
    ).astype(F32).astype(BF)
    rows = [ids[k : k + 1, :] for k in range(4)]
    hots = [(r == label).astype(F32) for r in rows]
    hot = hots[0] + hots[1] + hots[2] + hots[3]
    before = jnp.dot(hot.astype(BF), earlier, preferred_element_type=F32)
    spilled, seconds, second_hots, first_ranks = [], [], [], []
    for k in range(4):
        rank = jnp.sum(before * hots[k], axis=0, keepdims=True)
        limit = jnp.sum(lim * hots[k], axis=0, keepdims=True)
        spill = rank >= limit
        second = (rows[k] + shifts[k : k + 1, :]) & 63
        first_ranks.append(rank)
        spilled.append(spill)
        seconds.append(second)
        second_hots.append((second == label).astype(F32))
    spill_hots = [h * s.astype(F32) for h, s in zip(second_hots, spilled)]
    total = spill_hots[0] + spill_hots[1] + spill_hots[2] + spill_hots[3]
    run = jnp.dot(total.astype(BF), earlier, preferred_element_type=F32)
    out = []
    for k in range(4):
        rank = jnp.sum(run * second_hots[k], axis=0, keepdims=True)
        run = run + spill_hots[k]
        limit = jnp.sum(lim * second_hots[k], axis=0, keepdims=True)
        slot = jnp.where(spilled[k], limit + rank, first_ranks[k]).astype(jnp.int32)
        target = jnp.where(spilled[k], seconds[k], rows[k])
        out.append((target, slot, slot < CAP))
    return out


def place_kernel(tok_ref, ids_ref, shift_ref, raw_ref, lim_ref, out_ref):
    out_ref[:2880, :] = tok_ref[...]
    places = place(ids_ref[...], shift_ref[...], lim_ref[...])
    raw = raw_ref[...]
    share = raw / jnp.sum(raw, axis=0, keepdims=True)
    rows = [t.astype(F32) for t, _, _ in places]
    rows += [jnp.where(k, s, -1).astype(F32) for _, s, k in places]
    rows += [share, jnp.zeros((4, 128), F32)]
    out_ref[2880:, :] = jnp.concatenate(rows, axis=0).astype(BF)


def place_call(tok, ids, shifts, raw, lim):
    vm = pl.BlockSpec(memory_space=pltpu.VMEM)
    return pl.pallas_call(
        place_kernel,
        in_specs=[vm] * 5,
        out_specs=vm,
        out_shape=jax.ShapeDtypeStruct((2896, 128), BF),
        compiler_params=pltpu.CompilerParams(vmem_limit_bytes=16 << 20),
        cost_estimate=pl.CostEstimate(flops=1 << 22, bytes_accessed=1_500_000, transcendentals=0),
        name="place",
    )(tok, ids, shifts, raw, lim)


def slots_of(tail, core):
    tail = tail.astype(F32)
    out = []
    for k in range(4):
        target = tail[k : k + 1].astype(jnp.int32)
        slot = tail[4 + k : 5 + k].astype(jnp.int32)
        mine = (slot >= 0) & (((target >> 2) & 1) == core)
        out.append((mine, (target >> 3) * 4 + (target & 3), slot, tail[8 + k : 9 + k]))
    return out


def row_weights(tail, core, side, chunk, weighted):
    low, size = ((0, 8), (8, 16))[chunk]
    at = lax.broadcasted_iota(jnp.int32, (32 * size, 128), 0)
    total = jnp.zeros((32 * size, 128), F32)
    for mine, index, slot, share in slots_of(tail, core):
        row = slot + (side * CAP - low)
        row = jnp.where(mine & (row >= 0) & (row < size), index * size + row, -1)
        total = total + jnp.where(row == at, share if weighted else 1.0, 0.0)
    return total


def rows0_kernel(at_ref, own_ref, out_ref):
    hot = row_weights(own_ref[2880:, :], at_ref[0], 0, 0, False).astype(BF)
    got = lax.dot_general(hot, own_ref[:2880, :], NT, preferred_element_type=F32).astype(BF)
    out_ref[0] = got
    out_ref[1] = got


def rows0(at, own):
    vm = pl.BlockSpec(memory_space=pltpu.VMEM)
    return pl.pallas_call(
        rows0_kernel,
        grid=(1,),
        in_specs=[pl.BlockSpec(memory_space=pltpu.SMEM), vm],
        out_specs=pl.BlockSpec((2, 256, 2880), lambda i: (0, 0, 0)),
        out_shape=pltpu.HBM((2, 256, 2880), BF),
        compiler_params=pltpu.CompilerParams(vmem_limit_bytes=32 << 20),
        cost_estimate=pl.CostEstimate(flops=2 * 256 * 128 * 2880, bytes_accessed=3_700_000, transcendentals=0),
        name="rows0",
    )(at, own)


def rows1_kernel(at_ref, own_ref, sib_ref, out_ref, hot_ref):
    step = pl.program_id(0)

    @pl.when(step == 0)
    def _():
        for side, ref in enumerate((own_ref, sib_ref)):
            hot_ref[:, 128 * side : 128 * side + 128] = row_weights(
                ref[2880:, :], at_ref[0], side, 1, False
            ).astype(BF)

    both = jnp.concatenate([own_ref[:2880, :], sib_ref[:2880, :]], axis=1)
    hot = hot_ref[pl.ds(pl.multiple_of(step * 256, 256), 256), :]
    got = lax.dot_general(hot, both, NT, preferred_element_type=F32).astype(BF)
    out_ref[0] = got
    out_ref[1] = got


def rows1(at, own, sib):
    vm = pl.BlockSpec(memory_space=pltpu.VMEM)
    return pl.pallas_call(
        rows1_kernel,
        grid=(2,),
        in_specs=[pl.BlockSpec(memory_space=pltpu.SMEM), vm, vm],
        out_specs=pl.BlockSpec((2, 256, 2880), lambda i: (0, i, 0)),
        out_shape=pltpu.HBM((2, 512, 2880), BF),
        scratch_shapes=[pltpu.VMEM((512, 256), BF)],
        compiler_params=pltpu.CompilerParams(vmem_limit_bytes=32 << 20),
        cost_estimate=pl.CostEstimate(flops=2 * 512 * 256 * 2880, bytes_accessed=7_400_000, transcendentals=0),
        name="rows1",
    )(at, own, sib)


def ffn_kernel(x_ref, g_hbm, u_hbm, d_hbm, out_ref, g_ref, u_ref, d_ref, sems):
    step = pl.program_id(0)
    copies = [
        pltpu.make_async_copy(g_hbm.at[0], g_ref, sems.at[0]),
        pltpu.make_async_copy(u_hbm.at[0], u_ref, sems.at[1]),
        pltpu.make_async_copy(d_hbm, d_ref, sems.at[2]),
    ]

    @pl.when(step == 0)
    def _():
        for c in copies:
            c.start()
        copies[0].wait()

    x = x_ref[...]
    gating = jnp.dot(x, g_ref[...], preferred_element_type=F32)

    @pl.when(step == 0)
    def _():
        copies[1].wait()

    upward = jnp.dot(x, u_ref[...], preferred_element_type=F32)
    active = ((upward + 1.0) * gating * jax.nn.sigmoid(1.702 * gating)).astype(BF)

    @pl.when(step == 0)
    def _():
        copies[2].wait()

    out_ref[...] = lax.dot_general(active, d_ref[...], NT, preferred_element_type=F32).astype(BF)


def ffn(x, g, u, d_t):
    count = x.shape[0]
    hbm = pl.BlockSpec(memory_space=pltpu.HBM)
    held = pltpu.VMEM((2880, 768), BF)
    return pl.pallas_call(
        ffn_kernel,
        grid=(count // 512,),
        in_specs=[pl.BlockSpec((512, 2880), lambda i: (i, 0)), hbm, hbm, hbm],
        out_specs=pl.BlockSpec((512, 2880), lambda i: (i, 0)),
        out_shape=pltpu.HBM((count, 2880), BF),
        scratch_shapes=[held, held, held, pltpu.SemaphoreType.DMA((3,))],
        compiler_params=pltpu.CompilerParams(vmem_limit_bytes=58 << 20),
        cost_estimate=pl.CostEstimate(
            flops=6 * count * 2880 * 768, bytes_accessed=13_300_000 + count * 2880 * 4, transcendentals=count * 768
        ),
        name="ffn%d" % count,
    )(x, g, u, d_t)


def combine0_kernel(at_ref, y_ref, tail_ref, out_ref):
    w = row_weights(tail_ref[...], at_ref[0], 0, 0, True).T.astype(BF)
    out_ref[...] = jnp.dot(w, y_ref[0], preferred_element_type=F32) + jnp.dot(
        w, y_ref[1], preferred_element_type=F32
    )


def combine0(at, y, tail):
    vm = pl.BlockSpec(memory_space=pltpu.VMEM)
    return pl.pallas_call(
        combine0_kernel,
        in_specs=[pl.BlockSpec(memory_space=pltpu.SMEM), vm, vm],
        out_specs=vm,
        out_shape=jax.ShapeDtypeStruct((128, 2880), F32),
        compiler_params=pltpu.CompilerParams(vmem_limit_bytes=24 << 20),
        cost_estimate=pl.CostEstimate(flops=4 * 256 * 128 * 2880, bytes_accessed=4_400_000, transcendentals=0),
        name="combine0",
    )(at, y, tail)


def combine1_kernel(at_ref, y_ref, own_tail_ref, sib_tail_ref, first_ref, own_ref, sib_ref, w_ref, acc_ref):
    step = pl.program_id(0)

    @pl.when(step == 0)
    def _():
        for side, ref in enumerate((own_tail_ref, sib_tail_ref)):
            w = row_weights(ref[...], at_ref[0], side, 1, True).T.astype(BF)
            for b in range(4):
                w_ref[b, 128 * side : 128 * side + 128, :] = w[:, 128 * b : 128 * b + 128]
        acc_ref[:128, :] = first_ref[...]
        acc_ref[128:, :] = jnp.zeros((128, 2880), F32)

    w = w_ref[step]
    acc_ref[...] += jnp.dot(w, y_ref[0], preferred_element_type=F32) + jnp.dot(
        w, y_ref[1], preferred_element_type=F32
    )

    @pl.when(step == 3)
    def _():
        own_ref[...] = acc_ref[:128, :].T
        sib_ref[...] = acc_ref[128:, :].T.astype(BF)


def combine1(at, y, own_tail, sib_tail, first):
    vm = pl.BlockSpec(memory_space=pltpu.VMEM)
    return pl.pallas_call(
        combine1_kernel,
        grid=(4,),
        in_specs=[
            pl.BlockSpec(memory_space=pltpu.SMEM),
            pl.BlockSpec((2, 128, 2880), lambda i: (0, i, 0)),
            vm,
            vm,
            vm,
        ],
        out_specs=[pl.BlockSpec((2880, 128), lambda i: (0, 0))] * 2,
        out_shape=[jax.ShapeDtypeStruct((2880, 128), F32), jax.ShapeDtypeStruct((2880, 128), BF)],
        scratch_shapes=[pltpu.VMEM((4, 256, 128), BF), pltpu.VMEM((256, 2880), F32)],
        compiler_params=pltpu.CompilerParams(vmem_limit_bytes=48 << 20),
        cost_estimate=pl.CostEstimate(flops=4 * 512 * 256 * 2880, bytes_accessed=9_000_000, transcendentals=0),
        name="combine1",
    )(at, y, own_tail, sib_tail, first)


def grad_kernel(at_ref, p0_ref, p1_ref, p2_ref, p3_ref, mine_ref, far_ref, out_ref):
    y, x = at_ref[1], at_ref[3]
    total = None
    for o, (one, two) in ((0, (p0_ref, p1_ref)), (2, (p2_ref, p3_ref))):
        right = [
            jnp.concatenate([mine_ref[(y + o + i) & 3], far_ref[(y + o + i) & 3]], axis=1) for i in range(2)
        ]
        left = jnp.concatenate([one[...], two[...]], axis=1)
        term = jnp.dot(left, jnp.concatenate(right, axis=0), preferred_element_type=F32)
        total = term if total is None else total + term
    for j in range(4):
        for side in range(2):
            low = 512 * side + 128 * j
            out_ref[0, pl.ds((j - x) & 3, 1), 0, side] = total[None, :, low : low + 128].astype(BF)


def local_grad(at, blocks, mine, far):
    vm = pl.BlockSpec(memory_space=pltpu.VMEM)
    return pl.pallas_call(
        grad_kernel,
        grid_spec=pltpu.PrefetchScalarGridSpec(
            num_scalar_prefetch=1,
            grid=(4,),
            in_specs=[pl.BlockSpec((720, 128), lambda i, at: (i, 0))] * 4 + [vm, vm],
            out_specs=pl.BlockSpec(
                (1, 4, 1, 2, 720, 128), lambda i, at: ((i >> 1) ^ at[0], 0, (i & 1) ^ at[4], 0, 0, 0)
            ),
        ),
        out_shape=jax.ShapeDtypeStruct((2, 4, 2, 2, 720, 128), BF),
        compiler_params=pltpu.CompilerParams(vmem_limit_bytes=32 << 20),
        cost_estimate=pl.CostEstimate(flops=2 * 1024 * 512 * 2880, bytes_accessed=10_000_000, transcendentals=0),
        name="local_grad",
    )(at, *blocks, mine, far)


def spread_kernel(at_ref, own_ref, sib_ref, out_ref):
    core = at_ref[0]
    out_ref[pl.ds(core, 1)] = own_ref[...].astype(F32)
    out_ref[pl.ds(1 - core, 1)] = sib_ref[...].astype(F32)


def spread(at, own, sib):
    block = pl.BlockSpec((1, 1440, 128), lambda i, at: (i, 0, 0))
    return pl.pallas_call(
        spread_kernel,
        grid_spec=pltpu.PrefetchScalarGridSpec(
            num_scalar_prefetch=1,
            grid=(4,),
            in_specs=[block, block],
            out_specs=pl.BlockSpec((2, 1440, 128), lambda i, at: (0, 0, (at[3] + i) & 3)),
        ),
        out_shape=jax.ShapeDtypeStruct((2, 1440, 512), F32),
        compiler_params=pltpu.CompilerParams(vmem_limit_bytes=16 << 20),
        cost_estimate=pl.CostEstimate(flops=0, bytes_accessed=9_000_000, transcendentals=0),
        name="spread",
    )(at, own, sib)


def shift(axis, by, n):
    return functools.partial(lax.ppermute, axis_name=axis, perm=[(i, (i + by) % n) for i in range(n)])


def from_others(block, axis):
    return [shift(axis, -o, 4)(block) for o in (1, 2, 3)]


def after(value, *others):
    return lax.optimization_barrier((value,) + others)[0]


def toward(o, q):
    perm = [(i, (((i >> 1) + o) & 3) * 2 + ((i & 1) ^ q)) for i in range(8)]
    return functools.partial(lax.ppermute, axis_name=("x", "zh"), perm=perm)


OTHERS = [(o, q) for o in range(4) for q in range(2) if (o, q) != (0, 0)]


def local(tokens, expert_ids, gate_raw, overflow_shift, limits, gate_w, up_w, down_w, context, out_grad):
    at = jnp.stack([lax.axis_index(a) for a in ("core", "y", "zl", "x", "zh")]).astype(jnp.int32)
    zh, zl = lax.axis_index("zh"), lax.axis_index("zl")
    core_swap, zl_swap = shift("core", 1, 2), shift("zl", 1, 2)
    over = ("zl", "x", "zh", "y")
    weights = gate_w, up_w, down_w[0].T

    def exchange(rows):
        return lax.all_to_all(rows.reshape(64, -1, 2880), over, split_axis=0, concat_axis=0, tiled=True)

    lim = jnp.broadcast_to(limits.astype(F32)[:, None], (64, 128))
    mine = place_call(tokens.T, expert_ids.T, overflow_shift.T, gate_raw.T, lim)
    got0 = exchange(rows0(at, mine)).reshape(512, 2880)
    sibling = core_swap(mine)

    og = out_grad.T
    ogs = from_others(og, "y")
    ctx = context.reshape(4, 2, 128, 512)
    ctx_mine = lax.dynamic_index_in_dim(ctx, zl, 1, keepdims=False)
    ctx_far = zl_swap(lax.dynamic_index_in_dim(ctx, 1 - zl, 1, keepdims=False))
    send1 = after(rows1(at, mine, sibling), got0, ctx_far, *ogs)
    got1 = exchange(send1).reshape(1024, 2880)

    out0 = ffn(got0, *weights)
    grads = local_grad(at, [og] + ogs, ctx_mine, ctx_far)
    part = grads[0].astype(F32) + core_swap(grads[1]).astype(F32)
    terms = [toward(o, q)(part[o, q].astype(BF)) for o, q in OTHERS]
    back0 = exchange(after(out0, got1, part))
    out1 = ffn(got1, *weights)

    total = part[0, 0]
    for term in terms:
        total = total + term.astype(F32)
    final = (total[0] + zl_swap(total[1].astype(BF)).astype(F32)).astype(BF)
    back1 = exchange(after(out1, back0, final))
    first = combine0(at, back0.reshape(2, 256, 2880), mine[2880:])

    come = {(0, 0): final}
    for o, q in OTHERS:
        come[o, q] = toward(-o, q)(final)
    pieces = []
    for o in range(4):
        same, other = come[o, 0], come[o, 1]
        pieces.append(jnp.concatenate([jnp.where(zh == 0, same, other), jnp.where(zh == 0, other, same)]))
    full = jnp.stack(pieces)
    grad = spread(at, full, core_swap(full)).reshape(2880, 512)

    own, sib = combine1(at, back1.reshape(2, 512, 2880), mine[2880:], sibling[2880:], first)
    mixed = (own + core_swap(sib).astype(F32)).astype(BF)
    return mixed.T, grad.T


def solution(mesh):
    fine = Mesh(mesh.devices.reshape(4, 2, 2, 4, 2), ("x", "zh", "core", "y", "zl"))
    every = ("x", "zh", "core", "y", "zl")
    two, three = P(every, None), P(every, None, None)
    in_specs = (two, two, two, two, P(), three, three, three, P(("x", "zh", "core"), ("y", "zl")), two)
    out_specs = (two, P(("y", "zl"), None))
    return jax.shard_map(local, mesh=fine, in_specs=in_specs, out_specs=out_specs, check_vma=False)
```

time: 414 us -> 427 us (1.031)
  starting transfers between devices: 60.8 us -> 89.2 us
  waiting for transfers between devices: 269 us -> 249 us
    ppermute x9 -> x16, waiting for transfers between devices: 47.6 us -> 168 us  [the longest x7 76 us: local(): come[o, q] = toward(-o, q)(final)]
    all_to_all x3 -> x4, waiting for transfers between devices: 128 us -> 51.7 us  [exchange(): lax.all_to_all(rows.reshape(64, -1, 2880), over, split_axis=0, concat_axi...]
    ppermute x9 -> x3, waiting for transfers between devices: 89.3 us -> 23.8 us  [from_others(): return [shift(axis, -o, 4)(block) for o in (1, 2, 3)]]
    ppermute x9 -> x16, starting transfers between devices: 11.3 us -> 31.6 us  [the longest x7 16.3 us: local(): come[o, q] = toward(-o, q)(final)]
    all_to_all x3 -> x4, starting transfers between devices: 24.7 us -> 40.1 us  [exchange(): lax.all_to_all(rows.reshape(64, -1, 2880), over, split_axis=0, concat_axi...]
    ppermute x9 -> x3, starting transfers between devices: 12 us -> 4.77 us  [from_others(): return [shift(axis, -o, 4)(block) for o in (1, 2, 3)]]
    ppermute x1, starting transfers between devices: 5.43 us -> 0.09 us  [local(): mixed = (own + core_swap(sib).astype(F32)).astype(BF)]
    ppermute x1, starting transfers between devices: 4.59 us -> 9.33 us  [local(): grad = spread(at, full, core_swap(full)).reshape(2880, 512)]
  transfers between devices with their start and end apart: 25 -> 27, of which waited for: 12 -> 16; matrix products, arithmetic and copies ran while one was open for 2% -> 3% of each run, Pallas kernels for 15% -> 15%
where the time goes in v4:
time: 427 us; the launch traced here: 424 us
  waiting for transfers between devices  249 us (58%)
  starting transfers between devices  89.2 us (21%)
  Pallas kernels  66.4 us (16%)
  local copies, waits for them, and re-layouts  10.1 us (2%)
  other arithmetic  8.39 us (2%)
    ppermute x7, waiting for transfers between devices, local(): come[o, q] = toward(-o, q)(final)  76 us
    ppermute x7, waiting for transfers between devices, local(): terms = [toward(o, q)(part[o, q].astype(BF)) for o, q in OTHERS]  55.8 us
    all_to_all x4, waiting for transfers between devices, exchange(): lax.all_to_all(rows.reshape(64, -1, 2880), over, split_axis=0, concat_axi...  51.7 us
    all_to_all x4, starting transfers between devices, exchange(): lax.all_to_all(rows.reshape(64, -1, 2880), over, split_axis=0, concat_axi...  40.1 us
    pallas_call x2, Pallas kernels, ffn(): pl.pallas_call(ffn_kernel, grid=(count // 512,), in_specs=[pl.BlockSpec((...  40.1 us
    ppermute x1, waiting for transfers between devices, local(): ctx_far = zl_swap(lax.dynamic_index_in_dim(ctx, 1 - zl, 1, keepdims=False))  33.5 us
    ppermute x3, waiting for transfers between devices, from_others(): return [shift(axis, -o, 4)(block) for o in (1, 2, 3)]  23.8 us
    ppermute x7, starting transfers between devices, local(): come[o, q] = toward(-o, q)(final)  16.3 us
  transfers between devices with their start and end apart: 27, of which 16 were waited for; matrix products, arithmetic and copies ran while one was open for 3% of the time, Pallas kernels for 15%

profile of v4, /device:TPU:5, one launch (start us, length us, event | category | flops | bytes accessed | tf_op | source)
XLA Modules:
  0.0 423.9 jit_solution(10081963627587724436)
XLA Ops:
  7.7 11.2 %all-to-all-start = ((bf16[64,8,2880]{2,1,0:T(8,128)(2,1)}), bf16[64,8,2880]{2,1,0:T(8,128)(2,1)}, u32[]{:S(2)}, u32[]{:S(2)}) async-start(bf16[64,8,2880]{2,1,0:T(8,128)(2,1)} %bitcast.100), calls=%async_computation | async-start | bytes 6029312 | tf_op jit(solution)/shard_map/all_to_all | solution.py:349
  27.8 3.9 rows1.1
  31.7 33.5 %collective-permute-done.1.far_ref = bf16[4,128,512]{2,1,0:T(8,128)(2,1)S(1)} collective-permute-done((bf16[4,128,512]{2,1,0:T(8,128)(2,1)S(1)}, bf16[4,128,512]{2,1,0:T(8,128)(2,1)S(1)}, u32[]{:S(2)}, u32[]{:S(2)}) %collective-permute-start.1) | collective-permute-done | bytes 524320 | tf_op jit(solution)/shard_map/ppermute | solution.py:360
  65.2 7.0 %collective-permute-done.4.p3_ref = bf16[2880,128]{1,0:T(8,128)(2,1)} collective-permute-done((bf16[2880,128]{1,0:T(8,128)(2,1)S(1)}, bf16[2880,128]{1,0:T(8,128)(2,1)}, u32[]{:S(2)}, u32[]{:S(2)}) %collective-permute-start.4) | collective-permute-done | bytes 737312 | tf_op jit(solution)/shard_map/ppermute | solution.py:326
  72.3 15.9 %collective-permute-done.3.p2_ref = bf16[2880,128]{1,0:T(8,128)(2,1)} collective-permute-done((bf16[2880,128]{1,0:T(8,128)(2,1)S(1)}, bf16[2880,128]{1,0:T(8,128)(2,1)}, u32[]{:S(2)}, u32[]{:S(2)}) %collective-permute-start.3) | collective-permute-done | bytes 737312 | tf_op jit(solution)/shard_map/ppermute | solution.py:326
  89.0 10.3 %all-to-all-start.1 = ((bf16[64,16,2880]{2,1,0:T(8,128)(2,1)}), bf16[64,16,2880]{2,1,0:T(8,128)(2,1)}, u32[]{:S(2)}, u32[]{:S(2)}) async-start(bf16[64,16,2880]{2,1,0:T(8,128)(2,1)} %bitcast.99), calls=%async_computation.1 | async-start | bytes 12058624 | tf_op jit(solution)/shard_map/all_to_all | solution.py:349
  99.3 5.9 %local_grad.1 = bf16[2,4,2,2,720,128]{5,4,3,2,1,0:T(8,128)(2,1)S(1)} custom-call(s32[5]{0:T(128)S(1)} %stack.38.at_ref, bf16[2880,128]{1,0:T(8,128)(2,1)S(1)} %bitcast.98, bf16[2880,128]{1,0:T(8,128)(2,1)} %collective-permute-done.2.p1_ref, bf16[2880,128]{1,0:T(8,128)(2,1)} %collective-permute-done.3.p2_ref, ...), custom_call_target="tpu_custom_call" | custom-call | flops 3019898880 | bytes 10000000 | tf_op jit(solution)/shard_map/local_grad/pallas_call | solution.py:281
  107.5 5.0 %collective-permute-done.5 = bf16[4,2,2,720,128]{4,3,2,1,0:T(8,128)(2,1)S(1)} collective-permute-done((bf16[4,2,2,720,128]{4,3,2,1,0:T(8,128)(2,1)S(1)}, bf16[4,2,2,720,128]{4,3,2,1,0:T(8,128)(2,1)S(1)}, u32[]{:S(2)}, u32[]{:S(2)}) %collective-permute-start.5) | collective-permute-done | bytes 2949152 | tf_op jit(solution)/shard_map/ppermute | solution.py:366
  120.3 15.2 %ffn512.1 = bf16[512,2880]{1,0:T(8,128)(2,1)} custom-call(bf16[512,2880]{1,0:T(8,128)(2,1)} %bitcast.10.x_ref, bf16[1,2880,768]{2,1,0:T(8,128)(2,1)} %g_hbm.3, bf16[1,2880,768]{2,1,0:T(8,128)(2,1)} %u_hbm.3, bf16[2880,768]{1,0:T(8,128)(2,1)} %bitcast.105), custom_call_target="tpu_custom_call" | custom-call | flops 6794772480 | bytes 19198240 | tf_op jit(solution)/shard_map/ffn512/pallas_call | solution.py:184
  135.5 51.7 %all-to-all-done.1 = bf16[64,16,2880]{2,1,0:T(8,128)(2,1)} async-done(((bf16[64,16,2880]{2,1,0:T(8,128)(2,1)}), bf16[64,16,2880]{2,1,0:T(8,128)(2,1)}, u32[]{:S(2)}, u32[]{:S(2)}) %all-to-all-start.1) | async-done | bytes 5898272 | tf_op jit(solution)/shard_map/all_to_all | solution.py:349
  187.2 9.3 %all-to-all-start.2 = ((bf16[64,8,2880]{2,1,0:T(8,128)(2,1)}), bf16[64,8,2880]{2,1,0:T(8,128)(2,1)S(1)}, u32[]{:S(2)}, u32[]{:S(2)}) async-start(bf16[64,8,2880]{2,1,0:T(8,128)(2,1)} %bitcast.103), calls=%async_computation.2 | async-start | bytes 6029312 | tf_op jit(solution)/shard_map/all_to_all | solution.py:349
  196.9 4.9 %collective-permute-start.10 = (bf16[2,720,128]{2,1,0:T(8,128)(2,1)}, bf16[2,720,128]{2,1,0:T(8,128)(2,1)S(1)}, u32[]{:S(2)}, u32[]{:S(2)}) collective-permute-start(bf16[2,720,128]{2,1,0:T(8,128)(2,1)} %get-tuple-element.17), channel_id=1, source_target_pairs={{0,80},{16,64},{32,112},{48,96},{64,16},{80,0},{96,48},{112,32},{1... | collective-permute-start | bytes 1105928 | tf_op jit(solution)/shard_map/ppermute | solution.py:367
  205.6 32.5 %collective-permute-done.11 = bf16[2,720,128]{2,1,0:T(8,128)(2,1)S(1)} collective-permute-done((bf16[2,720,128]{2,1,0:T(8,128)(2,1)}, bf16[2,720,128]{2,1,0:T(8,128)(2,1)S(1)}, u32[]{:S(2)}, u32[]{:S(2)}) %collective-permute-start.11) | collective-permute-done | bytes 368672 | tf_op jit(solution)/shard_map/ppermute | solution.py:367
  238.1 3.7 collective-permute-done.10
  241.9 4.8 %collective-permute-done.9 = bf16[2,720,128]{2,1,0:T(8,128)(2,1)S(1)} collective-permute-done((bf16[2,720,128]{2,1,0:T(8,128)(2,1)}, bf16[2,720,128]{2,1,0:T(8,128)(2,1)S(1)}, u32[]{:S(2)}, u32[]{:S(2)}) %collective-permute-start.9) | collective-permute-done | bytes 368672 | tf_op jit(solution)/shard_map/ppermute | solution.py:367
  246.6 6.8 %collective-permute-done.8 = bf16[2,720,128]{2,1,0:T(8,128)(2,1)S(1)} collective-permute-done((bf16[2,720,128]{2,1,0:T(8,128)(2,1)}, bf16[2,720,128]{2,1,0:T(8,128)(2,1)S(1)}, u32[]{:S(2)}, u32[]{:S(2)}) %collective-permute-start.8) | collective-permute-done | bytes 368672 | tf_op jit(solution)/shard_map/ppermute | solution.py:367
  253.4 8.1 %collective-permute-done.7 = bf16[2,720,128]{2,1,0:T(8,128)(2,1)S(1)} collective-permute-done((bf16[2,720,128]{2,1,0:T(8,128)(2,1)S(1)}, bf16[2,720,128]{2,1,0:T(8,128)(2,1)S(1)}, u32[]{:S(2)}, u32[]{:S(2)}) %collective-permute-start.7) | collective-permute-done | bytes 368672 | tf_op jit(solution)/shard_map/ppermute | solution.py:367
  267.9 24.9 %ffn1024.1 = bf16[1024,2880]{1,0:T(8,128)(2,1)} custom-call(bf16[1024,2880]{1,0:T(8,128)(2,1)} %bitcast.15.x_ref, bf16[1,2880,768]{2,1,0:T(8,128)(2,1)} %g_hbm.3, bf16[1,2880,768]{2,1,0:T(8,128)(2,1)} %u_hbm.3, bf16[2880,768]{1,0:T(8,128)(2,1)} %bitcast.106), custom_call_target="tpu_custom_call" | custom-call | flops 13589544960 | bytes 25096480 | tf_op jit(solution)/shard_map/ffn1024/pallas_call | solution.py:184
  292.8 9.2 %all-to-all-start.3 = ((bf16[64,16,2880]{2,1,0:T(8,128)(2,1)}), bf16[64,16,2880]{2,1,0:T(8,128)(2,1)}, u32[]{:S(2)}, u32[]{:S(2)}) async-start(bf16[64,16,2880]{2,1,0:T(8,128)(2,1)} %bitcast.101), calls=%async_computation.3 | async-start | bytes 12058624 | tf_op jit(solution)/shard_map/all_to_all | solution.py:349
  311.7 64.2 %collective-permute-done.15 = bf16[720,128]{1,0:T(8,128)(2,1)S(1)} collective-permute-done((bf16[720,128]{1,0:T(8,128)(2,1)S(1)}, bf16[720,128]{1,0:T(8,128)(2,1)S(1)}, u32[]{:S(2)}, u32[]{:S(2)}) %collective-permute-start.15) | collective-permute-done | bytes 184352 | tf_op jit(solution)/shard_map/ppermute | solution.py:380
  386.6 7.9 %collective-permute-done.17 = bf16[720,128]{1,0:T(8,128)(2,1)S(1)} collective-permute-done((bf16[720,128]{1,0:T(8,128)(2,1)S(1)}, bf16[720,128]{1,0:T(8,128)(2,1)S(1)}, u32[]{:S(2)}, u32[]{:S(2)}) %collective-permute-start.17) | collective-permute-done | bytes 184352 | tf_op jit(solution)/shard_map/ppermute | solution.py:380
  396.1 9.3 %collective-permute-start.22 = (bf16[4,1440,128]{2,1,0:T(8,128)(2,1)}, bf16[4,1440,128]{2,1,0:T(8,128)(2,1)}, u32[]{:S(2)}, u32[]{:S(2)}) collective-permute-start(bf16[4,1440,128]{2,1,0:T(8,128)(2,1)} %pad_maximum_fusion.own_ref), channel_id=1, source_target_pairs={{0,8},{8,0},{1,9},{9,1},{2,10},{10,2},{3,11},{11,3},{4,12},{12,4},... | collective-permute-start | bytes 4423688 | tf_op jit(solution)/shard_map/ppermute | solution.py:386
  410.5 6.9 %combine1.1 = (f32[2880,128]{1,0:T(8,128)S(1)}, bf16[2880,128]{1,0:T(8,128)(2,1)S(1)}) custom-call(s32[5]{0:T(128)S(1)} %stack.38.at_ref, bf16[2,512,2880]{2,1,0:T(8,128)(2,1)} %bitcast.34.y_ref, bf16[16,128]{1,0:T(8,128)(2,1)S(1)} %slice.77.tail_ref.own_tail_ref, bf16[16,128]{1,0:T(8,128)(2,1)S(1)} %slice.78.sib_tail_ref, f32[128,2880]{1,0:T(8,128)S(1)} %copy-done.2), custom_call_target="tpu_custom_call" | custom-call | flops 1509949440 | bytes 9000000 | tf_op jit(solution)/shard_map/combine1/pallas_call | solution.py:244
  417.5 5.4 %spread.1 = f32[2,1440,512]{2,1,0:T(8,128)} custom-call(s32[5]{0:T(128)S(1)} %stack.38.at_ref, bf16[4,1440,128]{2,1,0:T(8,128)(2,1)} %pad_maximum_fusion.own_ref, bf16[4,1440,128]{2,1,0:T(8,128)(2,1)} %collective-permute-done.22.sib_ref), custom_call_target="tpu_custom_call" | custom-call | bytes 9000000 | tf_op jit(solution)/shard_map/spread/pallas_call | solution.py:306
  (77 shorter events, 65.4 us)
Async XLA Ops:
  7.7 81.4 %all-to-all-start = ((bf16[64,8,2880]{2,1,0:T(8,128)(2,1)}), bf16[64,8,2880]{2,1,0:T(8,128)(2,1)}, u32[]{:S(2)}, u32[]{:S(2)}) async-start(bf16[64,8,2880]{2,1,0:T(8,128)(2,1)} %bitcast.100), calls=%async_computation | async-start | bytes 6029312 | tf_op jit(solution)/shard_map/all_to_all | solution.py:349
  18.9 8.9 %collective-permute-start = (bf16[2896,128]{1,0:T(8,128)(2,1)S(1)}, bf16[2896,128]{1,0:T(8,128)(2,1)S(1)}, u32[]{:S(2)}, u32[]{:S(2)}) collective-permute-start(bf16[2896,128]{1,0:T(8,128)(2,1)S(1)} %place.1.own_ref), channel_id=1, source_target_pairs={{0,8},{8,0},{1,9},{9,1},{2,10},{10,2},{3,11},{11,3},{4,12},{12,4},... | collective-permute-start | bytes 2224136 | tf_op jit(solution)/shard_map/ppermute | solution.py:354
  20.2 52.0 %collective-permute-start.4 = (bf16[2880,128]{1,0:T(8,128)(2,1)S(1)}, bf16[2880,128]{1,0:T(8,128)(2,1)}, u32[]{:S(2)}, u32[]{:S(2)}) collective-permute-start(bf16[2880,128]{1,0:T(8,128)(2,1)S(1)} %bitcast.95), channel_id=1, source_target_pairs={{0,2},{2,4},{4,6},{6,0},{1,3},{3,5},{5,7},{7,1},{8,10},{10,12},{12... | collective-permute-start | bytes 2211848 | tf_op jit(solution)/shard_map/ppermute | solution.py:326
  21.4 66.7 %collective-permute-start.3 = (bf16[2880,128]{1,0:T(8,128)(2,1)S(1)}, bf16[2880,128]{1,0:T(8,128)(2,1)}, u32[]{:S(2)}, u32[]{:S(2)}) collective-permute-start(bf16[2880,128]{1,0:T(8,128)(2,1)S(1)} %bitcast.96), channel_id=1, source_target_pairs={{0,4},{2,6},{4,0},{6,2},{1,5},{3,7},{5,1},{7,3},{8,12},{10,14},{12... | collective-permute-start | bytes 2211848 | tf_op jit(solution)/shard_map/ppermute | solution.py:326
  23.8 65.2 %collective-permute-start.2 = (bf16[2880,128]{1,0:T(8,128)(2,1)S(1)}, bf16[2880,128]{1,0:T(8,128)(2,1)}, u32[]{:S(2)}, u32[]{:S(2)}) collective-permute-start(bf16[2880,128]{1,0:T(8,128)(2,1)S(1)} %bitcast.97), channel_id=1, source_target_pairs={{0,6},{2,0},{4,2},{6,4},{1,7},{3,1},{5,3},{7,5},{8,14},{10,8},{12,... | collective-permute-start | bytes 2211848 | tf_op jit(solution)/shard_map/ppermute | solution.py:326
  26.3 39.0 %collective-permute-start.1 = (bf16[4,128,512]{2,1,0:T(8,128)(2,1)S(1)}, bf16[4,128,512]{2,1,0:T(8,128)(2,1)S(1)}, u32[]{:S(2)}, u32[]{:S(2)}) collective-permute-start(bf16[4,128,512]{2,1,0:T(8,128)(2,1)S(1)} %get-tuple-element.22), channel_id=1, source_target_pairs={{0,1},{1,0},{2,3},{3,2},{4,5},{5,4},{6,7},{7,6},{8,9},{9,8},{10,11... | collective-permute-start | bytes 1572872 | tf_op jit(solution)/shard_map/ppermute | solution.py:360
  89.0 98.2 %all-to-all-start.1 = ((bf16[64,16,2880]{2,1,0:T(8,128)(2,1)}), bf16[64,16,2880]{2,1,0:T(8,128)(2,1)}, u32[]{:S(2)}, u32[]{:S(2)}) async-start(bf16[64,16,2880]{2,1,0:T(8,128)(2,1)} %bitcast.99), calls=%async_computation.1 | async-start | bytes 12058624 | tf_op jit(solution)/shard_map/all_to_all | solution.py:349
  117.4 84.9 %collective-permute-start.6 = (bf16[2,720,128]{2,1,0:T(8,128)(2,1)}, bf16[2,720,128]{2,1,0:T(8,128)(2,1)}, u32[]{:S(2)}, u32[]{:S(2)}) collective-permute-start(bf16[2,720,128]{2,1,0:T(8,128)(2,1)} %get-tuple-element.14), channel_id=1, source_target_pairs={{0,16},{16,0},{32,48},{48,32},{64,80},{80,64},{96,112},{112,96},{1... | collective-permute-start | bytes 1105928 | tf_op jit(solution)/shard_map/ppermute | solution.py:367
  120.0 83.4 %collective-permute-start.12 = (bf16[2,720,128]{2,1,0:T(8,128)(2,1)}, bf16[2,720,128]{2,1,0:T(8,128)(2,1)}, u32[]{:S(2)}, u32[]{:S(2)}) collective-permute-start(bf16[2,720,128]{2,1,0:T(8,128)(2,1)} %get-tuple-element.15), channel_id=1, source_target_pairs={{0,112},{16,96},{32,16},{48,0},{64,48},{80,32},{96,80},{112,64},{1... | collective-permute-start | bytes 1105928 | tf_op jit(solution)/shard_map/ppermute | solution.py:367
  187.2 105.6 %all-to-all-start.2 = ((bf16[64,8,2880]{2,1,0:T(8,128)(2,1)}), bf16[64,8,2880]{2,1,0:T(8,128)(2,1)S(1)}, u32[]{:S(2)}, u32[]{:S(2)}) async-start(bf16[64,8,2880]{2,1,0:T(8,128)(2,1)} %bitcast.103), calls=%async_computation.2 | async-start | bytes 6029312 | tf_op jit(solution)/shard_map/all_to_all | solution.py:349
  196.6 41.6 %collective-permute-start.11 = (bf16[2,720,128]{2,1,0:T(8,128)(2,1)}, bf16[2,720,128]{2,1,0:T(8,128)(2,1)S(1)}, u32[]{:S(2)}, u32[]{:S(2)}) collective-permute-start(bf16[2,720,128]{2,1,0:T(8,128)(2,1)} %get-tuple-element.16), channel_id=1, source_target_pairs={{0,96},{16,112},{32,0},{48,16},{64,32},{80,48},{96,64},{112,80},{1... | collective-permute-start | bytes 1105928 | tf_op jit(solution)/shard_map/ppermute | solution.py:367
  196.9 44.9 %collective-permute-start.10 = (bf16[2,720,128]{2,1,0:T(8,128)(2,1)}, bf16[2,720,128]{2,1,0:T(8,128)(2,1)S(1)}, u32[]{:S(2)}, u32[]{:S(2)}) collective-permute-start(bf16[2,720,128]{2,1,0:T(8,128)(2,1)} %get-tuple-element.17), channel_id=1, source_target_pairs={{0,80},{16,64},{32,112},{48,96},{64,16},{80,0},{96,48},{112,32},{1... | collective-permute-start | bytes 1105928 | tf_op jit(solution)/shard_map/ppermute | solution.py:367
  201.8 44.8 %collective-permute-start.9 = (bf16[2,720,128]{2,1,0:T(8,128)(2,1)}, bf16[2,720,128]{2,1,0:T(8,128)(2,1)S(1)}, u32[]{:S(2)}, u32[]{:S(2)}) collective-permute-start(bf16[2,720,128]{2,1,0:T(8,128)(2,1)} %get-tuple-element.18), channel_id=1, source_target_pairs={{0,64},{16,80},{32,96},{48,112},{64,0},{80,16},{96,32},{112,48},{1... | collective-permute-start | bytes 1105928 | tf_op jit(solution)/shard_map/ppermute | solution.py:367
  202.3 51.1 %collective-permute-start.8 = (bf16[2,720,128]{2,1,0:T(8,128)(2,1)}, bf16[2,720,128]{2,1,0:T(8,128)(2,1)S(1)}, u32[]{:S(2)}, u32[]{:S(2)}) collective-permute-start(bf16[2,720,128]{2,1,0:T(8,128)(2,1)} %get-tuple-element.19), channel_id=1, source_target_pairs={{0,48},{16,32},{32,80},{48,64},{64,112},{80,96},{96,16},{112,0},{1... | collective-permute-start | bytes 1105928 | tf_op jit(solution)/shard_map/ppermute | solution.py:367
  203.5 58.0 %collective-permute-start.7 = (bf16[2,720,128]{2,1,0:T(8,128)(2,1)S(1)}, bf16[2,720,128]{2,1,0:T(8,128)(2,1)S(1)}, u32[]{:S(2)}, u32[]{:S(2)}) collective-permute-start(bf16[2,720,128]{2,1,0:T(8,128)(2,1)S(1)} %get-tuple-element.20), channel_id=1, source_target_pairs={{0,32},{16,48},{32,64},{48,80},{64,96},{80,112},{96,0},{112,16},{1... | collective-permute-start | bytes 1105928 | tf_op jit(solution)/shard_map/ppermute | solution.py:367
  292.8 116.3 %all-to-all-start.3 = ((bf16[64,16,2880]{2,1,0:T(8,128)(2,1)}), bf16[64,16,2880]{2,1,0:T(8,128)(2,1)}, u32[]{:S(2)}, u32[]{:S(2)}) async-start(bf16[64,16,2880]{2,1,0:T(8,128)(2,1)} %bitcast.101), calls=%async_computation.3 | async-start | bytes 12058624 | tf_op jit(solution)/shard_map/all_to_all | solution.py:349
  302.1 73.8 %collective-permute-start.15 = (bf16[720,128]{1,0:T(8,128)(2,1)S(1)}, bf16[720,128]{1,0:T(8,128)(2,1)S(1)}, u32[]{:S(2)}, u32[]{:S(2)}) collective-permute-start(bf16[720,128]{1,0:T(8,128)(2,1)S(1)} %fusion.9), channel_id=1, source_target_pairs={{0,16},{16,0},{32,48},{48,32},{64,80},{80,64},{96,112},{112,96},{1... | collective-permute-start | bytes 552968 | tf_op jit(solution)/shard_map/ppermute | solution.py:380
  304.9 89.7 %collective-permute-start.20 = (bf16[720,128]{1,0:T(8,128)(2,1)S(1)}, bf16[720,128]{1,0:T(8,128)(2,1)S(1)}, u32[]{:S(2)}, u32[]{:S(2)}) collective-permute-start(bf16[720,128]{1,0:T(8,128)(2,1)S(1)} %fusion.9), channel_id=1, source_target_pairs={{0,32},{16,48},{32,64},{48,80},{64,96},{80,112},{96,0},{112,16},{1... | collective-permute-start | bytes 552968 | tf_op jit(solution)/shard_map/ppermute | solution.py:380
  305.8 76.8 %collective-permute-start.19 = (bf16[720,128]{1,0:T(8,128)(2,1)S(1)}, bf16[720,128]{1,0:T(8,128)(2,1)S(1)}, u32[]{:S(2)}, u32[]{:S(2)}) collective-permute-start(bf16[720,128]{1,0:T(8,128)(2,1)S(1)} %fusion.9), channel_id=1, source_target_pairs={{0,80},{16,64},{32,112},{48,96},{64,16},{80,0},{96,48},{112,32},{1... | collective-permute-start | bytes 552968 | tf_op jit(solution)/shard_map/ppermute | solution.py:380
  306.3 80.3 %collective-permute-start.18 = (bf16[720,128]{1,0:T(8,128)(2,1)S(1)}, bf16[720,128]{1,0:T(8,128)(2,1)S(1)}, u32[]{:S(2)}, u32[]{:S(2)}) collective-permute-start(bf16[720,128]{1,0:T(8,128)(2,1)S(1)} %fusion.9), channel_id=1, source_target_pairs={{0,64},{16,80},{32,96},{48,112},{64,0},{80,16},{96,32},{112,48},{1... | collective-permute-start | bytes 552968 | tf_op jit(solution)/shard_map/ppermute | solution.py:380
  308.7 85.8 %collective-permute-start.17 = (bf16[720,128]{1,0:T(8,128)(2,1)S(1)}, bf16[720,128]{1,0:T(8,128)(2,1)S(1)}, u32[]{:S(2)}, u32[]{:S(2)}) collective-permute-start(bf16[720,128]{1,0:T(8,128)(2,1)S(1)} %fusion.9), channel_id=1, source_target_pairs={{0,112},{16,96},{32,16},{48,0},{64,48},{80,32},{96,80},{112,64},{1... | collective-permute-start | bytes 552968 | tf_op jit(solution)/shard_map/ppermute | solution.py:380
  375.9 18.7 %collective-permute-start.16 = (bf16[720,128]{1,0:T(8,128)(2,1)S(1)}, bf16[720,128]{1,0:T(8,128)(2,1)S(1)}, u32[]{:S(2)}, u32[]{:S(2)}) collective-permute-start(bf16[720,128]{1,0:T(8,128)(2,1)S(1)} %fusion.9), channel_id=1, source_target_pairs={{0,96},{16,112},{32,0},{48,16},{64,32},{80,48},{96,64},{112,80},{1... | collective-permute-start | bytes 552968 | tf_op jit(solution)/shard_map/ppermute | solution.py:380
  382.6 12.0 %collective-permute-start.21 = (bf16[720,128]{1,0:T(8,128)(2,1)S(1)}, bf16[720,128]{1,0:T(8,128)(2,1)S(1)}, u32[]{:S(2)}, u32[]{:S(2)}) collective-permute-start(bf16[720,128]{1,0:T(8,128)(2,1)S(1)} %fusion.9), channel_id=1, source_target_pairs={{0,48},{16,32},{32,80},{48,64},{64,112},{80,96},{96,16},{112,0},{1... | collective-permute-start | bytes 552968 | tf_op jit(solution)/shard_map/ppermute | solution.py:380
  396.1 21.4 %collective-permute-start.22 = (bf16[4,1440,128]{2,1,0:T(8,128)(2,1)}, bf16[4,1440,128]{2,1,0:T(8,128)(2,1)}, u32[]{:S(2)}, u32[]{:S(2)}) collective-permute-start(bf16[4,1440,128]{2,1,0:T(8,128)(2,1)} %pad_maximum_fusion.own_ref), channel_id=1, source_target_pairs={{0,8},{8,0},{1,9},{9,1},{2,10},{10,2},{3,11},{11,3},{4,12},{12,4},... | collective-permute-start | bytes 4423688 | tf_op jit(solution)/shard_map/ppermute | solution.py:386
  (12 other events, 62.2 us)

commit v5 on v4

v5 whole, which is shorter than its diff:
```python
import functools

import jax
import jax.numpy as jnp
from jax import lax
from jax.experimental import pallas as pl
from jax.experimental.pallas import tpu as pltpu
from jax.sharding import Mesh, PartitionSpec as P

CAP = 12
BF = jnp.bfloat16
F32 = jnp.float32
NT = (((1,), (1,)), ((), ()))


def place(ids, shifts, lim):
    label = lax.broadcasted_iota(jnp.int32, (64, 128), 0)
    earlier = (
        lax.broadcasted_iota(jnp.int32, (128, 128), 0)
        < lax.broadcasted_iota(jnp.int32, (128, 128), 1)
    ).astype(F32).astype(BF)
    rows = [ids[k : k + 1, :] for k in range(4)]
    hots = [(r == label).astype(F32) for r in rows]
    hot = hots[0] + hots[1] + hots[2] + hots[3]
    before = jnp.dot(hot.astype(BF), earlier, preferred_element_type=F32)
    spilled, seconds, second_hots, first_ranks = [], [], [], []
    for k in range(4):
        rank = jnp.sum(before * hots[k], axis=0, keepdims=True)
        limit = jnp.sum(lim * hots[k], axis=0, keepdims=True)
        spill = rank >= limit
        second = (rows[k] + shifts[k : k + 1, :]) & 63
        first_ranks.append(rank)
        spilled.append(spill)
        seconds.append(second)
        second_hots.append((second == label).astype(F32))
    spill_hots = [h * s.astype(F32) for h, s in zip(second_hots, spilled)]
    total = spill_hots[0] + spill_hots[1] + spill_hots[2] + spill_hots[3]
    run = jnp.dot(total.astype(BF), earlier, preferred_element_type=F32)
    out = []
    for k in range(4):
        rank = jnp.sum(run * second_hots[k], axis=0, keepdims=True)
        run = run + spill_hots[k]
        limit = jnp.sum(lim * second_hots[k], axis=0, keepdims=True)
        slot = jnp.where(spilled[k], limit + rank, first_ranks[k]).astype(jnp.int32)
        target = jnp.where(spilled[k], seconds[k], rows[k])
        out.append((target, slot, slot < CAP))
    return out


def place_kernel(tok_ref, ids_ref, shift_ref, raw_ref, lim_ref, out_ref):
    out_ref[:2880, :] = tok_ref[...]
    places = place(ids_ref[...], shift_ref[...], lim_ref[...])
    raw = raw_ref[...]
    share = raw / jnp.sum(raw, axis=0, keepdims=True)
    rows = [t.astype(F32) for t, _, _ in places]
    rows += [jnp.where(k, s, -1).astype(F32) for _, s, k in places]
    rows += [share, jnp.zeros((4, 128), F32)]
    out_ref[2880:, :] = jnp.concatenate(rows, axis=0).astype(BF)


def place_call(tok, ids, shifts, raw, lim):
    vm = pl.BlockSpec(memory_space=pltpu.VMEM)
    return pl.pallas_call(
        place_kernel,
        in_specs=[vm] * 5,
        out_specs=vm,
        out_shape=jax.ShapeDtypeStruct((2896, 128), BF),
        compiler_params=pltpu.CompilerParams(vmem_limit_bytes=16 << 20),
        cost_estimate=pl.CostEstimate(flops=1 << 22, bytes_accessed=1_500_000, transcendentals=0),
        name="place",
    )(tok, ids, shifts, raw, lim)


def slots_of(tail, core):
    tail = tail.astype(F32)
    out = []
    for k in range(4):
        target = tail[k : k + 1].astype(jnp.int32)
        slot = tail[4 + k : 5 + k].astype(jnp.int32)
        mine = (slot >= 0) & (((target >> 2) & 1) == core)
        out.append((mine, (target >> 3) * 4 + (target & 3), slot, tail[8 + k : 9 + k]))
    return out


def row_weights(tail, core, side, weighted):
    at = lax.broadcasted_iota(jnp.int32, (768, 128), 0)
    total = jnp.zeros((768, 128), F32)
    for mine, index, slot, share in slots_of(tail, core):
        row = jnp.where(mine, index * 24 + side * CAP + slot, -1)
        total = total + jnp.where(row == at, share if weighted else 1.0, 0.0)
    return total


def rows_kernel(at_ref, own_ref, sib_ref, out_ref, hot_ref):
    step = pl.program_id(0)

    @pl.when(step == 0)
    def _():
        for side, ref in enumerate((own_ref, sib_ref)):
            hot_ref[:, 128 * side : 128 * side + 128] = row_weights(ref[2880:, :], at_ref[0], side, False).astype(BF)

    both = jnp.concatenate([own_ref[:2880, :], sib_ref[:2880, :]], axis=1)
    hot = hot_ref[pl.ds(pl.multiple_of(step * 256, 256), 256), :]
    got = lax.dot_general(hot, both, NT, preferred_element_type=F32).astype(BF)
    out_ref[0] = got
    out_ref[1] = got


def rows_of(at, own, sib):
    vm = pl.BlockSpec(memory_space=pltpu.VMEM)
    return pl.pallas_call(
        rows_kernel,
        grid=(3,),
        in_specs=[pl.BlockSpec(memory_space=pltpu.SMEM), vm, vm],
        out_specs=pl.BlockSpec((2, 256, 2880), lambda i: (0, i, 0)),
        out_shape=pltpu.HBM((2, 768, 2880), BF),
        scratch_shapes=[pltpu.VMEM((768, 256), BF)],
        compiler_params=pltpu.CompilerParams(vmem_limit_bytes=32 << 20),
        cost_estimate=pl.CostEstimate(flops=2 * 768 * 256 * 2880, bytes_accessed=10_000_000, transcendentals=0),
        name="rows",
    )(at, own, sib)


def ffn_kernel(x_ref, g_hbm, u_hbm, d_hbm, out_ref, g_ref, u_ref, d_ref, sems):
    step = pl.program_id(0)
    copies = [
        pltpu.make_async_copy(g_hbm.at[0], g_ref, sems.at[0]),
        pltpu.make_async_copy(u_hbm.at[0], u_ref, sems.at[1]),
        pltpu.make_async_copy(d_hbm, d_ref, sems.at[2]),
    ]

    @pl.when(step == 0)
    def _():
        for c in copies:
            c.start()
        copies[0].wait()

    x = x_ref[...]
    gating = jnp.dot(x, g_ref[...], preferred_element_type=F32)

    @pl.when(step == 0)
    def _():
        copies[1].wait()

    upward = jnp.dot(x, u_ref[...], preferred_element_type=F32)
    active = ((upward + 1.0) * gating * jax.nn.sigmoid(1.702 * gating)).astype(BF)

    @pl.when(step == 0)
    def _():
        copies[2].wait()

    out_ref[...] = lax.dot_general(active, d_ref[...], NT, preferred_element_type=F32).astype(BF)


def ffn(x, g, u, d_t):
    count = x.shape[0]
    hbm = pl.BlockSpec(memory_space=pltpu.HBM)
    held = pltpu.VMEM((2880, 768), BF)
    return pl.pallas_call(
        ffn_kernel,
        grid=(count // 512,),
        in_specs=[pl.BlockSpec((512, 2880), lambda i: (i, 0)), hbm, hbm, hbm],
        out_specs=pl.BlockSpec((512, 2880), lambda i: (i, 0)),
        out_shape=pltpu.HBM((count, 2880), BF),
        scratch_shapes=[held, held, held, pltpu.SemaphoreType.DMA((3,))],
        compiler_params=pltpu.CompilerParams(vmem_limit_bytes=58 << 20),
        cost_estimate=pl.CostEstimate(
            flops=6 * count * 2880 * 768, bytes_accessed=13_300_000 + count * 2880 * 4, transcendentals=count * 768
        ),
        name="ffn%d" % count,
    )(x, g, u, d_t)


def combine_kernel(at_ref, y_ref, own_tail_ref, sib_tail_ref, own_ref, sib_ref, w_ref, acc_ref):
    step = pl.program_id(0)

    @pl.when(step == 0)
    def _():
        for side, ref in enumerate((own_tail_ref, sib_tail_ref)):
            w = row_weights(ref[...], at_ref[0], side, True).T.astype(BF)
            for b in range(6):
                w_ref[b, 128 * side : 128 * side + 128, :] = w[:, 128 * b : 128 * b + 128]
        acc_ref[...] = jnp.zeros_like(acc_ref)

    w = w_ref[step]
    acc_ref[...] += jnp.dot(w, y_ref[0], preferred_element_type=F32) + jnp.dot(
        w, y_ref[1], preferred_element_type=F32
    )

    @pl.when(step == 5)
    def _():
        own_ref[...] = acc_ref[:128, :].T
        sib_ref[...] = acc_ref[128:, :].T.astype(BF)


def combine(at, y, own_tail, sib_tail):
    vm = pl.BlockSpec(memory_space=pltpu.VMEM)
    return pl.pallas_call(
        combine_kernel,
        grid=(6,),
        in_specs=[
            pl.BlockSpec(memory_space=pltpu.SMEM),
            pl.BlockSpec((2, 128, 2880), lambda i: (0, i, 0)),
            vm,
            vm,
        ],
        out_specs=[pl.BlockSpec((2880, 128), lambda i: (0, 0))] * 2,
        out_shape=[jax.ShapeDtypeStruct((2880, 128), F32), jax.ShapeDtypeStruct((2880, 128), BF)],
        scratch_shapes=[pltpu.VMEM((6, 256, 128), BF), pltpu.VMEM((256, 2880), F32)],
        compiler_params=pltpu.CompilerParams(vmem_limit_bytes=48 << 20),
        cost_estimate=pl.CostEstimate(flops=4 * 768 * 256 * 2880, bytes_accessed=12_000_000, transcendentals=0),
        name="combine",
    )(at, y, own_tail, sib_tail)


def grad_kernel(at_ref, og_ref, mine_ref, far_ref, out_ref):
    zl = at_ref[2]
    total = None
    for o in (0, 2):
        right = [jnp.concatenate([mine_ref[o + i], far_ref[o + i]], axis=1) for i in range(2)]
        left = jnp.concatenate([og_ref[o], og_ref[o + 1]], axis=1)
        term = jnp.dot(left, jnp.concatenate(right, axis=0), preferred_element_type=F32)
        total = term if total is None else total + term
    for j in range(4):
        for side in range(2):
            low = 512 * side + 128 * j
            out_ref[0, j, 0, pl.ds(side ^ zl, 1)] = total[None, :, low : low + 128].astype(BF)


def local_grad(at, og, mine, far):
    vm = pl.BlockSpec(memory_space=pltpu.VMEM)
    return pl.pallas_call(
        grad_kernel,
        grid_spec=pltpu.PrefetchScalarGridSpec(
            num_scalar_prefetch=1,
            grid=(4,),
            in_specs=[pl.BlockSpec((4, 720, 128), lambda i, at: (0, i, 0)), vm, vm],
            out_specs=pl.BlockSpec((1, 4, 1, 2, 720, 128), lambda i, at: ((i >> 1) ^ at[0], 0, i & 1, 0, 0, 0)),
        ),
        out_shape=jax.ShapeDtypeStruct((2, 4, 2, 2, 720, 128), BF),
        compiler_params=pltpu.CompilerParams(vmem_limit_bytes=32 << 20),
        cost_estimate=pl.CostEstimate(flops=2 * 1024 * 512 * 2880, bytes_accessed=10_000_000, transcendentals=0),
        name="local_grad",
    )(at, og, mine, far)


def spread_kernel(at_ref, own_ref, sib_ref, out_ref):
    core = at_ref[0]
    out_ref[pl.ds(core, 1)] = own_ref[...].astype(F32)
    out_ref[pl.ds(1 - core, 1)] = sib_ref[...].astype(F32)


def spread(at, own, sib):
    block = pl.BlockSpec((1, 1440, 128), lambda i, at: (i, 0, 0))
    return pl.pallas_call(
        spread_kernel,
        grid_spec=pltpu.PrefetchScalarGridSpec(
            num_scalar_prefetch=1,
            grid=(4,),
            in_specs=[block, block],
            out_specs=pl.BlockSpec((2, 1440, 128), lambda i, at: (0, 0, i)),
        ),
        out_shape=jax.ShapeDtypeStruct((2, 1440, 512), F32),
        compiler_params=pltpu.CompilerParams(vmem_limit_bytes=16 << 20),
        cost_estimate=pl.CostEstimate(flops=0, bytes_accessed=9_000_000, transcendentals=0),
        name="spread",
    )(at, own, sib)


def shift(axis, by, n):
    return functools.partial(lax.ppermute, axis_name=axis, perm=[(i, (i + by) % n) for i in range(n)])


def after(value, *others):
    return lax.optimization_barrier((value,) + others)[0]


def local(tokens, expert_ids, gate_raw, overflow_shift, limits, gate_w, up_w, down_w, context, out_grad):
    at = jnp.stack([lax.axis_index(a) for a in ("core", "y", "zl", "x", "zh")]).astype(jnp.int32)
    zl = lax.axis_index("zl")
    core_swap, zl_swap = shift("core", 1, 2), shift("zl", 1, 2)
    over = ("zl", "x", "zh", "y")

    def exchange(rows):
        return lax.all_to_all(rows.reshape(64, 24, 2880), over, split_axis=0, concat_axis=0, tiled=True)

    og = lax.all_gather(out_grad.T, "y", axis=0)
    ctx = context.reshape(4, 2, 128, 512)
    ctx_mine = lax.dynamic_index_in_dim(ctx, zl, 1, keepdims=False)
    ctx_far = zl_swap(lax.dynamic_index_in_dim(ctx, 1 - zl, 1, keepdims=False))

    lim = jnp.broadcast_to(limits.astype(F32)[:, None], (64, 128))
    mine = place_call(tokens.T, expert_ids.T, overflow_shift.T, gate_raw.T, lim)
    sibling = core_swap(mine)
    got = exchange(after(rows_of(at, mine, sibling), ctx_far)).reshape(1536, 2880)

    grads = local_grad(at, og, ctx_mine, ctx_far)
    part = (grads[0].astype(F32) + core_swap(grads[1]).astype(F32)).astype(BF)
    own_part = lax.psum_scatter(
        part.reshape(16 * 720, 128), ("x", "zh", "zl"), scatter_dimension=0, tiled=True
    )
    out = ffn(after(got, part), gate_w, up_w, down_w[0].T)
    back = exchange(out)
    full = lax.all_gather(after(own_part, out), ("x", "zh"), axis=0, tiled=True).reshape(4, 1440, 128)
    grad = spread(at, full, core_swap(full)).reshape(2880, 512)

    own, sib = combine(at, back.reshape(2, 768, 2880), mine[2880:], sibling[2880:])
    mixed = (own + core_swap(sib).astype(F32)).astype(BF)
    return mixed.T, grad.T


def solution(mesh):
    fine = Mesh(mesh.devices.reshape(4, 2, 2, 4, 2), ("x", "zh", "core", "y", "zl"))
    every = ("x", "zh", "core", "y", "zl")
    two, three = P(every, None), P(every, None, None)
    in_specs = (two, two, two, two, P(), three, three, three, P(("x", "zh", "core"), ("y", "zl")), two)
    out_specs = (two, P(("y", "zl"), None))
    return jax.shard_map(local, mesh=fine, in_specs=in_specs, out_specs=out_specs, check_vma=False)
```

time: 427 us -> 484 us (1.13)
  waiting for transfers between devices: 249 us -> 359 us
  starting transfers between devices: 89.2 us -> 39.4 us
  between operations: 0.86 us -> 13.8 us
  Pallas kernels: 66.4 us -> 58.5 us
    all_gather x0 -> x2, waiting for transfers between devices: none -> 206 us  [the longest x1 138 us: local(): og = lax.all_gather(out_grad.T, 'y', axis=0)]
    ppermute x19 -> x1, waiting for transfers between devices: 164 us -> 5 us  [local(): part = (grads[0].astype(F32) + core_swap(grads[1]).astype(F32)).astype(BF)]
    optimization_barrier x0 -> x1, waiting for transfers between devices: none -> 140 us  [after(): return lax.optimization_barrier((value,) + others)[0]]
    all_to_all x4 -> x2, waiting for transfers between devices: 51.7 us -> 0.01 us  [exchange(): lax.all_to_all(rows.reshape(64, 24, 2880), over, split_axis=0, concat_axi...]
    ppermute x19 -> x1, starting transfers between devices: 36.9 us -> 0.52 us  [local(): part = (grads[0].astype(F32) + core_swap(grads[1]).astype(F32)).astype(BF)]
    ppermute x1, waiting for transfers between devices: 33.5 us -> 6.59 us  [local(): ctx_far = zl_swap(lax.dynamic_index_in_dim(ctx, 1 - zl, 1, keepdims=False))]
    ppermute x1, starting transfers between devices: 9.33 us -> 2.19 us  [local(): grad = spread(at, full, core_swap(full)).reshape(2880, 512)]
    all_to_all x4 -> x2, starting transfers between devices: 40.1 us -> 34.1 us  [exchange(): lax.all_to_all(rows.reshape(64, 24, 2880), over, split_axis=0, concat_axi...]
  transfers between devices with their start and end apart: 27 -> 10, of which waited for: 16 -> 5; matrix products, arithmetic and copies ran while one was open for 3% -> 1% of each run, Pallas kernels for 15% -> 12%
where the time goes in v5:
time: 484 us; the launch traced here: 481 us
  waiting for transfers between devices  359 us (74%)
  Pallas kernels  58.5 us (12%)
  starting transfers between devices  39.4 us (8%)
  between operations  13.8 us (3%)
  local copies, waits for them, and re-layouts  6.65 us (1%)
    optimization_barrier x1, waiting for transfers between devices, after(): return lax.optimization_barrier((value,) + others)[0]  140 us
    all_gather x1, waiting for transfers between devices, local(): og = lax.all_gather(out_grad.T, 'y', axis=0)  138 us
    all_gather x1, waiting for transfers between devices, local(): lax.all_gather(after(own_part, out), ('x', 'zh'), axis=0, tiled=True)  68.2 us
    pallas_call x1, Pallas kernels, ffn(): pl.pallas_call(ffn_kernel, grid=(count // 512,), in_specs=[pl.BlockSpec((...  34.3 us
    all_to_all x2, starting transfers between devices, exchange(): lax.all_to_all(rows.reshape(64, 24, 2880), over, split_axis=0, concat_axi...  34.1 us
  transfers between devices with their start and end apart: 10, of which 5 were waited for; matrix products, arithmetic and copies ran while one was open for 1% of the time, Pallas kernels for 12%

profile of v5, /device:TPU:5, one launch (start us, length us, event | category | flops | bytes accessed | tf_op | source)
XLA Modules:
  0.0 481.1 jit_solution(10692170316456868113)
XLA Ops:
  7.9 1.1 copy-done.1
  9.0 0.7 copy-done.2
  9.7 0.7 copy-done.3
  10.4 0.7 copy-done.4
  11.4 0.8 collective-permute-start
  12.1 1.3 dynamic-slice_bitcast_fusion
  13.4 1.7 collective-permute-start.1
  15.2 5.5 %rows.1 = bf16[2,768,2880]{2,1,0:T(8,128)(2,1)} custom-call(s32[5]{0:T(128)S(1)} %stack.23.at_ref, bf16[2896,128]{1,0:T(8,128)(2,1)S(1)} %place.1.own_ref, bf16[2896,128]{1,0:T(8,128)(2,1)S(1)} %collective-permute-done.sib_ref), custom_call_target="tpu_custom_call" | custom-call | flops 1132462080 | bytes 10000000 | tf_op jit(solution)/shard_map/rows/pallas_call | solution.py:111
  20.7 6.6 %collective-permute-done.1.far_ref = bf16[4,128,512]{2,1,0:T(8,128)(2,1)S(1)} collective-permute-done((bf16[4,128,512]{2,1,0:T(8,128)(2,1)S(1)}, bf16[4,128,512]{2,1,0:T(8,128)(2,1)S(1)}, u32[]{:S(2)}, u32[]{:S(2)}) %collective-permute-start.1) | collective-permute-done | bytes 524320 | tf_op jit(solution)/shard_map/ppermute | solution.py:290
  27.3 10.8 %all-to-all-start = ((bf16[64,24,2880]{2,1,0:T(8,128)(2,1)}), bf16[64,24,2880]{2,1,0:T(8,128)(2,1)}, u32[]{:S(2)}, u32[]{:S(2)}) async-start(bf16[64,24,2880]{2,1,0:T(8,128)(2,1)} %bitcast.49), calls=%async_computation | async-start | bytes 18087936 | tf_op jit(solution)/shard_map/all_to_all | solution.py:285
  38.2 0.7 all-gather.6.cloned.1.call-update
  38.9 137.7 %all-gather.6.cloned.1.call-done = bf16[11520,128]{1,0:T(8,128)(2,1)} async-done(((bf16[2880,128]{1,0:T(8,128)(2,1)}), bf16[11520,128]{1,0:T(8,128)(2,1)}) %all-gather.6.cloned.1.call-update) | async-done | bytes 2949136 | tf_op jit(solution)/shard_map/all_gather | solution.py:287
  176.6 1.8 copy-done.5
  178.4 5.4 %local_grad.1 = bf16[2,4,2,2,720,128]{5,4,3,2,1,0:T(8,128)(2,1)S(1)} custom-call(s32[5]{0:T(128)S(1)} %stack.23.at_ref, bf16[4,2880,128]{2,1,0:T(8,128)(2,1)S(1)} %bitcast.48, bf16[4,128,512]{2,1,0:T(8,128)(2,1)S(1)} %get-tuple-element.12.mine_ref, bf16[4,128,512]{2,1,0:T(8,128)(2,1)S(1)} %collective-permute-done.1.far_ref), custom_call_target="tpu_custom_call" | custom-call | flops 3019898880 | bytes 10000000 | tf_op jit(solution)/shard_map/local_grad/pallas_call | solution.py:232
  184.5 5.0 %collective-permute-done.2 = bf16[4,2,2,720,128]{4,3,2,1,0:T(8,128)(2,1)S(1)} collective-permute-done((bf16[4,2,2,720,128]{4,3,2,1,0:T(8,128)(2,1)S(1)}, bf16[4,2,2,720,128]{4,3,2,1,0:T(8,128)(2,1)S(1)}, u32[]{:S(2)}, u32[]{:S(2)}) %collective-permute-start.2) | collective-permute-done | bytes 2949152 | tf_op jit(solution)/shard_map/ppermute | solution.py:298
  189.5 2.4 fusion
  191.9 34.3 %ffn1536.1 = bf16[1536,2880]{1,0:T(8,128)(2,1)} custom-call(bf16[1536,2880]{1,0:T(8,128)(2,1)} %bitcast.12.x_ref, bf16[1,2880,768]{2,1,0:T(8,128)(2,1)} %g_hbm.1, bf16[1,2880,768]{2,1,0:T(8,128)(2,1)} %u_hbm.1, bf16[2880,768]{1,0:T(8,128)(2,1)} %bitcast.55), custom_call_target="tpu_custom_call" | custom-call | flops 20384317440 | bytes 30994720 | tf_op jit(solution)/shard_map/ffn1536/pallas_call | solution.py:159
  226.2 23.3 %all-to-all-start.1 = ((bf16[64,24,2880]{2,1,0:T(8,128)(2,1)}), bf16[64,24,2880]{2,1,0:T(8,128)(2,1)}, u32[]{:S(2)}, u32[]{:S(2)}) async-start(bf16[64,24,2880]{2,1,0:T(8,128)(2,1)} %bitcast.51), calls=%async_computation.1 | async-start | bytes 18087936 | tf_op jit(solution)/shard_map/all_to_all | solution.py:285
  249.6 140.3 %reduce-scatter.4.cloned.1.call-done = bf16[720,128]{1,0:T(8,128)(2,1)} async-done(((bf16[11520,128]{1,0:T(8,128)(2,1)}), bf16[720,128]{1,0:T(8,128)(2,1)}) %reduce-scatter.4.cloned.1.call-update) | async-done | bytes 184336 | tf_op jit(solution)/shard_map/optimization_barrier | solution.py:275
  389.9 68.2 %all-gather.4.cloned.1.call-done = bf16[5760,128]{1,0:T(8,128)(2,1)} async-done(((bf16[720,128]{1,0:T(8,128)(2,1)}), bf16[5760,128]{1,0:T(8,128)(2,1)}) %all-gather.4.cloned.1.call-update) | async-done | bytes 1474576 | tf_op jit(solution)/shard_map/all_gather | solution.py:304
  458.1 2.2 collective-permute-start.4
  460.3 9.6 %combine.1 = (f32[2880,128]{1,0:T(8,128)S(1)}, bf16[2880,128]{1,0:T(8,128)(2,1)S(1)}) custom-call(s32[5]{0:T(128)S(1)} %stack.23.at_ref, bf16[2,768,2880]{2,1,0:T(8,128)(2,1)} %bitcast.21.y_ref, bf16[16,128]{1,0:T(8,128)(2,1)S(1)} %slice.18.own_tail_ref, bf16[16,128]{1,0:T(8,128)(2,1)S(1)} %slice.19.sib_tail_ref), custom_call_target="tpu_custom_call" | custom-call | flops 2264924160 | bytes 12000000 | tf_op jit(solution)/shard_map/combine/pallas_call | solution.py:198
  470.0 3.5 spread.1
  473.5 1.1 fusion.1
  (26 shorter events, 2.1 us)
Async XLA Ops:
  7.9 1.1 copy-start.1
  9.0 0.7 copy-start.2
  9.7 0.7 copy-start.3
  10.4 0.7 copy-start.4
  11.4 3.9 collective-permute-start
  13.4 13.9 %collective-permute-start.1 = (bf16[4,128,512]{2,1,0:T(8,128)(2,1)S(1)}, bf16[4,128,512]{2,1,0:T(8,128)(2,1)S(1)}, u32[]{:S(2)}, u32[]{:S(2)}) collective-permute-start(bf16[4,128,512]{2,1,0:T(8,128)(2,1)S(1)} %get-tuple-element.13), channel_id=1, source_target_pairs={{0,1},{1,0},{2,3},{3,2},{4,5},{5,4},{6,7},{7,6},{8,9},{9,8},{10,11... | collective-permute-start | bytes 1572872 | tf_op jit(solution)/shard_map/ppermute | solution.py:290
  27.3 164.6 %all-to-all-start = ((bf16[64,24,2880]{2,1,0:T(8,128)(2,1)}), bf16[64,24,2880]{2,1,0:T(8,128)(2,1)}, u32[]{:S(2)}, u32[]{:S(2)}) async-start(bf16[64,24,2880]{2,1,0:T(8,128)(2,1)} %bitcast.49), calls=%async_computation | async-start | bytes 18087936 | tf_op jit(solution)/shard_map/all_to_all | solution.py:285
  38.1 138.5 %all-gather.6.cloned.1.call-start = ((), (), s32[]{:S(2)}) async-start(), calls=%async_computation.4 | async-start | bytes 3686400 | tf_op jit(solution)/shard_map/all_gather | solution.py:287
  38.9 351.0 %reduce-scatter.4.cloned.1.call-start = ((), (), s32[]{:S(2)}) async-start(), calls=%async_computation.5 | async-start | bytes 3133440
  176.6 1.8 copy-start.5
  184.0 5.5 %collective-permute-start.2 = (bf16[4,2,2,720,128]{4,3,2,1,0:T(8,128)(2,1)S(1)}, bf16[4,2,2,720,128]{4,3,2,1,0:T(8,128)(2,1)S(1)}, u32[]{:S(2)}, u32[]{:S(2)}) collective-permute-start(bf16[4,2,2,720,128]{4,3,2,1,0:T(8,128)(2,1)S(1)} %slice_bitcast_fusion), channel_id=1, source_target_pairs={{0,8},{8,0},{1,9},{9,1},{2,10},{10,2},{3,11},{11,3},{4,12},{12,4},... | collective-permute-start | bytes 8847368 | tf_op jit(solution)/shard_map/ppermute | solution.py:298
  226.2 234.1 %all-to-all-start.1 = ((bf16[64,24,2880]{2,1,0:T(8,128)(2,1)}), bf16[64,24,2880]{2,1,0:T(8,128)(2,1)}, u32[]{:S(2)}, u32[]{:S(2)}) async-start(bf16[64,24,2880]{2,1,0:T(8,128)(2,1)} %bitcast.51), calls=%async_computation.1 | async-start | bytes 18087936 | tf_op jit(solution)/shard_map/all_to_all | solution.py:285
  249.5 208.6 %all-gather.4.cloned.1.call-start = ((), (), s32[]{:S(2)}) async-start(), calls=%async_computation.3 | async-start | bytes 1658880 | tf_op jit(solution)/shard_map/all_gather | solution.py:304
  458.1 11.9 %collective-permute-start.4 = (bf16[4,1440,128]{2,1,0:T(8,128)(2,1)}, bf16[4,1440,128]{2,1,0:T(8,128)(2,1)S(1)}, u32[]{:S(2)}, u32[]{:S(2)}) collective-permute-start(bf16[4,1440,128]{2,1,0:T(8,128)(2,1)} %bitcast.42), channel_id=1, source_target_pairs={{0,8},{8,0},{1,9},{9,1},{2,10},{10,2},{3,11},{11,3},{4,12},{12,4},... | collective-permute-start | bytes 4423688 | tf_op jit(solution)/shard_map/ppermute | solution.py:305
  460.3 9.7 %copy-start = (bf16[5760,128]{1,0:T(8,128)(2,1)S(1)}, bf16[5760,128]{1,0:T(8,128)(2,1)}, u32[]{:S(2)}) copy-start(bf16[5760,128]{1,0:T(8,128)(2,1)} %all-gather.4.cloned.1.call-done) | copy-start | bytes 4423684
  469.9 3.6 collective-permute-start.3
Sparse Core Ops, SparseCore 0:
  40.6 135.9 all-gather.5
  192.0 197.8 reduce-scatter.3
  392.2 65.8 all-gather.3

commit v6 on v5

--- a/solution.py
+++ b/solution.py
@@ -121,54 +121,59 @@
     )(at, own, sib)
 
 
-def ffn_kernel(x_ref, g_hbm, u_hbm, d_hbm, out_ref, g_ref, u_ref, d_ref, sems):
-    step = pl.program_id(0)
-    copies = [
-        pltpu.make_async_copy(g_hbm.at[0], g_ref, sems.at[0]),
-        pltpu.make_async_copy(u_hbm.at[0], u_ref, sems.at[1]),
-        pltpu.make_async_copy(d_hbm, d_ref, sems.at[2]),
-    ]
-
-    @pl.when(step == 0)
-    def _():
+def ffn_rows(x, g_ref, u_ref, d_ref, copies=()):
+    for c in copies[:1]:
+        c.wait()
+    gating = jnp.dot(x, g_ref[...], preferred_element_type=F32)
+    for c in copies[1:2]:
+        c.wait()
+    upward = jnp.dot(x, u_ref[...], preferred_element_type=F32)
+    active = ((upward + 1.0) * gating * jax.nn.sigmoid(1.702 * gating)).astype(BF)
+    for c in copies[2:]:
+        c.wait()
+    return lax.dot_general(active, d_ref[...], NT, preferred_element_type=F32).astype(BF)
+
+
+def first_kernel(x_ref, g_hbm, u_hbm, d_hbm, out_ref, g_ref, u_ref, d_ref, sems):
+    @pl.when(pl.program_id(0) == 0)
+    def _():
+        copies = [
+            pltpu.make_async_copy(g_hbm.at[0], g_ref, sems.at[0]),
+            pltpu.make_async_copy(u_hbm.at[0], u_ref, sems.at[1]),
+            pltpu.make_async_copy(d_hbm, d_ref, sems.at[2]),
+        ]
         for c in copies:
             c.start()
-        copies[0].wait()
-
-    x = x_ref[...]
-    gating = jnp.dot(x, g_ref[...], preferred_element_type=F32)
-
-    @pl.when(step == 0)
-    def _():
-        copies[1].wait()
-
-    upward = jnp.dot(x, u_ref[...], preferred_element_type=F32)
-    active = ((upward + 1.0) * gating * jax.nn.sigmoid(1.702 * gating)).astype(BF)
-
-    @pl.when(step == 0)
-    def _():
-        copies[2].wait()
-
-    out_ref[...] = lax.dot_general(active, d_ref[...], NT, preferred_element_type=F32).astype(BF)
-
-
-def ffn(x, g, u, d_t):
-    count = x.shape[0]
-    hbm = pl.BlockSpec(memory_space=pltpu.HBM)
-    held = pltpu.VMEM((2880, 768), BF)
-    return pl.pallas_call(
-        ffn_kernel,
-        grid=(count // 512,),
-        in_specs=[pl.BlockSpec((512, 2880), lambda i: (i, 0)), hbm, hbm, hbm],
-        out_specs=pl.BlockSpec((512, 2880), lambda i: (i, 0)),
-        out_shape=pltpu.HBM((count, 2880), BF),
-        scratch_shapes=[held, held, held, pltpu.SemaphoreType.DMA((3,))],
-        compiler_params=pltpu.CompilerParams(vmem_limit_bytes=58 << 20),
+        out_ref[...] = ffn_rows(x_ref[...], g_ref, u_ref, d_ref, copies)
+
+    @pl.when(pl.program_id(0) > 0)
+    def _():
+        out_ref[...] = ffn_rows(x_ref[...], g_ref, u_ref, d_ref)
+
+
+def part_kernel(x_ref, g_ref, u_ref, d_ref, into_ref, out_ref):
+    out_ref[...] = ffn_rows(x_ref[...], g_ref, u_ref, d_ref)
+
+
+def ffn_part(first, count, x, g, u, d_t, into=None):
+    hbm, vm = pl.BlockSpec(memory_space=pltpu.HBM), pl.BlockSpec(memory_space=pltpu.VMEM)
+    block = pl.BlockSpec((384, 2880), lambda i: (first + i, 0))
+    start = into is None
+    held = [pltpu.VMEM((2880, 768), BF)] * 3
+    return pl.pallas_call(
+        first_kernel if start else part_kernel,
+        grid=(count,),
+        in_specs=[block] + ([hbm] * 3 if start else [vm] * 3 + [hbm]),
+        out_specs=[block] + [vm] * 3 * start,
+        out_shape=[pltpu.HBM((1536, 2880), BF)] + held * start,
+        scratch_shapes=[pltpu.SemaphoreType.DMA((3,))] * start,
+        input_output_aliases={} if start else {4: 0},
+        compiler_params=pltpu.CompilerParams(vmem_limit_bytes=(41 if start else 30) << 20),
         cost_estimate=pl.CostEstimate(
-            flops=6 * count * 2880 * 768, bytes_accessed=13_300_000 + count * 2880 * 4, transcendentals=count * 768
+            flops=6 * 384 * count * 2880 * 768, bytes_accessed=4_500_000 * count, transcendentals=384 * 768 * count
         ),
-        name="ffn%d" % count,
-    )(x, g, u, d_t)
+        name="ffn_part%d" % first,
+    )(x, g, u, d_t, *([] if start else [into]))
 
 
 def combine_kernel(at_ref, y_ref, own_tail_ref, sib_tail_ref, own_ref, sib_ref, w_ref, acc_ref):
@@ -213,35 +218,58 @@
     )(at, y, own_tail, sib_tail)
 
 
-def grad_kernel(at_ref, og_ref, mine_ref, far_ref, out_ref):
-    zl = at_ref[2]
+def grad_kernel(at_ref, p0_ref, p1_ref, p2_ref, p3_ref, mine_ref, far_ref, out_ref):
+    y, x = at_ref[1], at_ref[3]
     total = None
-    for o in (0, 2):
-        right = [jnp.concatenate([mine_ref[o + i], far_ref[o + i]], axis=1) for i in range(2)]
-        left = jnp.concatenate([og_ref[o], og_ref[o + 1]], axis=1)
+    for o, (one, two) in ((0, (p0_ref, p1_ref)), (2, (p2_ref, p3_ref))):
+        right = [
+            jnp.concatenate([mine_ref[(y + o + i) & 3], far_ref[(y + o + i) & 3]], axis=1) for i in range(2)
+        ]
+        left = jnp.concatenate([one[...], two[...]], axis=1)
         term = jnp.dot(left, jnp.concatenate(right, axis=0), preferred_element_type=F32)
         total = term if total is None else total + term
     for j in range(4):
         for side in range(2):
             low = 512 * side + 128 * j
-            out_ref[0, j, 0, pl.ds(side ^ zl, 1)] = total[None, :, low : low + 128].astype(BF)
-
-
-def local_grad(at, og, mine, far):
+            out_ref[0, pl.ds((j - x) & 3, 1), 0, side] = total[None, :, low : low + 128].astype(BF)
+
+
+def local_grad(at, blocks, mine, far):
     vm = pl.BlockSpec(memory_space=pltpu.VMEM)
     return pl.pallas_call(
         grad_kernel,
         grid_spec=pltpu.PrefetchScalarGridSpec(
             num_scalar_prefetch=1,
             grid=(4,),
-            in_specs=[pl.BlockSpec((4, 720, 128), lambda i, at: (0, i, 0)), vm, vm],
-            out_specs=pl.BlockSpec((1, 4, 1, 2, 720, 128), lambda i, at: ((i >> 1) ^ at[0], 0, i & 1, 0, 0, 0)),
+            in_specs=[pl.BlockSpec((720, 128), lambda i, at: (i, 0))] * 4 + [vm, vm],
+            out_specs=pl.BlockSpec(
+                (1, 4, 1, 2, 720, 128), lambda i, at: ((i >> 1) ^ at[0], 0, (i & 1) ^ at[4], 0, 0, 0)
+            ),
         ),
         out_shape=jax.ShapeDtypeStruct((2, 4, 2, 2, 720, 128), BF),
         compiler_params=pltpu.CompilerParams(vmem_limit_bytes=32 << 20),
         cost_estimate=pl.CostEstimate(flops=2 * 1024 * 512 * 2880, bytes_accessed=10_000_000, transcendentals=0),
         name="local_grad",
-    )(at, og, mine, far)
+    )(at, *blocks, mine, far)
+
+
+def sum_kernel(a_ref, b_ref, c_ref, d_ref, kept_ref, gone_ref):
+    total = a_ref[...] + b_ref[...].astype(F32) + c_ref[...].astype(F32) + d_ref[...].astype(F32)
+    kept_ref[...] = total[0]
+    gone_ref[...] = total[1].astype(BF)
+
+
+def sum_terms(own, terms):
+    vm = pl.BlockSpec(memory_space=pltpu.VMEM)
+    return pl.pallas_call(
+        sum_kernel,
+        in_specs=[vm] * 4,
+        out_specs=[vm] * 2,
+        out_shape=[jax.ShapeDtypeStruct((2, 720, 128), F32), jax.ShapeDtypeStruct((2, 720, 128), BF)],
+        compiler_params=pltpu.CompilerParams(vmem_limit_bytes=16 << 20),
+        cost_estimate=pl.CostEstimate(flops=1 << 20, bytes_accessed=4_800_000, transcendentals=0),
+        name="sum_terms",
+    )(own, *terms)
 
 
 def spread_kernel(at_ref, own_ref, sib_ref, out_ref):
@@ -258,7 +286,7 @@
             num_scalar_prefetch=1,
             grid=(4,),
             in_specs=[block, block],
-            out_specs=pl.BlockSpec((2, 1440, 128), lambda i, at: (0, 0, i)),
+            out_specs=pl.BlockSpec((2, 1440, 128), lambda i, at: (0, 0, (at[3] + i) & 3)),
         ),
         out_shape=jax.ShapeDtypeStruct((2, 1440, 512), F32),
         compiler_params=pltpu.CompilerParams(vmem_limit_bytes=16 << 20),
@@ -271,20 +299,25 @@
     return functools.partial(lax.ppermute, axis_name=axis, perm=[(i, (i + by) % n) for i in range(n)])
 
 
+def from_others(block, axis):
+    return [shift(axis, -o, 4)(block) for o in (1, 2, 3)]
+
+
 def after(value, *others):
     return lax.optimization_barrier((value,) + others)[0]
 
 
 def local(tokens, expert_ids, gate_raw, overflow_shift, limits, gate_w, up_w, down_w, context, out_grad):
     at = jnp.stack([lax.axis_index(a) for a in ("core", "y", "zl", "x", "zh")]).astype(jnp.int32)
-    zl = lax.axis_index("zl")
-    core_swap, zl_swap = shift("core", 1, 2), shift("zl", 1, 2)
+    zh, zl = lax.axis_index("zh"), lax.axis_index("zl")
+    core_swap, zl_swap, zh_swap = shift("core", 1, 2), shift("zl", 1, 2), shift("zh", 1, 2)
     over = ("zl", "x", "zh", "y")
 
     def exchange(rows):
         return lax.all_to_all(rows.reshape(64, 24, 2880), over, split_axis=0, concat_axis=0, tiled=True)
 
-    og = lax.all_gather(out_grad.T, "y", axis=0)
+    og = out_grad.T
+    ogs = from_others(og, "y")
     ctx = context.reshape(4, 2, 128, 512)
     ctx_mine = lax.dynamic_index_in_dim(ctx, zl, 1, keepdims=False)
     ctx_far = zl_swap(lax.dynamic_index_in_dim(ctx, 1 - zl, 1, keepdims=False))
@@ -292,19 +325,30 @@
     lim = jnp.broadcast_to(limits.astype(F32)[:, None], (64, 128))
     mine = place_call(tokens.T, expert_ids.T, overflow_shift.T, gate_raw.T, lim)
     sibling = core_swap(mine)
-    got = exchange(after(rows_of(at, mine, sibling), ctx_far)).reshape(1536, 2880)
-
-    grads = local_grad(at, og, ctx_mine, ctx_far)
-    part = (grads[0].astype(F32) + core_swap(grads[1]).astype(F32)).astype(BF)
-    own_part = lax.psum_scatter(
-        part.reshape(16 * 720, 128), ("x", "zh", "zl"), scatter_dimension=0, tiled=True
-    )
-    out = ffn(after(got, part), gate_w, up_w, down_w[0].T)
-    back = exchange(out)
-    full = lax.all_gather(after(own_part, out), ("x", "zh"), axis=0, tiled=True).reshape(4, 1440, 128)
+    got = exchange(after(rows_of(at, mine, sibling), ctx_far, *ogs)).reshape(1536, 2880)
+
+    grads = local_grad(at, [og] + ogs, ctx_mine, ctx_far)
+    part = grads[0].astype(F32) + core_swap(grads[1]).astype(F32)
+    terms = [shift("x", o, 4)(part[o].astype(BF)) for o in (1, 2, 3)]
+    out, *weights = ffn_part(0, 1, after(got, part), gate_w, up_w, down_w[0].T)
+    terms = lax.optimization_barrier((*terms, out))[:-1]
+    kept, gone = sum_terms(part[0], terms)
+    came = zh_swap(gone)
+    (out,) = ffn_part(1, 1, got, *weights, after(out, gone))
+    total = kept + after(came, out).astype(F32)
+    gone = total[1].astype(BF)
+    came = zl_swap(gone)
+    (out,) = ffn_part(2, 1, got, *weights, after(out, gone))
+    final = (total[0] + after(came, out).astype(F32)).astype(BF)
+    back = zh_swap(final)
+    (out,) = ffn_part(3, 1, got, *weights, after(out, final))
+    back = after(back, out)
+    block = jnp.concatenate([jnp.where(zh == 0, final, back), jnp.where(zh == 0, back, final)])
+    full = jnp.stack([block] + from_others(block, "x"))
     grad = spread(at, full, core_swap(full)).reshape(2880, 512)
 
-    own, sib = combine(at, back.reshape(2, 768, 2880), mine[2880:], sibling[2880:])
+    out = exchange(after(out, block))
+    own, sib = combine(at, out.reshape(2, 768, 2880), mine[2880:], sibling[2880:])
     mixed = (own + core_swap(sib).astype(F32)).astype(BF)
     return mixed.T, grad.T
 

time: 484 us -> 437 us (0.903)
  waiting for transfers between devices: 359 us -> 294 us
  starting transfers between devices: 39.4 us -> 56 us
  between operations: 13.8 us -> 0.79 us
  Pallas kernels: 58.5 us -> 66.8 us
  local copies, waits for them, and re-layouts: 6.65 us -> 12.3 us
    all_gather x2 -> x0, waiting for transfers between devices: 206 us -> none  [the longest x1 138 us: local(): og = lax.all_gather(out_grad.T, 'y', axis=0)]
    ppermute x1 -> x13, waiting for transfers between devices: 5 us -> 182 us  [the longest x6 166 us: from_others(): return [shift(axis, -o, 4)(block) for o in (1, 2, 3)]]
    optimization_barrier x1 -> x0, waiting for transfers between devices: 140 us -> none  [after(): return lax.optimization_barrier((value,) + others)[0]]
    all_to_all x2, waiting for transfers between devices: 0.01 us -> 107 us  [exchange(): lax.all_to_all(rows.reshape(64, 24, 2880), over, split_axis=0, concat_axi...]
    ppermute x1 -> x13, starting transfers between devices: 0.52 us -> 15.1 us  [the longest x6 7.19 us: from_others(): return [shift(axis, -o, 4)(block) for o in (1, 2, 3)]]
    pallas_call x1 -> x5, Pallas kernels: 34.3 us -> 40.8 us  [the longest x4 38.9 us: ffn_part(): pl.pallas_call(first_kernel if start else part_kernel, grid=(count,), in_...]
  transfers between devices with their start and end apart: 10 -> 19, of which waited for: 5 -> 7; matrix products, arithmetic and copies ran while one was open for 1% -> 2% of each run, Pallas kernels for 12% -> 15%
where the time goes in v6:
time: 437 us; the launch traced here: 436 us
  waiting for transfers between devices  294 us (67%)
  Pallas kernels  66.8 us (15%)
  starting transfers between devices  56 us (13%)
  local copies, waits for them, and re-layouts  12.3 us (3%)
  other arithmetic  5.7 us (1%)
    ppermute x6, waiting for transfers between devices, from_others(): return [shift(axis, -o, 4)(block) for o in (1, 2, 3)]  166 us
    all_to_all x2, waiting for transfers between devices, exchange(): lax.all_to_all(rows.reshape(64, 24, 2880), over, split_axis=0, concat_axi...  107 us
    pallas_call x4, Pallas kernels, ffn_part(): pl.pallas_call(first_kernel if start else part_kernel, grid=(count,), in_...  38.9 us
    all_to_all x2, starting transfers between devices, exchange(): lax.all_to_all(rows.reshape(64, 24, 2880), over, split_axis=0, concat_axi...  34.3 us
    ppermute x3, waiting for transfers between devices, local(): terms = [shift('x', o, 4)(part[o].astype(BF)) for o in (1, 2, 3)]  10.9 us
    pallas_call x1, Pallas kernels, combine(): pl.pallas_call(combine_kernel, grid=(6,), in_specs=[pl.BlockSpec(memory_s...  9.45 us
  transfers between devices with their start and end apart: 19, of which 7 were waited for; matrix products, arithmetic and copies ran while one was open for 2% of the time, Pallas kernels for 15%

profile of v6, /device:TPU:5, one launch (start us, length us, event | category | flops | bytes accessed | tf_op | source)
XLA Modules:
  0.0 435.9 jit_solution(335863797337714818)
XLA Ops:
  6.9 2.6 collective-permute-start.3
  10.6 2.1 dynamic-slice_bitcast_fusion
  14.4 5.5 %rows.1 = bf16[2,768,2880]{2,1,0:T(8,128)(2,1)} custom-call(s32[5]{0:T(128)S(1)} %stack.38.at_ref, bf16[2896,128]{1,0:T(8,128)(2,1)S(1)} %place.1.own_ref, bf16[2896,128]{1,0:T(8,128)(2,1)S(1)} %collective-permute-done.sib_ref), custom_call_target="tpu_custom_call" | custom-call | flops 1132462080 | bytes 10000000 | tf_op jit(solution)/shard_map/rows/pallas_call | solution.py:111
  19.9 5.9 %collective-permute-done.1.far_ref = bf16[4,128,512]{2,1,0:T(8,128)(2,1)S(1)} collective-permute-done((bf16[4,128,512]{2,1,0:T(8,128)(2,1)}, bf16[4,128,512]{2,1,0:T(8,128)(2,1)S(1)}, u32[]{:S(2)}, u32[]{:S(2)}) %collective-permute-start.1) | collective-permute-done | bytes 524320 | tf_op jit(solution)/shard_map/ppermute | solution.py:323
  26.6 15.6 %collective-permute-done.3.p2_ref = bf16[2880,128]{1,0:T(8,128)(2,1)} collective-permute-done((bf16[2880,128]{1,0:T(8,128)(2,1)}, bf16[2880,128]{1,0:T(8,128)(2,1)}, u32[]{:S(2)}, u32[]{:S(2)}) %collective-permute-start.3) | collective-permute-done | bytes 737312 | tf_op jit(solution)/shard_map/ppermute | solution.py:303
  42.2 10.4 %all-to-all-start = ((bf16[64,24,2880]{2,1,0:T(8,128)(2,1)}), bf16[64,24,2880]{2,1,0:T(8,128)(2,1)}, u32[]{:S(2)}, u32[]{:S(2)}) async-start(bf16[64,24,2880]{2,1,0:T(8,128)(2,1)} %bitcast.70), calls=%async_computation | async-start | bytes 18087936 | tf_op jit(solution)/shard_map/all_to_all | solution.py:317
  53.8 5.8 %local_grad.1 = bf16[2,4,2,2,720,128]{5,4,3,2,1,0:T(8,128)(2,1)S(1)} custom-call(s32[5]{0:T(128)S(1)} %stack.38.at_ref, bf16[2880,128]{1,0:T(8,128)(2,1)S(1)} %bitcast.68, bf16[2880,128]{1,0:T(8,128)(2,1)} %collective-permute-done.2.p1_ref, bf16[2880,128]{1,0:T(8,128)(2,1)} %collective-permute-done.3.p2_ref, bf16[2880,128]{1,0:T(8,128)(2,1)S(1)} %copy-done.7, ...), custom_call_target="tpu_custom_call" | custom-call | flops 3019898880 | bytes 10000000 | tf_op jit(solution)/shard_map/local_grad/pallas_call | solution.py:239
  59.6 1.9 slice_bitcast_fusion
  64.7 5.3 %collective-permute-done.5 = bf16[4,2,2,720,128]{4,3,2,1,0:T(8,128)(2,1)} collective-permute-done((bf16[4,2,2,720,128]{4,3,2,1,0:T(8,128)(2,1)}, bf16[4,2,2,720,128]{4,3,2,1,0:T(8,128)(2,1)}, u32[]{:S(2)}, u32[]{:S(2)}) %collective-permute-start.5) | collective-permute-done | bytes 2949152 | tf_op jit(solution)/shard_map/ppermute | solution.py:331
  70.0 3.6 fusion.5
  75.3 2.4 collective-permute-start.7
  77.8 106.6 %all-to-all-done = bf16[64,24,2880]{2,1,0:T(8,128)(2,1)} async-done(((bf16[64,24,2880]{2,1,0:T(8,128)(2,1)}), bf16[64,24,2880]{2,1,0:T(8,128)(2,1)}, u32[]{:S(2)}, u32[]{:S(2)}) %all-to-all-start) | async-done | bytes 8847392 | tf_op jit(solution)/shard_map/all_to_all | solution.py:317
  184.5 12.5 %ffn_part0.1 = (bf16[1536,2880]{1,0:T(8,128)(2,1)}, bf16[2880,768]{1,0:T(8,128)(2,1)S(1)}, bf16[2880,768]{1,0:T(8,128)(2,1)S(1)}, bf16[2880,768]{1,0:T(8,128)(2,1)S(1)}) custom-call(bf16[1536,2880]{1,0:T(8,128)(2,1)} %bitcast.13.x_ref, bf16[1,2880,768]{2,1,0:T(8,128)(2,1)} %g_hbm.1, bf16[1,2880,768]{2,1,0:T(8,128)(2,1)} %u_hbm.1, bf16[2880,768]{1,0:T(8,128)(2,1)} %bitcast.72), custom_call_target="tpu_custom_call" | custom-call | flops 5096079360 | bytes 4500000 | tf_op jit(solution)/shard_map/ffn_part0/pallas_call | solution.py:163
  197.0 10.9 %collective-permute-done.8.d_ref = bf16[2,2,720,128]{3,2,1,0:T(8,128)(2,1)} collective-permute-done((bf16[2,2,720,128]{3,2,1,0:T(8,128)(2,1)}, bf16[2,2,720,128]{3,2,1,0:T(8,128)(2,1)}, u32[]{:S(2)}, u32[]{:S(2)}) %collective-permute-start.8) | collective-permute-done | bytes 737312 | tf_op jit(solution)/shard_map/ppermute | solution.py:332
  209.9 8.9 %ffn_part1.1.into_ref = bf16[1536,2880]{1,0:T(8,128)(2,1)} custom-call(bf16[1536,2880]{1,0:T(8,128)(2,1)} %bitcast.13.x_ref, bf16[2880,768]{1,0:T(8,128)(2,1)S(1)} %get-tuple-element.24.g_ref, bf16[2880,768]{1,0:T(8,128)(2,1)S(1)} %get-tuple-element.25.u_ref, bf16[2880,768]{1,0:T(8,128)(2,1)S(1)} %get-tuple-element.26.d_ref, ...), custom_call_target="tpu_custom_call", output_to_operand_aliasing={{}: (4, {})} | custom-call | flops 5096079360 | bytes 4500000 | tf_op jit(solution)/shard_map/ffn_part1/pallas_call | solution.py:163
  219.1 8.7 %ffn_part2.1.into_ref = bf16[1536,2880]{1,0:T(8,128)(2,1)} custom-call(bf16[1536,2880]{1,0:T(8,128)(2,1)} %bitcast.13.x_ref, bf16[2880,768]{1,0:T(8,128)(2,1)S(1)} %get-tuple-element.24.g_ref, bf16[2880,768]{1,0:T(8,128)(2,1)S(1)} %get-tuple-element.25.u_ref, bf16[2880,768]{1,0:T(8,128)(2,1)S(1)} %get-tuple-element.26.d_ref, ...), custom_call_target="tpu_custom_call", output_to_operand_aliasing={{}: (4, {})} | custom-call | flops 5096079360 | bytes 4500000 | tf_op jit(solution)/shard_map/ffn_part2/pallas_call | solution.py:163
  227.9 3.2 collective-permute-start.11
  231.1 8.8 %ffn_part3.1 = bf16[1536,2880]{1,0:T(8,128)(2,1)} custom-call(bf16[1536,2880]{1,0:T(8,128)(2,1)} %bitcast.13.x_ref, bf16[2880,768]{1,0:T(8,128)(2,1)S(1)} %get-tuple-element.24.g_ref, bf16[2880,768]{1,0:T(8,128)(2,1)S(1)} %get-tuple-element.25.u_ref, bf16[2880,768]{1,0:T(8,128)(2,1)S(1)} %get-tuple-element.26.d_ref, ...), custom_call_target="tpu_custom_call", output_to_operand_aliasing={{}: (4, {})} | custom-call | flops 5096079360 | bytes 4500000 | tf_op jit(solution)/shard_map/ffn_part3/pallas_call | solution.py:163
  240.0 23.8 %all-to-all-start.1 = ((bf16[64,24,2880]{2,1,0:T(8,128)(2,1)}), bf16[64,24,2880]{2,1,0:T(8,128)(2,1)}, u32[]{:S(2)}, u32[]{:S(2)}) async-start(bf16[64,24,2880]{2,1,0:T(8,128)(2,1)} %bitcast.69), calls=%async_computation.1 | async-start | bytes 18087936 | tf_op jit(solution)/shard_map/all_to_all | solution.py:317
  266.0 130.5 %collective-permute-done.14 = bf16[1440,128]{1,0:T(8,128)(2,1)S(1)} collective-permute-done((bf16[1440,128]{1,0:T(8,128)(2,1)S(1)}, bf16[1440,128]{1,0:T(8,128)(2,1)S(1)}, u32[]{:S(2)}, u32[]{:S(2)}) %collective-permute-start.14) | collective-permute-done | bytes 368672 | tf_op jit(solution)/shard_map/ppermute | solution.py:303
  396.5 19.4 %collective-permute-done.13 = bf16[1440,128]{1,0:T(8,128)(2,1)S(1)} collective-permute-done((bf16[1440,128]{1,0:T(8,128)(2,1)S(1)}, bf16[1440,128]{1,0:T(8,128)(2,1)S(1)}, u32[]{:S(2)}, u32[]{:S(2)}) %collective-permute-start.13) | collective-permute-done | bytes 368672 | tf_op jit(solution)/shard_map/ppermute | solution.py:303
  416.1 4.2 collective-permute-start.16
  420.3 9.4 %combine.1 = (f32[2880,128]{1,0:T(8,128)S(1)}, bf16[2880,128]{1,0:T(8,128)(2,1)S(1)}) custom-call(s32[5]{0:T(128)S(1)} %stack.38.at_ref, bf16[2,768,2880]{2,1,0:T(8,128)(2,1)} %bitcast.26.y_ref, bf16[16,128]{1,0:T(8,128)(2,1)S(1)} %slice.52.own_tail_ref, bf16[16,128]{1,0:T(8,128)(2,1)S(1)} %slice.53.sib_tail_ref), custom_call_target="tpu_custom_call" | custom-call | flops 2264924160 | bytes 12000000 | tf_op jit(solution)/shard_map/combine/pallas_call | solution.py:203
  429.9 5.0 %spread.1 = f32[2,1440,512]{2,1,0:T(8,128)} custom-call(s32[5]{0:T(128)S(1)} %stack.38.at_ref, bf16[4,1440,128]{2,1,0:T(8,128)(2,1)S(1)} %pad_maximum_fusion.own_ref, bf16[4,1440,128]{2,1,0:T(8,128)(2,1)} %collective-permute-done.16.sib_ref), custom_call_target="tpu_custom_call" | custom-call | bytes 9000000 | tf_op jit(solution)/shard_map/spread/pallas_call | solution.py:283
  (57 shorter events, 22.0 us)
Async XLA Ops:
  1.4 1.1 copy-start.1
  4.8 9.5 %collective-permute-start = (bf16[2896,128]{1,0:T(8,128)(2,1)S(1)}, bf16[2896,128]{1,0:T(8,128)(2,1)S(1)}, u32[]{:S(2)}, u32[]{:S(2)}) collective-permute-start(bf16[2896,128]{1,0:T(8,128)(2,1)S(1)} %place.1.own_ref), channel_id=1, source_target_pairs={{0,8},{8,0},{1,9},{9,1},{2,10},{10,2},{3,11},{11,3},{4,12},{12,4},... | collective-permute-start | bytes 2224136 | tf_op jit(solution)/shard_map/ppermute | solution.py:327
  5.6 20.2 %collective-permute-start.4 = (bf16[2880,128]{1,0:T(8,128)(2,1)}, bf16[2880,128]{1,0:T(8,128)(2,1)S(1)}, u32[]{:S(2)}, u32[]{:S(2)}) collective-permute-start(bf16[2880,128]{1,0:T(8,128)(2,1)} %bitcast.65), channel_id=1, source_target_pairs={{0,2},{2,4},{4,6},{6,0},{1,3},{3,5},{5,7},{7,1},{8,10},{10,12},{12... | collective-permute-start | bytes 2211848 | tf_op jit(solution)/shard_map/ppermute | solution.py:303
  6.9 35.3 %collective-permute-start.3 = (bf16[2880,128]{1,0:T(8,128)(2,1)}, bf16[2880,128]{1,0:T(8,128)(2,1)}, u32[]{:S(2)}, u32[]{:S(2)}) collective-permute-start(bf16[2880,128]{1,0:T(8,128)(2,1)} %bitcast.66), channel_id=1, source_target_pairs={{0,4},{2,6},{4,0},{6,2},{1,5},{3,7},{5,1},{7,3},{8,12},{10,14},{12... | collective-permute-start | bytes 2211848 | tf_op jit(solution)/shard_map/ppermute | solution.py:303
  9.5 32.7 %collective-permute-start.2 = (bf16[2880,128]{1,0:T(8,128)(2,1)}, bf16[2880,128]{1,0:T(8,128)(2,1)}, u32[]{:S(2)}, u32[]{:S(2)}) collective-permute-start(bf16[2880,128]{1,0:T(8,128)(2,1)} %bitcast.67), channel_id=1, source_target_pairs={{0,6},{2,0},{4,2},{6,4},{1,7},{3,1},{5,3},{7,5},{8,14},{10,8},{12,... | collective-permute-start | bytes 2211848 | tf_op jit(solution)/shard_map/ppermute | solution.py:303
  12.7 13.1 %collective-permute-start.1 = (bf16[4,128,512]{2,1,0:T(8,128)(2,1)}, bf16[4,128,512]{2,1,0:T(8,128)(2,1)S(1)}, u32[]{:S(2)}, u32[]{:S(2)}) collective-permute-start(bf16[4,128,512]{2,1,0:T(8,128)(2,1)} %get-tuple-element.48), channel_id=1, source_target_pairs={{0,1},{1,0},{2,3},{3,2},{4,5},{5,4},{6,7},{7,6},{8,9},{9,8},{10,11... | collective-permute-start | bytes 1572872 | tf_op jit(solution)/shard_map/ppermute | solution.py:323
  25.8 0.9 copy-start.6
  42.2 10.4 %copy-start.5 = (bf16[128,2880]{0,1:T(8,128)(2,1)S(1)}, bf16[128,2880]{0,1:T(8,128)(2,1)}, u32[]{:S(2)}) copy-start(bf16[128,2880]{0,1:T(8,128)(2,1)} %param.19) | copy-start | bytes 2211844
  42.2 142.3 %all-to-all-start = ((bf16[64,24,2880]{2,1,0:T(8,128)(2,1)}), bf16[64,24,2880]{2,1,0:T(8,128)(2,1)}, u32[]{:S(2)}, u32[]{:S(2)}) async-start(bf16[64,24,2880]{2,1,0:T(8,128)(2,1)} %bitcast.70), calls=%async_computation | async-start | bytes 18087936 | tf_op jit(solution)/shard_map/all_to_all | solution.py:317
  52.7 1.1 copy-start.7
  59.6 3.5 copy-start
  63.1 6.9 %collective-permute-start.5 = (bf16[4,2,2,720,128]{4,3,2,1,0:T(8,128)(2,1)}, bf16[4,2,2,720,128]{4,3,2,1,0:T(8,128)(2,1)}, u32[]{:S(2)}, u32[]{:S(2)}) collective-permute-start(bf16[4,2,2,720,128]{4,3,2,1,0:T(8,128)(2,1)} %slice_bitcast_fusion), channel_id=1, source_target_pairs={{0,8},{8,0},{1,9},{9,1},{2,10},{10,2},{3,11},{11,3},{4,12},{12,4},... | collective-permute-start | bytes 8847368 | tf_op jit(solution)/shard_map/ppermute | solution.py:331
  75.0 132.8 %collective-permute-start.8 = (bf16[2,2,720,128]{3,2,1,0:T(8,128)(2,1)}, bf16[2,2,720,128]{3,2,1,0:T(8,128)(2,1)}, u32[]{:S(2)}, u32[]{:S(2)}) collective-permute-start(bf16[2,2,720,128]{3,2,1,0:T(8,128)(2,1)} %get-tuple-element.44), channel_id=1, source_target_pairs={{0,96},{32,0},{64,32},{96,64},{1,97},{33,1},{65,33},{97,65},{2,98}... | collective-permute-start | bytes 2211848 | tf_op jit(solution)/shard_map/ppermute | solution.py:332
  75.3 132.6 %collective-permute-start.7 = (bf16[2,2,720,128]{3,2,1,0:T(8,128)(2,1)}, bf16[2,2,720,128]{3,2,1,0:T(8,128)(2,1)}, u32[]{:S(2)}, u32[]{:S(2)}) collective-permute-start(bf16[2,2,720,128]{3,2,1,0:T(8,128)(2,1)} %get-tuple-element.45), channel_id=1, source_target_pairs={{0,64},{32,96},{64,0},{96,32},{1,65},{33,97},{65,1},{97,33},{2,66}... | collective-permute-start | bytes 2211848 | tf_op jit(solution)/shard_map/ppermute | solution.py:332
  77.7 130.1 %collective-permute-start.6 = (bf16[2,2,720,128]{3,2,1,0:T(8,128)(2,1)}, bf16[2,2,720,128]{3,2,1,0:T(8,128)(2,1)}, u32[]{:S(2)}, u32[]{:S(2)}) collective-permute-start(bf16[2,2,720,128]{3,2,1,0:T(8,128)(2,1)} %get-tuple-element.46), channel_id=1, source_target_pairs={{0,32},{32,64},{64,96},{96,0},{1,33},{33,65},{65,97},{97,1},{2,34}... | collective-permute-start | bytes 2211848 | tf_op jit(solution)/shard_map/ppermute | solution.py:332
  209.8 9.0 %collective-permute-start.9 = (bf16[2,720,128]{2,1,0:T(8,128)(2,1)S(1)}, bf16[2,720,128]{2,1,0:T(8,128)(2,1)S(1)}, u32[]{:S(2)}, u32[]{:S(2)}) collective-permute-start(bf16[2,720,128]{2,1,0:T(8,128)(2,1)S(1)} %get-tuple-element.31), channel_id=1, source_target_pairs={{0,16},{16,0},{1,17},{17,1},{2,18},{18,2},{3,19},{19,3},{4,20},{20... | collective-permute-start | bytes 1105928 | tf_op jit(solution)/shard_map/ppermute | solution.py:336
  218.8 9.1 %collective-permute-start.10 = (bf16[720,128]{1,0:T(8,128)(2,1)S(1)}, bf16[720,128]{1,0:T(8,128)(2,1)S(1)}, u32[]{:S(2)}, u32[]{:S(2)}) collective-permute-start(bf16[720,128]{1,0:T(8,128)(2,1)S(1)} %fusion.3), channel_id=1, source_target_pairs={{0,1},{1,0},{2,3},{3,2},{4,5},{5,4},{6,7},{7,6},{8,9},{9,8},{10,11... | collective-permute-start | bytes 552968 | tf_op jit(solution)/shard_map/ppermute | solution.py:340
  227.9 11.9 %collective-permute-start.11 = (bf16[720,128]{1,0:T(8,128)(2,1)S(1)}, bf16[720,128]{1,0:T(8,128)(2,1)S(1)}, u32[]{:S(2)}, u32[]{:S(2)}) collective-permute-start(bf16[720,128]{1,0:T(8,128)(2,1)S(1)} %fusion.2), channel_id=1, source_target_pairs={{0,16},{16,0},{1,17},{17,1},{2,18},{18,2},{3,19},{19,3},{4,20},{20... | collective-permute-start | bytes 552968 | tf_op jit(solution)/shard_map/ppermute | solution.py:343
  240.0 180.3 %all-to-all-start.1 = ((bf16[64,24,2880]{2,1,0:T(8,128)(2,1)}), bf16[64,24,2880]{2,1,0:T(8,128)(2,1)}, u32[]{:S(2)}, u32[]{:S(2)}) async-start(bf16[64,24,2880]{2,1,0:T(8,128)(2,1)} %bitcast.69), calls=%async_computation.1 | async-start | bytes 18087936 | tf_op jit(solution)/shard_map/all_to_all | solution.py:317
  263.8 132.7 %collective-permute-start.14 = (bf16[1440,128]{1,0:T(8,128)(2,1)S(1)}, bf16[1440,128]{1,0:T(8,128)(2,1)S(1)}, u32[]{:S(2)}, u32[]{:S(2)}) collective-permute-start(bf16[1440,128]{1,0:T(8,128)(2,1)S(1)} %get-tuple-element.50), channel_id=1, source_target_pairs={{0,64},{32,96},{64,0},{96,32},{1,65},{33,97},{65,1},{97,33},{2,66}... | collective-permute-start | bytes 1105928 | tf_op jit(solution)/shard_map/ppermute | solution.py:303
  264.4 151.5 %collective-permute-start.13 = (bf16[1440,128]{1,0:T(8,128)(2,1)S(1)}, bf16[1440,128]{1,0:T(8,128)(2,1)S(1)}, u32[]{:S(2)}, u32[]{:S(2)}) collective-permute-start(bf16[1440,128]{1,0:T(8,128)(2,1)S(1)} %get-tuple-element.50), channel_id=1, source_target_pairs={{0,96},{32,0},{64,32},{96,64},{1,97},{33,1},{65,33},{97,65},{2,98}... | collective-permute-start | bytes 1105928 | tf_op jit(solution)/shard_map/ppermute | solution.py:303
  266.0 149.9 %collective-permute-start.15 = (bf16[1440,128]{1,0:T(8,128)(2,1)S(1)}, bf16[1440,128]{1,0:T(8,128)(2,1)S(1)}, u32[]{:S(2)}, u32[]{:S(2)}) collective-permute-start(bf16[1440,128]{1,0:T(8,128)(2,1)S(1)} %get-tuple-element.50), channel_id=1, source_target_pairs={{0,32},{32,64},{64,96},{96,0},{1,33},{33,65},{65,97},{97,1},{2,34}... | collective-permute-start | bytes 1105928 | tf_op jit(solution)/shard_map/ppermute | solution.py:303
  416.1 13.8 %collective-permute-start.16 = (bf16[4,1440,128]{2,1,0:T(8,128)(2,1)S(1)}, bf16[4,1440,128]{2,1,0:T(8,128)(2,1)}, u32[]{:S(2)}, u32[]{:S(2)}) collective-permute-start(bf16[4,1440,128]{2,1,0:T(8,128)(2,1)S(1)} %pad_maximum_fusion.own_ref), channel_id=1, source_target_pairs={{0,8},{8,0},{1,9},{9,1},{2,10},{10,2},{3,11},{11,3},{4,12},{12,4},... | collective-permute-start | bytes 4423688 | tf_op jit(solution)/shard_map/ppermute | solution.py:348
  429.8 5.1 %collective-permute-start.12 = (bf16[2880,128]{1,0:T(8,128)(2,1)S(1)}, bf16[2880,128]{1,0:T(8,128)(2,1)S(1)}, u32[]{:S(2)}, u32[]{:S(2)}) collective-permute-start(bf16[2880,128]{1,0:T(8,128)(2,1)S(1)} %get-tuple-element.41), channel_id=1, source_target_pairs={{0,8},{8,0},{1,9},{9,1},{2,10},{10,2},{3,11},{11,3},{4,12},{12,4},... | collective-permute-start | bytes 2211848 | tf_op jit(solution)/shard_map/ppermute | solution.py:352
  (3 other events, 2.0 us)

commit v7 on v3

--- a/solution.py
+++ b/solution.py
@@ -272,7 +272,7 @@
         term = jnp.dot(left, jnp.concatenate([same, other], axis=0), preferred_element_type=F32)
         total = term if total is None else total + term
     for j in range(4):
-        out_ref[0, pl.ds((j - x) & 3, 1)] = total[None, :, 128 * j : 128 * j + 128].astype(BF)
+        out_ref[0, 0, pl.ds((j - x) & 3, 1)] = total[None, :, 128 * j : 128 * j + 128].astype(BF)
 
 
 def local_grad(at, pairs, context):
@@ -283,9 +283,9 @@
             grid=(4,),
             in_specs=[pl.BlockSpec((2, 720, 128), lambda i, at: (0, i, 0))] * 4
             + [pl.BlockSpec(memory_space=pltpu.VMEM)],
-            out_specs=pl.BlockSpec((1, 4, 720, 128), lambda i, at: ((i >> 1) ^ at[0], 0, i & 1, 0)),
+            out_specs=pl.BlockSpec((1, 1, 4, 720, 128), lambda i, at: ((i >> 1) ^ at[0], (i & 1) ^ at[4], 0, 0, 0)),
         ),
-        out_shape=jax.ShapeDtypeStruct((2, 4, 1440, 128), BF),
+        out_shape=jax.ShapeDtypeStruct((2, 2, 4, 720, 128), BF),
         compiler_params=pltpu.CompilerParams(vmem_limit_bytes=24 << 20),
         cost_estimate=pl.CostEstimate(flops=2 * 1024 * 512 * 2880, bytes_accessed=10_000_000, transcendentals=0),
         name="local_grad",
@@ -293,22 +293,23 @@
 
 
 def spread_kernel(at_ref, own_ref, sib_ref, out_ref):
-    core = at_ref[0]
-    out_ref[pl.ds(core, 1)] = own_ref[...].astype(F32)
-    out_ref[pl.ds(1 - core, 1)] = sib_ref[...].astype(F32)
+    core, zh = at_ref[0], at_ref[4]
+    for c, ref in ((core, own_ref), (1 - core, sib_ref)):
+        for k, z in ((0, zh), (1, 1 - zh)):
+            out_ref[pl.ds(c, 1), pl.ds(z, 1)] = ref[k : k + 1].astype(F32)
 
 
 def spread(at, own, sib):
-    block = pl.BlockSpec((1, 1440, 128), lambda i, at: (i, 0, 0))
+    block = pl.BlockSpec((2, 1, 720, 128), lambda i, at: (0, i, 0, 0))
     return pl.pallas_call(
         spread_kernel,
         grid_spec=pltpu.PrefetchScalarGridSpec(
             num_scalar_prefetch=1,
             grid=(4,),
             in_specs=[block, block],
-            out_specs=pl.BlockSpec((2, 1440, 128), lambda i, at: (0, 0, (at[3] + i) & 3)),
+            out_specs=pl.BlockSpec((2, 2, 720, 128), lambda i, at: (0, 0, 0, (at[3] + i) & 3)),
         ),
-        out_shape=jax.ShapeDtypeStruct((2, 1440, 512), F32),
+        out_shape=jax.ShapeDtypeStruct((2, 2, 720, 512), F32),
         compiler_params=pltpu.CompilerParams(vmem_limit_bytes=16 << 20),
         cost_estimate=pl.CostEstimate(flops=0, bytes_accessed=9_000_000, transcendentals=0),
         name="spread",
@@ -329,7 +330,6 @@
 
 def local(tokens, expert_ids, gate_raw, overflow_shift, limits, gate_w, up_w, down_w, context, out_grad):
     at = jnp.stack([lax.axis_index(a) for a in ("core", "y", "zl", "x", "zh")]).astype(jnp.int32)
-    zh = lax.axis_index("zh")
     core_swap, zl_swap, zh_swap = shift("core", 1, 2), shift("zl", 1, 2), shift("zh", 1, 2)
     over = ("zl", "x", "zh")
 
@@ -339,13 +339,13 @@
     og_other = zl_swap(og)
     sibling = core_swap(mine)
     others = from_others(mine, "y")
-    near = after(near_rows(at, mine, sibling), og_other, others[0], others[2]).reshape(16, 24, 2880)
+    near = near_rows(at, mine, sibling).reshape(16, 24, 2880)
     near = lax.all_to_all(near, over, split_axis=0, concat_axis=0, tiled=True)
     blocks = []
     for block in others:
         blocks += [block, core_swap(block)]
     pair = jnp.stack([og, og_other])
-    far = after(far_rows(at, blocks), pair, near).reshape(16, 72, 2880)
+    far = after(far_rows(at, blocks), og_other, near).reshape(16, 72, 2880)
     far = lax.all_to_all(far, over, split_axis=0, concat_axis=0, tiled=True)
     far = far.reshape(16, 3, 24, 2880)
 
@@ -354,24 +354,22 @@
     pairs = [after(pair, out)] + from_others(pair, "y")
     grads = local_grad(at, pairs, context)
     part = grads[0].astype(F32) + core_swap(grads[1]).astype(F32)
-    terms = [shift("x", o, 4)(part[o].astype(BF)) for o in (1, 2, 3)]
-    out, *weights = ffn_part(at, 1, far, *hbm_weights, out)
+    part = part[0] + zh_swap(part[1].astype(BF)).astype(F32)
+    sends = [part[o].astype(BF) for o in (1, 2, 3)]
+    terms = [shift("x", o, 4)(block) for o, block in zip((1, 2, 3), sends)]
+    out, *weights = ffn_part(at, 1, after(far, *sends), *hbm_weights, out)
     terms = lax.optimization_barrier((*terms, out))[:3]
-    total = part[0] + terms[0].astype(F32) + terms[1].astype(F32) + terms[2].astype(F32)
-    rows = total.reshape(2, 720, 128)
-    kept = lax.dynamic_index_in_dim(rows, zh, 0, keepdims=False)
-    gone = lax.dynamic_index_in_dim(rows, 1 - zh, 0, keepdims=False).astype(BF)
-    came = zh_swap(gone)
-    (out,) = ffn_part(at, 2, far, *weights, after(out, gone))
-    total = (kept + after(came, out).astype(F32)).astype(BF)
-    back = zh_swap(total)
-    (out,) = ffn_part(at, 3, far, *weights, after(out, total))
-    back = after(back, out)
-    block = jnp.concatenate([jnp.where(zh == 0, total, back), jnp.where(zh == 0, back, total)])
-    full = jnp.stack([block] + from_others(block, "x"))
+    final = (part[0] + terms[0].astype(F32) + terms[1].astype(F32) + terms[2].astype(F32)).astype(BF)
+    blocks = from_others(final, "x")
+    (out,) = ffn_part(at, 2, far, *weights, after(out, final))
+    blocks = lax.optimization_barrier((*blocks, out))[:3]
+    half = jnp.stack([final, *blocks])
+    opposite = zh_swap(half)
+    full = jnp.stack([half, opposite])
+    (out,) = ffn_part(at, 3, far, *weights, after(out, half))
     grad = spread(at, full, core_swap(full)).reshape(2880, 512)
 
-    out = after(out, block).reshape(64, 24, 2880)
+    out = after(out, opposite).reshape(64, 24, 2880)
     out = lax.all_to_all(out, over + ("y",), split_axis=0, concat_axis=0, tiled=True)
     own, sib = combine(at, out.reshape(2, 768, 2880), mine[2880:], sibling[2880:], grad)
     mixed = (own + core_swap(sib).astype(F32)).astype(BF)

time: 398 us -> 406 us (1.020); the launches traced: 397 us -> 398 us
  starting transfers between devices: 47.9 us -> 60.4 us
  local copies, waits for them, and re-layouts: 11.1 us -> 4.95 us
  other arithmetic: 8.18 us -> 2.74 us
    ppermute x9, waiting for transfers between devices: 218 us -> 77.2 us  [from_others(): return [shift(axis, -o, 4)(block) for o in (1, 2, 3)]]
    all_to_all x1, waiting for transfers between devices: 0.01 us -> 119 us  [local(): lax.all_to_all(out, over + ('y',), split_axis=0, concat_axis=0, tiled=True)]
    ppermute x5, waiting for transfers between devices: 2.03 us -> 43.7 us  [the longest x1 36.6 us: local(): part = part[0] + zh_swap(part[1].astype(BF)).astype(F32)]
    all_to_all x1, waiting for transfers between devices: 10.6 us -> 0.01 us  [local(): far = lax.all_to_all(far, over, split_axis=0, concat_axis=0, tiled=True)]
    all_to_all x1, waiting for transfers between devices: 6.07 us -> 0.01 us  [local(): near = lax.all_to_all(near, over, split_axis=0, concat_axis=0, tiled=True)]
    ppermute x9, starting transfers between devices: 7.52 us -> 13.2 us  [from_others(): return [shift(axis, -o, 4)(block) for o in (1, 2, 3)]]
    unnamed x28 -> x22, local copies, waits for them, and re-layouts: 8.27 us -> 3.19 us
    ppermute x1, starting transfers between devices: 0.46 us -> 5.36 us  [local(): mixed = (own + core_swap(sib).astype(F32)).astype(BF)]
  transfers between devices with their start and end apart: 25 -> 25, of which waited for: 17 -> 15; matrix products, arithmetic and copies ran while one was open for 2% -> 1% of each run, Pallas kernels for 16% -> 15%
where the time goes in v7:
time: 406 us; the launch traced here: 398 us
  waiting for transfers between devices  260 us (64%)
  Pallas kernels  69.8 us (17%)
  starting transfers between devices  60.4 us (15%)
  local copies, waits for them, and re-layouts  4.95 us (1%)
    all_to_all x1, waiting for transfers between devices, local(): lax.all_to_all(out, over + ('y',), split_axis=0, concat_axis=0, tiled=True)  119 us
    ppermute x9, waiting for transfers between devices, from_others(): return [shift(axis, -o, 4)(block) for o in (1, 2, 3)]  77.2 us
    pallas_call x4, Pallas kernels, ffn_part(): pl.pallas_call(kernel, grid_spec=pltpu.PrefetchScalarGridSpec(num_scalar_...  45.1 us
    ppermute x1, waiting for transfers between devices, local(): part = part[0] + zh_swap(part[1].astype(BF)).astype(F32)  36.6 us
    ppermute x9, starting transfers between devices, from_others(): return [shift(axis, -o, 4)(block) for o in (1, 2, 3)]  13.2 us
    ppermute x1, waiting for transfers between devices, local(): og_other = zl_swap(og)  10.2 us
    all_to_all x1, starting transfers between devices, local(): lax.all_to_all(out, over + ('y',), split_axis=0, concat_axis=0, tiled=True)  8.29 us
  transfers between devices with their start and end apart: 25, of which 15 were waited for; matrix products, arithmetic and copies ran while one was open for 1% of the time, Pallas kernels for 15%

profile of v7, /device:TPU:5, one launch (start us, length us, event | category | flops | bytes accessed | tf_op | source)
XLA Modules:
  0.0 398.2 jit_solution(11154172524322659817)
XLA Ops:
  10.0 7.9 %all-to-all-start = ((bf16[16,24,2880]{2,1,0:T(8,128)(2,1)}), bf16[16,24,2880]{2,1,0:T(8,128)(2,1)}, u32[]{:S(2)}, u32[]{:S(2)}) async-start(bf16[16,24,2880]{2,1,0:T(8,128)(2,1)} %bitcast.10), calls=%async_computation | async-start | bytes 4521984 | tf_op jit(solution)/shard_map/all_to_all | solution.py:343
  19.2 2.6 collective-permute-start.2
  22.9 13.6 %collective-permute-done.4.refs_4_ = bf16[2896,128]{1,0:T(8,128)(2,1)S(1)} collective-permute-done((bf16[2896,128]{1,0:T(8,128)(2,1)S(1)}, bf16[2896,128]{1,0:T(8,128)(2,1)S(1)}, u32[]{:S(2)}, u32[]{:S(2)}) %collective-permute-start.4) | collective-permute-done | bytes 741408 | tf_op jit(solution)/shard_map/ppermute | solution.py:324
  38.4 15.1 %collective-permute-done.2.refs_2_ = bf16[2896,128]{1,0:T(8,128)(2,1)S(1)} collective-permute-done((bf16[2896,128]{1,0:T(8,128)(2,1)S(1)}, bf16[2896,128]{1,0:T(8,128)(2,1)S(1)}, u32[]{:S(2)}, u32[]{:S(2)}) %collective-permute-start.2) | collective-permute-done | bytes 741408 | tf_op jit(solution)/shard_map/ppermute | solution.py:324
  58.1 4.6 %far_rows.1 = bf16[2,8,3,24,2880]{4,3,2,1,0:T(8,128)(2,1)} custom-call(s32[5]{0:T(128)S(1)} %stack.56.at_ref, bf16[2896,128]{1,0:T(8,128)(2,1)S(1)} %collective-permute-done.refs_0_, bf16[2896,128]{1,0:T(8,128)(2,1)S(1)} %collective-permute-done.1.refs_1_, bf16[2896,128]{1,0:T(8,128)(2,1)S(1)} %collective-permute-done.2.refs_2_, ...), custom_call_target="tpu_custom_call" | custom-call | flops 849346560 | bytes 11000000 | tf_op jit(solution)/shard_map/far_rows/pallas_call | solution.py:128
  62.7 10.2 %collective-permute-done.6 = bf16[2880,128]{1,0:T(8,128)(2,1)S(1)} collective-permute-done((bf16[2880,128]{1,0:T(8,128)(2,1)S(1)}, bf16[2880,128]{1,0:T(8,128)(2,1)S(1)}, u32[]{:S(2)}, u32[]{:S(2)}) %collective-permute-start.6) | collective-permute-done | bytes 737312 | tf_op jit(solution)/shard_map/ppermute | solution.py:339
  73.0 6.7 %all-to-all-start.1 = ((bf16[16,72,2880]{2,1,0:T(8,128)(2,1)}), bf16[16,72,2880]{2,1,0:T(8,128)(2,1)}, u32[]{:S(2)}, u32[]{:S(2)}) async-start(bf16[16,72,2880]{2,1,0:T(8,128)(2,1)} %bitcast.69), calls=%async_computation.1 | async-start | bytes 13565952 | tf_op jit(solution)/shard_map/all_to_all | solution.py:349
  84.6 13.3 %ffn_part0.1.into_ref = bf16[16,4,24,2880]{3,2,1,0:T(8,128)(2,1)} custom-call(s32[5]{0:T(128)} %copy-done.3, bf16[384,2880]{1,0:T(8,128)(2,1)} %bitcast.15.x_ref, bf16[1,2880,768]{2,1,0:T(8,128)(2,1)} %g_hbm.3, bf16[1,2880,768]{2,1,0:T(8,128)(2,1)} %u_hbm.3, bf16[2880,768]{1,0:T(8,128)(2,1)} %bitcast.72), custom_call_target="tpu_custom_call" | custom-call | flops 5096079360 | bytes 18000000 | tf_op jit(solution)/shard_map/ffn_part0/pallas_call | solution.py:191
  97.9 15.2 %collective-permute-done.10.p3_ref = bf16[2,2880,128]{2,1,0:T(8,128)(2,1)S(1)} collective-permute-done((bf16[2,2880,128]{2,1,0:T(8,128)(2,1)S(1)}, bf16[2,2880,128]{2,1,0:T(8,128)(2,1)S(1)}, u32[]{:S(2)}, u32[]{:S(2)}) %collective-permute-start.10) | collective-permute-done | bytes 1474592 | tf_op jit(solution)/shard_map/ppermute | solution.py:324
  113.1 32.8 %collective-permute-done.9.p2_ref = bf16[2,2880,128]{2,1,0:T(8,128)(2,1)} collective-permute-done((bf16[2,2880,128]{2,1,0:T(8,128)(2,1)S(1)}, bf16[2,2880,128]{2,1,0:T(8,128)(2,1)}, u32[]{:S(2)}, u32[]{:S(2)}) %collective-permute-start.9) | collective-permute-done | bytes 1474592 | tf_op jit(solution)/shard_map/ppermute | solution.py:324
  146.4 5.9 %local_grad.1 = bf16[2,2,4,720,128]{4,3,2,1,0:T(8,128)(2,1)S(1)} custom-call(s32[5]{0:T(128)S(1)} %copy-done.4, bf16[2,2880,128]{2,1,0:T(8,128)(2,1)S(1)} %pad_maximum_fusion.p0_ref, bf16[2,2880,128]{2,1,0:T(8,128)(2,1)} %collective-permute-done.8.p1_ref, bf16[2,2880,128]{2,1,0:T(8,128)(2,1)} %collective-permute-done.9.p2_ref, ...), custom_call_target="tpu_custom_call" | custom-call | flops 3019898880 | bytes 10000000 | tf_op jit(solution)/shard_map/local_grad/pallas_call | solution.py:279
  154.3 2.9 collective-permute-done.11
  157.6 2.8 collective-permute-start.12
  160.3 36.6 %collective-permute-done.12 = bf16[4,720,128]{2,1,0:T(8,128)(2,1)S(1)} collective-permute-done((bf16[4,720,128]{2,1,0:T(8,128)(2,1)S(1)}, bf16[4,720,128]{2,1,0:T(8,128)(2,1)S(1)}, u32[]{:S(2)}, u32[]{:S(2)}) %collective-permute-start.12) | collective-permute-done | bytes 737312 | tf_op jit(solution)/shard_map/ppermute | solution.py:357
  200.9 13.3 %ffn_part1.1 = (bf16[16,4,24,2880]{3,2,1,0:T(8,128)(2,1)}, bf16[2880,768]{1,0:T(8,128)(2,1)S(1)}, bf16[2880,768]{1,0:T(8,128)(2,1)S(1)}, bf16[2880,768]{1,0:T(8,128)(2,1)S(1)}) custom-call(s32[5]{0:T(128)} %copy-done.3, bf16[16,3,24,2880]{3,2,1,0:T(8,128)(2,1)} %bitcast.12.x_ref, bf16[1,2880,768]{2,1,0:T(8,128)(2,1)} %g_hbm.3, ...), custom_call_target="tpu_custom_call", output_to_operand_aliasing={{0}: (5, {})} | custom-call | flops 5096079360 | bytes 18000000 | tf_op jit(solution)/shard_map/ffn_part1/pallas_call | solution.py:191
  217.7 9.3 %ffn_part2.1.into_ref = bf16[16,4,24,2880]{3,2,1,0:T(8,128)(2,1)} custom-call(s32[5]{0:T(128)S(1)} %copy-done.5, bf16[16,3,24,2880]{3,2,1,0:T(8,128)(2,1)} %bitcast.12.x_ref, bf16[2880,768]{1,0:T(8,128)(2,1)S(1)} %get-tuple-element.23.g_ref, bf16[2880,768]{1,0:T(8,128)(2,1)S(1)} %get-tuple-element.24.u_ref, ...), custom_call_target="tpu_custom_call", output_to_operand_aliasing={{}: (5, {})} | custom-call | flops 5096079360 | bytes 18000000 | tf_op jit(solution)/shard_map/ffn_part2/pallas_call | solution.py:191
  227.7 9.2 %ffn_part3.1 = bf16[16,4,24,2880]{3,2,1,0:T(8,128)(2,1)} custom-call(s32[5]{0:T(128)S(1)} %copy-done.5, bf16[16,3,24,2880]{3,2,1,0:T(8,128)(2,1)} %bitcast.12.x_ref, bf16[2880,768]{1,0:T(8,128)(2,1)S(1)} %get-tuple-element.23.g_ref, bf16[2880,768]{1,0:T(8,128)(2,1)S(1)} %get-tuple-element.24.u_ref, ...), custom_call_target="tpu_custom_call", output_to_operand_aliasing={{}: (5, {})} | custom-call | flops 5096079360 | bytes 18000000 | tf_op jit(solution)/shard_map/ffn_part3/pallas_call | solution.py:191
  236.9 7.1 %collective-permute-done.19 = bf16[4,720,128]{2,1,0:T(8,128)(2,1)S(1)} collective-permute-done((bf16[4,720,128]{2,1,0:T(8,128)(2,1)S(1)}, bf16[4,720,128]{2,1,0:T(8,128)(2,1)S(1)}, u32[]{:S(2)}, u32[]{:S(2)}) %collective-permute-start.19) | collective-permute-done | bytes 737312 | tf_op jit(solution)/shard_map/ppermute | solution.py:367
  244.0 8.3 %all-to-all-start.2 = ((bf16[64,24,2880]{2,1,0:T(8,128)(2,1)}), bf16[64,24,2880]{2,1,0:T(8,128)(2,1)}, u32[]{:S(2)}, u32[]{:S(2)}) async-start(bf16[64,24,2880]{2,1,0:T(8,128)(2,1)} %bitcast.68), calls=%async_computation.2 | async-start | bytes 18087936 | tf_op jit(solution)/shard_map/all_to_all | solution.py:373
  252.4 4.5 %collective-permute-start.20 = (bf16[2,4,720,128]{3,2,1,0:T(8,128)(2,1)S(1)}, bf16[2,4,720,128]{3,2,1,0:T(8,128)(2,1)S(1)}, u32[]{:S(2)}, u32[]{:S(2)}) collective-permute-start(bf16[2,4,720,128]{3,2,1,0:T(8,128)(2,1)S(1)} %pad_maximum_fusion.1.own_ref), channel_id=1, source_target_pairs={{0,8},{8,0},{1,9},{9,1},{2,10},{10,2},{3,11},{11,3},{4,12},{12,4},... | collective-permute-start | bytes 4423688 | tf_op jit(solution)/shard_map/ppermute | solution.py:370
  259.8 3.6 spread.1
  263.5 118.8 %all-to-all-done.2 = bf16[64,24,2880]{2,1,0:T(8,128)(2,1)} async-done(((bf16[64,24,2880]{2,1,0:T(8,128)(2,1)}), bf16[64,24,2880]{2,1,0:T(8,128)(2,1)}, u32[]{:S(2)}, u32[]{:S(2)}) %all-to-all-start.2) | async-done | bytes 8847392 | tf_op jit(solution)/shard_map/all_to_all | solution.py:373
  382.2 7.7 %combine.1 = (f32[2880,128]{1,0:T(8,128)S(1)}, bf16[2880,128]{1,0:T(8,128)(2,1)S(1)}) custom-call(s32[5]{0:T(128)S(1)} %copy-done.5, bf16[2,768,2880]{2,1,0:T(8,128)(2,1)} %bitcast.31.y_ref, bf16[16,128]{1,0:T(8,128)(2,1)S(1)} %slice.52.own_tail_ref, bf16[16,128]{1,0:T(8,128)(2,1)S(1)} %slice.53.sib_tail_ref, f32[2880,512]{1,0:T(8,128)} %bitcast.70), custom_call_target="tpu_custom_call" | custom-call | flops 2264924160 | bytes 12000000 | tf_op jit(solution)/shard_map/combine/pallas_call | solution.py:245
  389.9 5.4 %collective-permute-start.21 = (bf16[2880,128]{1,0:T(8,128)(2,1)S(1)}, bf16[2880,128]{1,0:T(8,128)(2,1)S(1)}, u32[]{:S(2)}, u32[]{:S(2)}) collective-permute-start(bf16[2880,128]{1,0:T(8,128)(2,1)S(1)} %get-tuple-element.37), channel_id=1, source_target_pairs={{0,8},{8,0},{1,9},{9,1},{2,10},{10,2},{3,11},{11,3},{4,12},{12,4},... | collective-permute-start | bytes 2211848 | tf_op jit(solution)/shard_map/ppermute | solution.py:375
  (73 shorter events, 40.1 us)
Async XLA Ops:
  10.0 62.9 %all-to-all-start = ((bf16[16,24,2880]{2,1,0:T(8,128)(2,1)}), bf16[16,24,2880]{2,1,0:T(8,128)(2,1)}, u32[]{:S(2)}, u32[]{:S(2)}) async-start(bf16[16,24,2880]{2,1,0:T(8,128)(2,1)} %bitcast.10), calls=%async_computation | async-start | bytes 4521984 | tf_op jit(solution)/shard_map/all_to_all | solution.py:343
  17.9 18.6 %collective-permute-start.4 = (bf16[2896,128]{1,0:T(8,128)(2,1)S(1)}, bf16[2896,128]{1,0:T(8,128)(2,1)S(1)}, u32[]{:S(2)}, u32[]{:S(2)}) collective-permute-start(bf16[2896,128]{1,0:T(8,128)(2,1)S(1)} %place.1.own_ref), channel_id=1, source_target_pairs={{0,2},{2,4},{4,6},{6,0},{1,3},{3,5},{5,7},{7,1},{8,10},{10,12},{12... | collective-permute-start | bytes 2224136 | tf_op jit(solution)/shard_map/ppermute | solution.py:324
  19.2 34.3 %collective-permute-start.2 = (bf16[2896,128]{1,0:T(8,128)(2,1)S(1)}, bf16[2896,128]{1,0:T(8,128)(2,1)S(1)}, u32[]{:S(2)}, u32[]{:S(2)}) collective-permute-start(bf16[2896,128]{1,0:T(8,128)(2,1)S(1)} %place.1.own_ref), channel_id=1, source_target_pairs={{0,4},{2,6},{4,0},{6,2},{1,5},{3,7},{5,1},{7,3},{8,12},{10,14},{12... | collective-permute-start | bytes 2224136 | tf_op jit(solution)/shard_map/ppermute | solution.py:324
  21.8 33.4 %collective-permute-start = (bf16[2896,128]{1,0:T(8,128)(2,1)S(1)}, bf16[2896,128]{1,0:T(8,128)(2,1)S(1)}, u32[]{:S(2)}, u32[]{:S(2)}) collective-permute-start(bf16[2896,128]{1,0:T(8,128)(2,1)S(1)} %place.1.own_ref), channel_id=1, source_target_pairs={{0,6},{2,0},{4,2},{6,4},{1,7},{3,1},{5,3},{7,5},{8,14},{10,8},{12,... | collective-permute-start | bytes 2224136 | tf_op jit(solution)/shard_map/ppermute | solution.py:324
  36.5 20.0 %collective-permute-start.5 = (bf16[2896,128]{1,0:T(8,128)(2,1)S(1)}, bf16[2896,128]{1,0:T(8,128)(2,1)S(1)}, u32[]{:S(2)}, u32[]{:S(2)}) collective-permute-start(bf16[2896,128]{1,0:T(8,128)(2,1)S(1)} %collective-permute-done.4.refs_4_), channel_id=1, source_target_pairs={{0,8},{8,0},{1,9},{9,1},{2,10},{10,2},{3,11},{11,3},{4,12},{12,4},... | collective-permute-start | bytes 2224136 | tf_op jit(solution)/shard_map/ppermute | solution.py:346
  53.5 3.6 collective-permute-start.3
  55.2 2.9 collective-permute-start.1
  55.2 17.7 %collective-permute-start.6 = (bf16[2880,128]{1,0:T(8,128)(2,1)S(1)}, bf16[2880,128]{1,0:T(8,128)(2,1)S(1)}, u32[]{:S(2)}, u32[]{:S(2)}) collective-permute-start(bf16[2880,128]{1,0:T(8,128)(2,1)S(1)} %bitcast.74), channel_id=1, source_target_pairs={{0,1},{1,0},{2,3},{3,2},{4,5},{5,4},{6,7},{7,6},{8,9},{9,8},{10,11... | collective-permute-start | bytes 2211848 | tf_op jit(solution)/shard_map/ppermute | solution.py:339
  73.0 127.9 %all-to-all-start.1 = ((bf16[16,72,2880]{2,1,0:T(8,128)(2,1)}), bf16[16,72,2880]{2,1,0:T(8,128)(2,1)}, u32[]{:S(2)}, u32[]{:S(2)}) async-start(bf16[16,72,2880]{2,1,0:T(8,128)(2,1)} %bitcast.69), calls=%async_computation.1 | async-start | bytes 13565952 | tf_op jit(solution)/shard_map/all_to_all | solution.py:349
  79.8 33.3 %collective-permute-start.10 = (bf16[2,2880,128]{2,1,0:T(8,128)(2,1)S(1)}, bf16[2,2880,128]{2,1,0:T(8,128)(2,1)S(1)}, u32[]{:S(2)}, u32[]{:S(2)}) collective-permute-start(bf16[2,2880,128]{2,1,0:T(8,128)(2,1)S(1)} %pad_maximum_fusion.p0_ref), channel_id=1, source_target_pairs={{0,2},{2,4},{4,6},{6,0},{1,3},{3,5},{5,7},{7,1},{8,10},{10,12},{12... | collective-permute-start | bytes 4423688 | tf_op jit(solution)/shard_map/ppermute | solution.py:324
  81.2 64.8 %collective-permute-start.9 = (bf16[2,2880,128]{2,1,0:T(8,128)(2,1)S(1)}, bf16[2,2880,128]{2,1,0:T(8,128)(2,1)}, u32[]{:S(2)}, u32[]{:S(2)}) collective-permute-start(bf16[2,2880,128]{2,1,0:T(8,128)(2,1)S(1)} %pad_maximum_fusion.p0_ref), channel_id=1, source_target_pairs={{0,4},{2,6},{4,0},{6,2},{1,5},{3,7},{5,1},{7,3},{8,12},{10,14},{12... | collective-permute-start | bytes 4423688 | tf_op jit(solution)/shard_map/ppermute | solution.py:324
  83.3 63.1 %collective-permute-start.8 = (bf16[2,2880,128]{2,1,0:T(8,128)(2,1)S(1)}, bf16[2,2880,128]{2,1,0:T(8,128)(2,1)}, u32[]{:S(2)}, u32[]{:S(2)}) collective-permute-start(bf16[2,2880,128]{2,1,0:T(8,128)(2,1)S(1)} %pad_maximum_fusion.p0_ref), channel_id=1, source_target_pairs={{0,6},{2,0},{4,2},{6,4},{1,7},{3,1},{5,3},{7,5},{8,14},{10,8},{12,... | collective-permute-start | bytes 4423688 | tf_op jit(solution)/shard_map/ppermute | solution.py:324
  152.4 4.8 %collective-permute-start.11 = (bf16[2,4,720,128]{3,2,1,0:T(8,128)(2,1)S(1)}, bf16[2,4,720,128]{3,2,1,0:T(8,128)(2,1)S(1)}, u32[]{:S(2)}, u32[]{:S(2)}) collective-permute-start(bf16[2,4,720,128]{3,2,1,0:T(8,128)(2,1)S(1)} %slice_bitcast_fusion.1), channel_id=1, source_target_pairs={{0,8},{8,0},{1,9},{9,1},{2,10},{10,2},{3,11},{11,3},{4,12},{12,4},... | collective-permute-start | bytes 4423688 | tf_op jit(solution)/shard_map/ppermute | solution.py:356
  157.6 39.4 %collective-permute-start.12 = (bf16[4,720,128]{2,1,0:T(8,128)(2,1)S(1)}, bf16[4,720,128]{2,1,0:T(8,128)(2,1)S(1)}, u32[]{:S(2)}, u32[]{:S(2)}) collective-permute-start(bf16[4,720,128]{2,1,0:T(8,128)(2,1)S(1)} %fusion.2), channel_id=1, source_target_pairs={{0,16},{16,0},{1,17},{17,1},{2,18},{18,2},{3,19},{19,3},{4,20},{20... | collective-permute-start | bytes 2211848 | tf_op jit(solution)/shard_map/ppermute | solution.py:357
  197.3 17.0 %collective-permute-start.15 = (bf16[720,128]{1,0:T(8,128)(2,1)S(1)}, bf16[720,128]{1,0:T(8,128)(2,1)S(1)}, u32[]{:S(2)}, u32[]{:S(2)}) collective-permute-start(bf16[720,128]{1,0:T(8,128)(2,1)S(1)} %get-tuple-element.42), channel_id=1, source_target_pairs={{0,96},{32,0},{64,32},{96,64},{1,97},{33,1},{65,33},{97,65},{2,98}... | collective-permute-start | bytes 552968 | tf_op jit(solution)/shard_map/ppermute | solution.py:359
  199.0 15.2 %collective-permute-start.14 = (bf16[720,128]{1,0:T(8,128)(2,1)S(1)}, bf16[720,128]{1,0:T(8,128)(2,1)S(1)}, u32[]{:S(2)}, u32[]{:S(2)}) collective-permute-start(bf16[720,128]{1,0:T(8,128)(2,1)S(1)} %get-tuple-element.43), channel_id=1, source_target_pairs={{0,64},{32,96},{64,0},{96,32},{1,65},{33,97},{65,1},{97,33},{2,66}... | collective-permute-start | bytes 552968 | tf_op jit(solution)/shard_map/ppermute | solution.py:359
  199.5 14.7 %collective-permute-start.13 = (bf16[720,128]{1,0:T(8,128)(2,1)S(1)}, bf16[720,128]{1,0:T(8,128)(2,1)S(1)}, u32[]{:S(2)}, u32[]{:S(2)}) collective-permute-start(bf16[720,128]{1,0:T(8,128)(2,1)S(1)} %get-tuple-element.44), channel_id=1, source_target_pairs={{0,32},{32,64},{64,96},{96,0},{1,33},{33,65},{65,97},{97,1},{2,34}... | collective-permute-start | bytes 552968 | tf_op jit(solution)/shard_map/ppermute | solution.py:359
  214.3 12.6 %collective-permute-start.18 = (bf16[720,128]{1,0:T(8,128)(2,1)S(1)}, bf16[720,128]{1,0:T(8,128)(2,1)S(1)}, u32[]{:S(2)}, u32[]{:S(2)}) collective-permute-start(bf16[720,128]{1,0:T(8,128)(2,1)S(1)} %fusion.6), channel_id=1, source_target_pairs={{0,32},{32,64},{64,96},{96,0},{1,33},{33,65},{65,97},{97,1},{2,34}... | collective-permute-start | bytes 552968 | tf_op jit(solution)/shard_map/ppermute | solution.py:324
  216.4 10.5 %collective-permute-start.17 = (bf16[720,128]{1,0:T(8,128)(2,1)S(1)}, bf16[720,128]{1,0:T(8,128)(2,1)S(1)}, u32[]{:S(2)}, u32[]{:S(2)}) collective-permute-start(bf16[720,128]{1,0:T(8,128)(2,1)S(1)} %fusion.6), channel_id=1, source_target_pairs={{0,64},{32,96},{64,0},{96,32},{1,65},{33,97},{65,1},{97,33},{2,66}... | collective-permute-start | bytes 552968 | tf_op jit(solution)/shard_map/ppermute | solution.py:324
  216.4 10.5 %collective-permute-start.16 = (bf16[720,128]{1,0:T(8,128)(2,1)S(1)}, bf16[720,128]{1,0:T(8,128)(2,1)S(1)}, u32[]{:S(2)}, u32[]{:S(2)}) collective-permute-start(bf16[720,128]{1,0:T(8,128)(2,1)S(1)} %fusion.6), channel_id=1, source_target_pairs={{0,96},{32,0},{64,32},{96,64},{1,97},{33,1},{65,33},{97,65},{2,98}... | collective-permute-start | bytes 552968 | tf_op jit(solution)/shard_map/ppermute | solution.py:324
  227.1 16.9 %collective-permute-start.19 = (bf16[4,720,128]{2,1,0:T(8,128)(2,1)S(1)}, bf16[4,720,128]{2,1,0:T(8,128)(2,1)S(1)}, u32[]{:S(2)}, u32[]{:S(2)}) collective-permute-start(bf16[4,720,128]{2,1,0:T(8,128)(2,1)S(1)} %get-tuple-element.41), channel_id=1, source_target_pairs={{0,16},{16,0},{1,17},{17,1},{2,18},{18,2},{3,19},{19,3},{4,20},{20... | collective-permute-start | bytes 2211848 | tf_op jit(solution)/shard_map/ppermute | solution.py:367
  244.0 138.2 %all-to-all-start.2 = ((bf16[64,24,2880]{2,1,0:T(8,128)(2,1)}), bf16[64,24,2880]{2,1,0:T(8,128)(2,1)}, u32[]{:S(2)}, u32[]{:S(2)}) async-start(bf16[64,24,2880]{2,1,0:T(8,128)(2,1)} %bitcast.68), calls=%async_computation.2 | async-start | bytes 18087936 | tf_op jit(solution)/shard_map/all_to_all | solution.py:373
  252.4 7.4 %collective-permute-start.20 = (bf16[2,4,720,128]{3,2,1,0:T(8,128)(2,1)S(1)}, bf16[2,4,720,128]{3,2,1,0:T(8,128)(2,1)S(1)}, u32[]{:S(2)}, u32[]{:S(2)}) collective-permute-start(bf16[2,4,720,128]{3,2,1,0:T(8,128)(2,1)S(1)} %pad_maximum_fusion.1.own_ref), channel_id=1, source_target_pairs={{0,8},{8,0},{1,9},{9,1},{2,10},{10,2},{3,11},{11,3},{4,12},{12,4},... | collective-permute-start | bytes 4423688 | tf_op jit(solution)/shard_map/ppermute | solution.py:370
  389.9 7.2 %collective-permute-start.21 = (bf16[2880,128]{1,0:T(8,128)(2,1)S(1)}, bf16[2880,128]{1,0:T(8,128)(2,1)S(1)}, u32[]{:S(2)}, u32[]{:S(2)}) collective-permute-start(bf16[2880,128]{1,0:T(8,128)(2,1)S(1)} %get-tuple-element.37), channel_id=1, source_target_pairs={{0,8},{8,0},{1,9},{9,1},{2,10},{10,2},{3,11},{11,3},{4,12},{12,4},... | collective-permute-start | bytes 2211848 | tf_op jit(solution)/shard_map/ppermute | solution.py:375
  (12 other events, 263.4 us)

commit v8 on v3

--- a/solution.py
+++ b/solution.py
@@ -181,26 +181,26 @@
 
 def ffn_part(at, o, x, g, u, d_t, into=None):
     hbm, vm = pl.BlockSpec(memory_space=pltpu.HBM), pl.BlockSpec(memory_space=pltpu.VMEM)
-    kernel = (near_ffn_kernel, first_kernel, part_kernel, part_kernel)[o]
+    kernel = (near_ffn_kernel, first_kernel, part_kernel)[o]
     held = [pltpu.VMEM((2880, 768), BF)] * 3
     sems = [pltpu.SemaphoreType.DMA((3,))]
     if o == 0:
         x_spec = pl.BlockSpec((384, 2880), lambda i, at: (0, 0))
     else:
-        x_spec = pl.BlockSpec((16, 1, 24, 2880), lambda i, at: (0, o - 1, 0, 0))
+        x_spec = pl.BlockSpec((16, 1, 24, 2880), lambda i, at: (0, o - 1 + i, 0, 0))
     return pl.pallas_call(
         kernel,
         grid_spec=pltpu.PrefetchScalarGridSpec(
             num_scalar_prefetch=1,
-            grid=(1,),
+            grid=(2 if o == 2 else 1,),
             in_specs=[x_spec] + [vm if o > 1 else hbm] * 3 + [hbm] * (o > 0),
-            out_specs=[pl.BlockSpec((16, 1, 24, 2880), lambda i, at: (0, (at[1] + o) & 3, 0, 0))]
+            out_specs=[pl.BlockSpec((16, 1, 24, 2880), lambda i, at: (0, (at[1] + o + i) & 3, 0, 0))]
             + [vm] * 3 * (o == 1),
-            scratch_shapes=(held + sems, sems, [], [])[o],
+            scratch_shapes=(held + sems, sems, [])[o],
         ),
         out_shape=[pltpu.HBM((16, 4, 24, 2880), BF)] + held * (o == 1),
         input_output_aliases={5: 0} if o else {},
-        compiler_params=pltpu.CompilerParams(vmem_limit_bytes=(60, 47, 30, 30)[o] << 20),
+        compiler_params=pltpu.CompilerParams(vmem_limit_bytes=(60, 47, 30)[o] << 20),
         cost_estimate=pl.CostEstimate(
             flops=6 * 384 * 2880 * 768, bytes_accessed=18_000_000, transcendentals=384 * 768
         ),
@@ -306,7 +306,7 @@
             num_scalar_prefetch=1,
             grid=(4,),
             in_specs=[block, block],
-            out_specs=pl.BlockSpec((2, 1440, 128), lambda i, at: (0, 0, (at[3] + i) & 3)),
+            out_specs=pl.BlockSpec((2, 1440, 128), lambda i, at: (0, 0, i)),
         ),
         out_shape=jax.ShapeDtypeStruct((2, 1440, 512), F32),
         compiler_params=pltpu.CompilerParams(vmem_limit_bytes=16 << 20),
@@ -364,14 +364,10 @@
     came = zh_swap(gone)
     (out,) = ffn_part(at, 2, far, *weights, after(out, gone))
     total = (kept + after(came, out).astype(F32)).astype(BF)
-    back = zh_swap(total)
-    (out,) = ffn_part(at, 3, far, *weights, after(out, total))
-    back = after(back, out)
-    block = jnp.concatenate([jnp.where(zh == 0, total, back), jnp.where(zh == 0, back, total)])
-    full = jnp.stack([block] + from_others(block, "x"))
+    full = lax.all_gather(after(total, out), ("x", "zh"), axis=0, tiled=True).reshape(4, 1440, 128)
     grad = spread(at, full, core_swap(full)).reshape(2880, 512)
 
-    out = after(out, block).reshape(64, 24, 2880)
+    out = after(out, total).reshape(64, 24, 2880)
     out = lax.all_to_all(out, over + ("y",), split_axis=0, concat_axis=0, tiled=True)
     own, sib = combine(at, out.reshape(2, 768, 2880), mine[2880:], sibling[2880:], grad)
     mixed = (own + core_swap(sib).astype(F32)).astype(BF)

time: 398 us -> 399 us (level)
  between operations: 0.79 us -> 14.2 us
  waiting for transfers between devices: 259 us -> 252 us
  starting transfers between devices: 47.9 us -> 42.9 us
    ppermute x9 -> x6, waiting for transfers between devices: 218 us -> 67.9 us  [from_others(): return [shift(axis, -o, 4)(block) for o in (1, 2, 3)]]
    all_gather x0 -> x1, waiting for transfers between devices: none -> 143 us  [local(): lax.all_gather(after(total, out), ('x', 'zh'), axis=0, tiled=True)]
    pallas_call x4 -> x3, Pallas kernels: 45.1 us -> 41.6 us  [ffn_part(): pl.pallas_call(kernel, grid_spec=pltpu.PrefetchScalarGridSpec(num_scalar_...]
    unnamed x28 -> x30, local copies, waits for them, and re-layouts: 8.27 us -> 9.64 us
  transfers between devices with their start and end apart: 25 -> 22, of which waited for: 17 -> 15; matrix products, arithmetic and copies ran while one was open for 2% -> 2% of each run, Pallas kernels for 16% -> 15%
where the time goes in v8:
time: 399 us; the launch traced here: 396 us
  waiting for transfers between devices  252 us (63%)
  Pallas kernels  66.2 us (17%)
  starting transfers between devices  42.9 us (11%)
  between operations  14.2 us (4%)
  local copies, waits for them, and re-layouts  12.5 us (3%)
  other arithmetic  8.58 us (2%)
    all_gather x1, waiting for transfers between devices, local(): lax.all_gather(after(total, out), ('x', 'zh'), axis=0, tiled=True)  143 us
    ppermute x6, waiting for transfers between devices, from_others(): return [shift(axis, -o, 4)(block) for o in (1, 2, 3)]  67.9 us
    pallas_call x3, Pallas kernels, ffn_part(): pl.pallas_call(kernel, grid_spec=pltpu.PrefetchScalarGridSpec(num_scalar_...  41.6 us
    ppermute x1, waiting for transfers between devices, local(): og_other = zl_swap(og)  14.1 us
    all_to_all x1, waiting for transfers between devices, local(): far = lax.all_to_all(far, over, split_axis=0, concat_axis=0, tiled=True)  10.6 us
    all_to_all x1, starting transfers between devices, local(): lax.all_to_all(out, over + ('y',), split_axis=0, concat_axis=0, tiled=True)  10.6 us
    unnamed x30, local copies, waits for them, and re-layouts  9.64 us
  transfers between devices with their start and end apart: 22, of which 15 were waited for; matrix products, arithmetic and copies ran while one was open for 2% of the time, Pallas kernels for 15%

profile of v8, /device:TPU:5, one launch (start us, length us, event | category | flops | bytes accessed | tf_op | source)
XLA Modules:
  0.0 396.4 jit_solution(18275806631819040876)
XLA Ops:
  12.1 2.7 collective-permute-start
  16.6 2.6 near_rows.1
  19.2 14.1 %collective-permute-done.6 = bf16[2880,128]{1,0:T(8,128)(2,1)} collective-permute-done((bf16[2880,128]{1,0:T(8,128)(2,1)}, bf16[2880,128]{1,0:T(8,128)(2,1)}, u32[]{:S(2)}, u32[]{:S(2)}) %collective-permute-start.6) | collective-permute-done | bytes 737312 | tf_op jit(solution)/shard_map/ppermute | solution.py:339
  33.9 7.7 %all-to-all-start = ((bf16[16,24,2880]{2,1,0:T(8,128)(2,1)}), bf16[16,24,2880]{2,1,0:T(8,128)(2,1)}, u32[]{:S(2)}, u32[]{:S(2)}) async-start(bf16[16,24,2880]{2,1,0:T(8,128)(2,1)} %bitcast.12), calls=%async_computation | async-start | bytes 4521984 | tf_op jit(solution)/shard_map/all_to_all | solution.py:343
  42.1 2.3 collective-permute-start.1
  44.4 15.2 %collective-permute-done.2.refs_2_ = bf16[2896,128]{1,0:T(8,128)(2,1)S(1)} collective-permute-done((bf16[2896,128]{1,0:T(8,128)(2,1)S(1)}, bf16[2896,128]{1,0:T(8,128)(2,1)S(1)}, u32[]{:S(2)}, u32[]{:S(2)}) %collective-permute-start.2) | collective-permute-done | bytes 741408 | tf_op jit(solution)/shard_map/ppermute | solution.py:323
  59.7 2.6 collective-permute-start.3
  65.1 4.6 %far_rows.1 = bf16[2,8,3,24,2880]{4,3,2,1,0:T(8,128)(2,1)} custom-call(s32[5]{0:T(128)S(1)} %stack.32.at_ref, bf16[2896,128]{1,0:T(8,128)(2,1)S(1)} %collective-permute-done.refs_0_, bf16[2896,128]{1,0:T(8,128)(2,1)S(1)} %collective-permute-done.1.refs_1_, bf16[2896,128]{1,0:T(8,128)(2,1)S(1)} %collective-permute-done.2.refs_2_, ...), custom_call_target="tpu_custom_call" | custom-call | flops 849346560 | bytes 11000000 | tf_op jit(solution)/shard_map/far_rows/pallas_call | solution.py:128
  69.8 6.1 %all-to-all-done = bf16[16,24,2880]{2,1,0:T(8,128)(2,1)} async-done(((bf16[16,24,2880]{2,1,0:T(8,128)(2,1)}), bf16[16,24,2880]{2,1,0:T(8,128)(2,1)}, u32[]{:S(2)}, u32[]{:S(2)}) %all-to-all-start) | async-done | bytes 2211872 | tf_op jit(solution)/shard_map/all_to_all | solution.py:343
  75.9 4.9 %all-to-all-start.1 = ((bf16[16,72,2880]{2,1,0:T(8,128)(2,1)}), bf16[16,72,2880]{2,1,0:T(8,128)(2,1)}, u32[]{:S(2)}, u32[]{:S(2)}) async-start(bf16[16,72,2880]{2,1,0:T(8,128)(2,1)} %bitcast.65), calls=%async_computation.1 | async-start | bytes 13565952 | tf_op jit(solution)/shard_map/all_to_all | solution.py:349
  82.5 13.3 %ffn_part0.1.into_ref = bf16[16,4,24,2880]{3,2,1,0:T(8,128)(2,1)} custom-call(s32[5]{0:T(128)} %copy-done.6, bf16[384,2880]{1,0:T(8,128)(2,1)} %bitcast.17.x_ref, bf16[1,2880,768]{2,1,0:T(8,128)(2,1)} %g_hbm.3, bf16[1,2880,768]{2,1,0:T(8,128)(2,1)} %u_hbm.3, bf16[2880,768]{1,0:T(8,128)(2,1)} %bitcast.68), custom_call_target="tpu_custom_call" | custom-call | flops 5096079360 | bytes 18000000 | tf_op jit(solution)/shard_map/ffn_part0/pallas_call | solution.py:191
  95.8 15.9 %collective-permute-done.8.p1_ref = bf16[2,2880,128]{2,1,0:T(8,128)(2,1)S(1)} collective-permute-done((bf16[2,2880,128]{2,1,0:T(8,128)(2,1)S(1)}, bf16[2,2880,128]{2,1,0:T(8,128)(2,1)S(1)}, u32[]{:S(2)}, u32[]{:S(2)}) %collective-permute-start.8) | collective-permute-done | bytes 1474592 | tf_op jit(solution)/shard_map/ppermute | solution.py:323
  114.1 34.9 %collective-permute-done.10.p3_ref = bf16[2,2880,128]{2,1,0:T(8,128)(2,1)} collective-permute-done((bf16[2,2880,128]{2,1,0:T(8,128)(2,1)S(1)}, bf16[2,2880,128]{2,1,0:T(8,128)(2,1)}, u32[]{:S(2)}, u32[]{:S(2)}) %collective-permute-start.10) | collective-permute-done | bytes 1474592 | tf_op jit(solution)/shard_map/ppermute | solution.py:323
  153.0 5.9 %local_grad.1 = bf16[2,4,1440,128]{3,2,1,0:T(8,128)(2,1)S(1)} custom-call(s32[5]{0:T(128)S(1)} %copy-done.7, bf16[2,2880,128]{2,1,0:T(8,128)(2,1)S(1)} %copy-done.3, bf16[2,2880,128]{2,1,0:T(8,128)(2,1)S(1)} %copy-done.13, bf16[2,2880,128]{2,1,0:T(8,128)(2,1)} %collective-permute-done.9.p2_ref, bf16[2,2880,128]{2,1,0:T(8,128)(2,1)} %collective-permute-done.10.p3_ref, ...), custom_call_target="tpu_custom_call" | custom-call | flops 3019898880 | bytes 10000000 | tf_op jit(solution)/shard_map/local_grad/pallas_call | solution.py:279
  160.7 3.2 collective-permute-done.11
  164.0 3.4 fusion.6
  169.8 10.6 %all-to-all-done.1 = bf16[16,72,2880]{2,1,0:T(8,128)(2,1)} async-done(((bf16[16,72,2880]{2,1,0:T(8,128)(2,1)}), bf16[16,72,2880]{2,1,0:T(8,128)(2,1)}, u32[]{:S(2)}, u32[]{:S(2)}) %all-to-all-start.1) | async-done | bytes 6635552 | tf_op jit(solution)/shard_map/all_to_all | solution.py:349
  180.4 13.2 %ffn_part1.1 = (bf16[16,4,24,2880]{3,2,1,0:T(8,128)(2,1)}, bf16[2880,768]{1,0:T(8,128)(2,1)S(1)}, bf16[2880,768]{1,0:T(8,128)(2,1)S(1)}, bf16[2880,768]{1,0:T(8,128)(2,1)S(1)}) custom-call(s32[5]{0:T(128)} %copy-done.6, bf16[16,3,24,2880]{3,2,1,0:T(8,128)(2,1)} %bitcast.14.x_ref, bf16[1,2880,768]{2,1,0:T(8,128)(2,1)} %g_hbm.3, ...), custom_call_target="tpu_custom_call", output_to_operand_aliasing={{0}: (5, {})} | custom-call | flops 5096079360 | bytes 18000000 | tf_op jit(solution)/shard_map/ffn_part1/pallas_call | solution.py:191
  198.2 15.0 %ffn_part2.1 = bf16[16,4,24,2880]{3,2,1,0:T(8,128)(2,1)} custom-call(s32[5]{0:T(128)S(1)} %copy-done.8, bf16[16,3,24,2880]{3,2,1,0:T(8,128)(2,1)} %bitcast.14.x_ref, bf16[2880,768]{1,0:T(8,128)(2,1)S(1)} %get-tuple-element.20.g_ref, bf16[2880,768]{1,0:T(8,128)(2,1)S(1)} %get-tuple-element.21.u_ref, ...), custom_call_target="tpu_custom_call", output_to_operand_aliasing={{}: (5, {})} | custom-call | flops 5096079360 | bytes 18000000 | tf_op jit(solution)/shard_map/ffn_part2/pallas_call | solution.py:191
  213.9 10.6 %all-to-all-start.2 = ((bf16[64,24,2880]{2,1,0:T(8,128)(2,1)}), bf16[64,24,2880]{2,1,0:T(8,128)(2,1)}, u32[]{:S(2)}, u32[]{:S(2)}) async-start(bf16[64,24,2880]{2,1,0:T(8,128)(2,1)} %bitcast.64), calls=%async_computation.2 | async-start | bytes 18087936 | tf_op jit(solution)/shard_map/all_to_all | solution.py:371
  225.3 142.5 %all-gather.2.cloned.1.call-done = bf16[5760,128]{1,0:T(8,128)(2,1)} async-done(((bf16[720,128]{1,0:T(8,128)(2,1)}), bf16[5760,128]{1,0:T(8,128)(2,1)}) %all-gather.2.cloned.1.call-update) | async-done | bytes 1474576 | tf_op jit(solution)/shard_map/all_gather | solution.py:367
  367.8 2.8 collective-permute-start.16
  375.0 3.5 spread.1
  378.5 7.7 %combine.1 = (f32[2880,128]{1,0:T(8,128)S(1)}, bf16[2880,128]{1,0:T(8,128)(2,1)S(1)}) custom-call(s32[5]{0:T(128)S(1)} %copy-done.8, bf16[2,768,2880]{2,1,0:T(8,128)(2,1)} %bitcast.29.y_ref, bf16[16,128]{1,0:T(8,128)(2,1)S(1)} %slice.41.own_tail_ref, bf16[16,128]{1,0:T(8,128)(2,1)S(1)} %slice.42.sib_tail_ref, f32[2880,512]{1,0:T(8,128)} %bitcast.66), custom_call_target="tpu_custom_call" | custom-call | flops 2264924160 | bytes 12000000 | tf_op jit(solution)/shard_map/combine/pallas_call | solution.py:245
  (73 shorter events, 36.8 us)
Async XLA Ops:
  11.4 5.2 %collective-permute-start.7 = (bf16[2896,128]{1,0:T(8,128)(2,1)S(1)}, bf16[2896,128]{1,0:T(8,128)(2,1)S(1)}, u32[]{:S(2)}, u32[]{:S(2)}) collective-permute-start(bf16[2896,128]{1,0:T(8,128)(2,1)S(1)} %place.1.own_ref), channel_id=1, source_target_pairs={{0,8},{8,0},{1,9},{9,1},{2,10},{10,2},{3,11},{11,3},{4,12},{12,4},... | collective-permute-start | bytes 2224136 | tf_op jit(solution)/shard_map/ppermute | solution.py:340
  12.1 21.2 %collective-permute-start = (bf16[2896,128]{1,0:T(8,128)(2,1)S(1)}, bf16[2896,128]{1,0:T(8,128)(2,1)S(1)}, u32[]{:S(2)}, u32[]{:S(2)}) collective-permute-start(bf16[2896,128]{1,0:T(8,128)(2,1)S(1)} %place.1.own_ref), channel_id=1, source_target_pairs={{0,6},{2,0},{4,2},{6,4},{1,7},{3,1},{5,3},{7,5},{8,14},{10,8},{12,... | collective-permute-start | bytes 2224136 | tf_op jit(solution)/shard_map/ppermute | solution.py:323
  14.9 19.0 %collective-permute-start.4 = (bf16[2896,128]{1,0:T(8,128)(2,1)S(1)}, bf16[2896,128]{1,0:T(8,128)(2,1)S(1)}, u32[]{:S(2)}, u32[]{:S(2)}) collective-permute-start(bf16[2896,128]{1,0:T(8,128)(2,1)S(1)} %place.1.own_ref), channel_id=1, source_target_pairs={{0,2},{2,4},{4,6},{6,0},{1,3},{3,5},{5,7},{7,1},{8,10},{10,12},{12... | collective-permute-start | bytes 2224136 | tf_op jit(solution)/shard_map/ppermute | solution.py:323
  14.9 18.4 %collective-permute-start.6 = (bf16[2880,128]{1,0:T(8,128)(2,1)}, bf16[2880,128]{1,0:T(8,128)(2,1)}, u32[]{:S(2)}, u32[]{:S(2)}) collective-permute-start(bf16[2880,128]{1,0:T(8,128)(2,1)} %bitcast.72), channel_id=1, source_target_pairs={{0,1},{1,0},{2,3},{3,2},{4,5},{5,4},{6,7},{7,6},{8,9},{9,8},{10,11... | collective-permute-start | bytes 2211848 | tf_op jit(solution)/shard_map/ppermute | solution.py:339
  16.6 48.5 %copy-start.6 = (s32[5]{0:T(128)}, s32[5]{0:T(128)S(1)}, u32[]{:S(2)}) copy-start(s32[5]{0:T(128)S(1)} %stack.32.at_ref) | copy-start | bytes 64
  33.9 42.0 %all-to-all-start = ((bf16[16,24,2880]{2,1,0:T(8,128)(2,1)}), bf16[16,24,2880]{2,1,0:T(8,128)(2,1)}, u32[]{:S(2)}, u32[]{:S(2)}) async-start(bf16[16,24,2880]{2,1,0:T(8,128)(2,1)} %bitcast.12), calls=%async_computation | async-start | bytes 4521984 | tf_op jit(solution)/shard_map/all_to_all | solution.py:343
  41.7 18.0 %collective-permute-start.2 = (bf16[2896,128]{1,0:T(8,128)(2,1)S(1)}, bf16[2896,128]{1,0:T(8,128)(2,1)S(1)}, u32[]{:S(2)}, u32[]{:S(2)}) collective-permute-start(bf16[2896,128]{1,0:T(8,128)(2,1)S(1)} %place.1.own_ref), channel_id=1, source_target_pairs={{0,4},{2,6},{4,0},{6,2},{1,5},{3,7},{5,1},{7,3},{8,12},{10,14},{12... | collective-permute-start | bytes 2224136 | tf_op jit(solution)/shard_map/ppermute | solution.py:323
  42.1 21.6 %collective-permute-start.1 = (bf16[2896,128]{1,0:T(8,128)(2,1)S(1)}, bf16[2896,128]{1,0:T(8,128)(2,1)S(1)}, u32[]{:S(2)}, u32[]{:S(2)}) collective-permute-start(bf16[2896,128]{1,0:T(8,128)(2,1)S(1)} %collective-permute-done.refs_0_), channel_id=1, source_target_pairs={{0,8},{8,0},{1,9},{9,1},{2,10},{10,2},{3,11},{11,3},{4,12},{12,4},... | collective-permute-start | bytes 2224136 | tf_op jit(solution)/shard_map/ppermute | solution.py:346
  59.7 4.4 %collective-permute-start.3 = (bf16[2896,128]{1,0:T(8,128)(2,1)S(1)}, bf16[2896,128]{1,0:T(8,128)(2,1)S(1)}, u32[]{:S(2)}, u32[]{:S(2)}) collective-permute-start(bf16[2896,128]{1,0:T(8,128)(2,1)S(1)} %collective-permute-done.2.refs_2_), channel_id=1, source_target_pairs={{0,8},{8,0},{1,9},{9,1},{2,10},{10,2},{3,11},{11,3},{4,12},{12,4},... | collective-permute-start | bytes 2224136 | tf_op jit(solution)/shard_map/ppermute | solution.py:346
  62.2 2.9 collective-permute-start.5
  75.9 104.5 %all-to-all-start.1 = ((bf16[16,72,2880]{2,1,0:T(8,128)(2,1)}), bf16[16,72,2880]{2,1,0:T(8,128)(2,1)}, u32[]{:S(2)}, u32[]{:S(2)}) async-start(bf16[16,72,2880]{2,1,0:T(8,128)(2,1)} %bitcast.65), calls=%async_computation.1 | async-start | bytes 13565952 | tf_op jit(solution)/shard_map/all_to_all | solution.py:349
  80.8 31.0 %collective-permute-start.8 = (bf16[2,2880,128]{2,1,0:T(8,128)(2,1)S(1)}, bf16[2,2880,128]{2,1,0:T(8,128)(2,1)S(1)}, u32[]{:S(2)}, u32[]{:S(2)}) collective-permute-start(bf16[2,2880,128]{2,1,0:T(8,128)(2,1)S(1)} %pad_maximum_fusion.p0_ref), channel_id=1, source_target_pairs={{0,6},{2,0},{4,2},{6,4},{1,7},{3,1},{5,3},{7,5},{8,14},{10,8},{12,... | collective-permute-start | bytes 4423688 | tf_op jit(solution)/shard_map/ppermute | solution.py:323
  81.8 32.3 %collective-permute-start.9 = (bf16[2,2880,128]{2,1,0:T(8,128)(2,1)S(1)}, bf16[2,2880,128]{2,1,0:T(8,128)(2,1)}, u32[]{:S(2)}, u32[]{:S(2)}) collective-permute-start(bf16[2,2880,128]{2,1,0:T(8,128)(2,1)S(1)} %pad_maximum_fusion.p0_ref), channel_id=1, source_target_pairs={{0,4},{2,6},{4,0},{6,2},{1,5},{3,7},{5,1},{7,3},{8,12},{10,14},{12... | collective-permute-start | bytes 4423688 | tf_op jit(solution)/shard_map/ppermute | solution.py:323
  82.0 67.0 %collective-permute-start.10 = (bf16[2,2880,128]{2,1,0:T(8,128)(2,1)S(1)}, bf16[2,2880,128]{2,1,0:T(8,128)(2,1)}, u32[]{:S(2)}, u32[]{:S(2)}) collective-permute-start(bf16[2,2880,128]{2,1,0:T(8,128)(2,1)S(1)} %pad_maximum_fusion.p0_ref), channel_id=1, source_target_pairs={{0,2},{2,4},{4,6},{6,0},{1,3},{3,5},{5,7},{7,1},{8,10},{10,12},{12... | collective-permute-start | bytes 4423688 | tf_op jit(solution)/shard_map/ppermute | solution.py:323
  82.5 66.5 %copy-start.7 = (s32[5]{0:T(128)S(1)}, s32[5]{0:T(128)}, u32[]{:S(2)}) copy-start(s32[5]{0:T(128)} %copy-done.6) | copy-start | bytes 64
  160.1 3.9 collective-permute-start.11
  167.4 26.2 %collective-permute-start.12 = (bf16[1440,128]{1,0:T(8,128)(2,1)S(1)}, bf16[1440,128]{1,0:T(8,128)(2,1)S(1)}, u32[]{:S(2)}, u32[]{:S(2)}) collective-permute-start(bf16[1440,128]{1,0:T(8,128)(2,1)S(1)} %get-tuple-element.38), channel_id=1, source_target_pairs={{0,32},{32,64},{64,96},{96,0},{1,33},{33,65},{65,97},{97,1},{2,34}... | collective-permute-start | bytes 1105928 | tf_op jit(solution)/shard_map/ppermute | solution.py:357
  168.4 27.2 %collective-permute-start.13 = (bf16[1440,128]{1,0:T(8,128)(2,1)S(1)}, bf16[1440,128]{1,0:T(8,128)(2,1)S(1)}, u32[]{:S(2)}, u32[]{:S(2)}) collective-permute-start(bf16[1440,128]{1,0:T(8,128)(2,1)S(1)} %get-tuple-element.37), channel_id=1, source_target_pairs={{0,64},{32,96},{64,0},{96,32},{1,65},{33,97},{65,1},{97,33},{2,66}... | collective-permute-start | bytes 1105928 | tf_op jit(solution)/shard_map/ppermute | solution.py:357
  169.4 26.2 %collective-permute-start.14 = (bf16[1440,128]{1,0:T(8,128)(2,1)S(1)}, bf16[1440,128]{1,0:T(8,128)(2,1)S(1)}, u32[]{:S(2)}, u32[]{:S(2)}) collective-permute-start(bf16[1440,128]{1,0:T(8,128)(2,1)S(1)} %get-tuple-element.36), channel_id=1, source_target_pairs={{0,96},{32,0},{64,32},{96,64},{1,97},{33,1},{65,33},{97,65},{2,98}... | collective-permute-start | bytes 1105928 | tf_op jit(solution)/shard_map/ppermute | solution.py:357
  196.9 16.3 %collective-permute-start.15 = (bf16[720,128]{1,0:T(8,128)(2,1)S(1)}, bf16[720,128]{1,0:T(8,128)(2,1)S(1)}, u32[]{:S(2)}, u32[]{:S(2)}) collective-permute-start(bf16[720,128]{1,0:T(8,128)(2,1)S(1)} %fusion.5), channel_id=1, source_target_pairs={{0,16},{16,0},{1,17},{17,1},{2,18},{18,2},{3,19},{19,3},{4,20},{20... | collective-permute-start | bytes 552968 | tf_op jit(solution)/shard_map/ppermute | solution.py:364
  213.9 164.5 %all-to-all-start.2 = ((bf16[64,24,2880]{2,1,0:T(8,128)(2,1)}), bf16[64,24,2880]{2,1,0:T(8,128)(2,1)}, u32[]{:S(2)}, u32[]{:S(2)}) async-start(bf16[64,24,2880]{2,1,0:T(8,128)(2,1)} %bitcast.64), calls=%async_computation.2 | async-start | bytes 18087936 | tf_op jit(solution)/shard_map/all_to_all | solution.py:371
  224.5 143.2 %all-gather.2.cloned.1.call-start = ((), (), s32[]{:S(2)}) async-start(), calls=%async_computation.3 | async-start | bytes 1658880 | tf_op jit(solution)/shard_map/all_gather | solution.py:367
  367.8 5.9 %collective-permute-start.16 = (bf16[4,1440,128]{2,1,0:T(8,128)(2,1)}, bf16[4,1440,128]{2,1,0:T(8,128)(2,1)S(1)}, u32[]{:S(2)}, u32[]{:S(2)}) collective-permute-start(bf16[4,1440,128]{2,1,0:T(8,128)(2,1)} %bitcast.58), channel_id=1, source_target_pairs={{0,8},{8,0},{1,9},{9,1},{2,10},{10,2},{3,11},{11,3},{4,12},{12,4},... | collective-permute-start | bytes 4423688 | tf_op jit(solution)/shard_map/ppermute | solution.py:368
  386.2 2.3 collective-permute-start.17
  (13 other events, 80.1 us)
Sparse Core Ops, SparseCore 0:
  228.3 139.4 all-gather.1

commit v9 on v3

--- a/solution.py
+++ b/solution.py
@@ -368,10 +368,11 @@
     (out,) = ffn_part(at, 3, far, *weights, after(out, total))
     back = after(back, out)
     block = jnp.concatenate([jnp.where(zh == 0, total, back), jnp.where(zh == 0, back, total)])
-    full = jnp.stack([block] + from_others(block, "x"))
+    blocks = from_others(block, "x")
+    full = jnp.stack([block] + blocks)
     grad = spread(at, full, core_swap(full)).reshape(2880, 512)
 
-    out = after(out, block).reshape(64, 24, 2880)
+    out = after(out, *blocks).reshape(64, 24, 2880)
     out = lax.all_to_all(out, over + ("y",), split_axis=0, concat_axis=0, tiled=True)
     own, sib = combine(at, out.reshape(2, 768, 2880), mine[2880:], sibling[2880:], grad)
     mixed = (own + core_swap(sib).astype(F32)).astype(BF)

time: 398 us -> 405 us (1.018); the launches traced: 397 us -> 397 us
    ppermute x9, waiting for transfers between devices: 218 us -> 84.3 us  [from_others(): return [shift(axis, -o, 4)(block) for o in (1, 2, 3)]]
    all_to_all x1, waiting for transfers between devices: 0.01 us -> 132 us  [local(): lax.all_to_all(out, over + ('y',), split_axis=0, concat_axis=0, tiled=True)]
  transfers between devices with their start and end apart: 25 -> 25, of which waited for: 17 -> 18; matrix products, arithmetic and copies ran while one was open for 2% -> 2% of each run, Pallas kernels for 16% -> 16%
where the time goes in v9:
time: 405 us; the launch traced here: 397 us
  waiting for transfers between devices  257 us (63%)
  Pallas kernels  69.7 us (17%)
  starting transfers between devices  50 us (12%)
  local copies, waits for them, and re-layouts  11.1 us (3%)
  other arithmetic  8.18 us (2%)
    all_to_all x1, waiting for transfers between devices, local(): lax.all_to_all(out, over + ('y',), split_axis=0, concat_axis=0, tiled=True)  132 us
    ppermute x9, waiting for transfers between devices, from_others(): return [shift(axis, -o, 4)(block) for o in (1, 2, 3)]  84.3 us
    pallas_call x4, Pallas kernels, ffn_part(): pl.pallas_call(kernel, grid_spec=pltpu.PrefetchScalarGridSpec(num_scalar_...  45.1 us
    ppermute x1, waiting for transfers between devices, local(): og_other = zl_swap(og)  14.1 us
    ppermute x9, starting transfers between devices, from_others(): return [shift(axis, -o, 4)(block) for o in (1, 2, 3)]  11.5 us
    all_to_all x1, waiting for transfers between devices, local(): far = lax.all_to_all(far, over, split_axis=0, concat_axis=0, tiled=True)  10.6 us
    unnamed x28, local copies, waits for them, and re-layouts  8.27 us
    all_to_all x1, starting transfers between devices, local(): lax.all_to_all(out, over + ('y',), split_axis=0, concat_axis=0, tiled=True)  8.12 us
  transfers between devices with their start and end apart: 25, of which 18 were waited for; matrix products, arithmetic and copies ran while one was open for 2% of the time, Pallas kernels for 16%

profile of v9, /device:TPU:5, one launch (start us, length us, event | category | flops | bytes accessed | tf_op | source)
XLA Modules:
  0.0 397.2 jit_solution(3076604088150612886)
XLA Ops:
  12.7 14.1 %collective-permute-done.6 = bf16[2880,128]{1,0:T(8,128)(2,1)} collective-permute-done((bf16[2880,128]{1,0:T(8,128)(2,1)}, bf16[2880,128]{1,0:T(8,128)(2,1)}, u32[]{:S(2)}, u32[]{:S(2)}) %collective-permute-start.6) | collective-permute-done | bytes 737312 | tf_op jit(solution)/shard_map/ppermute | solution.py:339
  27.4 7.7 %all-to-all-start = ((bf16[16,24,2880]{2,1,0:T(8,128)(2,1)}), bf16[16,24,2880]{2,1,0:T(8,128)(2,1)}, u32[]{:S(2)}, u32[]{:S(2)}) async-start(bf16[16,24,2880]{2,1,0:T(8,128)(2,1)} %bitcast.12), calls=%async_computation | async-start | bytes 4521984 | tf_op jit(solution)/shard_map/all_to_all | solution.py:343
  37.9 15.2 %collective-permute-done.2.refs_2_ = bf16[2896,128]{1,0:T(8,128)(2,1)S(1)} collective-permute-done((bf16[2896,128]{1,0:T(8,128)(2,1)S(1)}, bf16[2896,128]{1,0:T(8,128)(2,1)S(1)}, u32[]{:S(2)}, u32[]{:S(2)}) %collective-permute-start.2) | collective-permute-done | bytes 741408 | tf_op jit(solution)/shard_map/ppermute | solution.py:323
  58.6 4.7 %far_rows.1 = bf16[2,8,3,24,2880]{4,3,2,1,0:T(8,128)(2,1)} custom-call(s32[5]{0:T(128)S(1)} %stack.47.at_ref, bf16[2896,128]{1,0:T(8,128)(2,1)S(1)} %collective-permute-done.refs_0_, bf16[2896,128]{1,0:T(8,128)(2,1)S(1)} %collective-permute-done.1.refs_1_, bf16[2896,128]{1,0:T(8,128)(2,1)S(1)} %collective-permute-done.2.refs_2_, ...), custom_call_target="tpu_custom_call" | custom-call | flops 849346560 | bytes 11000000 | tf_op jit(solution)/shard_map/far_rows/pallas_call | solution.py:128
  63.3 6.1 %all-to-all-done = bf16[16,24,2880]{2,1,0:T(8,128)(2,1)} async-done(((bf16[16,24,2880]{2,1,0:T(8,128)(2,1)}), bf16[16,24,2880]{2,1,0:T(8,128)(2,1)}, u32[]{:S(2)}, u32[]{:S(2)}) %all-to-all-start) | async-done | bytes 2211872 | tf_op jit(solution)/shard_map/all_to_all | solution.py:343
  69.4 4.9 %all-to-all-start.1 = ((bf16[16,72,2880]{2,1,0:T(8,128)(2,1)}), bf16[16,72,2880]{2,1,0:T(8,128)(2,1)}, u32[]{:S(2)}, u32[]{:S(2)}) async-start(bf16[16,72,2880]{2,1,0:T(8,128)(2,1)} %bitcast.67), calls=%async_computation.1 | async-start | bytes 13565952 | tf_op jit(solution)/shard_map/all_to_all | solution.py:349
  75.9 13.3 %ffn_part0.1.into_ref = bf16[16,4,24,2880]{3,2,1,0:T(8,128)(2,1)} custom-call(s32[5]{0:T(128)} %copy-done.5, bf16[384,2880]{1,0:T(8,128)(2,1)} %bitcast.17.x_ref, bf16[1,2880,768]{2,1,0:T(8,128)(2,1)} %g_hbm.3, bf16[1,2880,768]{2,1,0:T(8,128)(2,1)} %u_hbm.3, bf16[2880,768]{1,0:T(8,128)(2,1)} %bitcast.70), custom_call_target="tpu_custom_call" | custom-call | flops 5096079360 | bytes 18000000 | tf_op jit(solution)/shard_map/ffn_part0/pallas_call | solution.py:191
  89.3 15.9 %collective-permute-done.8.p1_ref = bf16[2,2880,128]{2,1,0:T(8,128)(2,1)S(1)} collective-permute-done((bf16[2,2880,128]{2,1,0:T(8,128)(2,1)S(1)}, bf16[2,2880,128]{2,1,0:T(8,128)(2,1)S(1)}, u32[]{:S(2)}, u32[]{:S(2)}) %collective-permute-start.8) | collective-permute-done | bytes 1474592 | tf_op jit(solution)/shard_map/ppermute | solution.py:323
  107.5 35.0 %collective-permute-done.10.p3_ref = bf16[2,2880,128]{2,1,0:T(8,128)(2,1)} collective-permute-done((bf16[2,2880,128]{2,1,0:T(8,128)(2,1)S(1)}, bf16[2,2880,128]{2,1,0:T(8,128)(2,1)}, u32[]{:S(2)}, u32[]{:S(2)}) %collective-permute-start.10) | collective-permute-done | bytes 1474592 | tf_op jit(solution)/shard_map/ppermute | solution.py:323
  146.5 5.9 %local_grad.1 = bf16[2,4,1440,128]{3,2,1,0:T(8,128)(2,1)S(1)} custom-call(s32[5]{0:T(128)S(1)} %copy-done.6, bf16[2,2880,128]{2,1,0:T(8,128)(2,1)S(1)} %copy-done.2, bf16[2,2880,128]{2,1,0:T(8,128)(2,1)S(1)} %copy-done.12, bf16[2,2880,128]{2,1,0:T(8,128)(2,1)} %collective-permute-done.9.p2_ref, bf16[2,2880,128]{2,1,0:T(8,128)(2,1)} %collective-permute-done.10.p3_ref, ...), custom_call_target="tpu_custom_call" | custom-call | flops 3019898880 | bytes 10000000 | tf_op jit(solution)/shard_map/local_grad/pallas_call | solution.py:279
  154.2 3.2 collective-permute-done.11
  157.5 3.4 fusion.7
  163.3 10.6 %all-to-all-done.1 = bf16[16,72,2880]{2,1,0:T(8,128)(2,1)} async-done(((bf16[16,72,2880]{2,1,0:T(8,128)(2,1)}), bf16[16,72,2880]{2,1,0:T(8,128)(2,1)}, u32[]{:S(2)}, u32[]{:S(2)}) %all-to-all-start.1) | async-done | bytes 6635552 | tf_op jit(solution)/shard_map/all_to_all | solution.py:349
  173.8 13.2 %ffn_part1.1 = (bf16[16,4,24,2880]{3,2,1,0:T(8,128)(2,1)}, bf16[2880,768]{1,0:T(8,128)(2,1)S(1)}, bf16[2880,768]{1,0:T(8,128)(2,1)S(1)}, bf16[2880,768]{1,0:T(8,128)(2,1)S(1)}) custom-call(s32[5]{0:T(128)} %copy-done.5, bf16[16,3,24,2880]{3,2,1,0:T(8,128)(2,1)} %bitcast.14.x_ref, bf16[1,2880,768]{2,1,0:T(8,128)(2,1)} %g_hbm.3, ...), custom_call_target="tpu_custom_call", output_to_operand_aliasing={{0}: (5, {})} | custom-call | flops 5096079360 | bytes 18000000 | tf_op jit(solution)/shard_map/ffn_part1/pallas_call | solution.py:191
  191.7 9.3 %ffn_part2.1.into_ref = bf16[16,4,24,2880]{3,2,1,0:T(8,128)(2,1)} custom-call(s32[5]{0:T(128)S(1)} %copy-done.7, bf16[16,3,24,2880]{3,2,1,0:T(8,128)(2,1)} %bitcast.14.x_ref, bf16[2880,768]{1,0:T(8,128)(2,1)S(1)} %get-tuple-element.21.g_ref, bf16[2880,768]{1,0:T(8,128)(2,1)S(1)} %get-tuple-element.22.u_ref, ...), custom_call_target="tpu_custom_call", output_to_operand_aliasing={{}: (5, {})} | custom-call | flops 5096079360 | bytes 18000000 | tf_op jit(solution)/shard_map/ffn_part2/pallas_call | solution.py:191
  203.1 9.3 %ffn_part3.1 = bf16[16,4,24,2880]{3,2,1,0:T(8,128)(2,1)} custom-call(s32[5]{0:T(128)S(1)} %copy-done.7, bf16[16,3,24,2880]{3,2,1,0:T(8,128)(2,1)} %bitcast.14.x_ref, bf16[2880,768]{1,0:T(8,128)(2,1)S(1)} %get-tuple-element.21.g_ref, bf16[2880,768]{1,0:T(8,128)(2,1)S(1)} %get-tuple-element.22.u_ref, ...), custom_call_target="tpu_custom_call", output_to_operand_aliasing={{}: (5, {})} | custom-call | flops 5096079360 | bytes 18000000 | tf_op jit(solution)/shard_map/ffn_part3/pallas_call | solution.py:191
  213.6 5.5 %collective-permute-start.18 = (bf16[1440,128]{1,0:T(8,128)(2,1)S(1)}, bf16[1440,128]{1,0:T(8,128)(2,1)S(1)}, u32[]{:S(2)}, u32[]{:S(2)}) collective-permute-start(bf16[1440,128]{1,0:T(8,128)(2,1)S(1)} %get-tuple-element.42), channel_id=1, source_target_pairs={{0,64},{32,96},{64,0},{96,32},{1,65},{33,97},{65,1},{97,33},{2,66}... | collective-permute-start | bytes 1105928 | tf_op jit(solution)/shard_map/ppermute | solution.py:323
  219.1 4.0 %collective-permute-done.17 = bf16[1440,128]{1,0:T(8,128)(2,1)S(1)} collective-permute-done((bf16[1440,128]{1,0:T(8,128)(2,1)S(1)}, bf16[1440,128]{1,0:T(8,128)(2,1)S(1)}, u32[]{:S(2)}, u32[]{:S(2)}) %collective-permute-start.17) | collective-permute-done | bytes 368672 | tf_op jit(solution)/shard_map/ppermute | solution.py:323
  224.8 10.7 %collective-permute-done.19 = bf16[1440,128]{1,0:T(8,128)(2,1)S(1)} collective-permute-done((bf16[1440,128]{1,0:T(8,128)(2,1)S(1)}, bf16[1440,128]{1,0:T(8,128)(2,1)S(1)}, u32[]{:S(2)}, u32[]{:S(2)}) %collective-permute-start.19) | collective-permute-done | bytes 368672 | tf_op jit(solution)/shard_map/ppermute | solution.py:323
  235.5 8.1 %all-to-all-start.2 = ((bf16[64,24,2880]{2,1,0:T(8,128)(2,1)}), bf16[64,24,2880]{2,1,0:T(8,128)(2,1)}, u32[]{:S(2)}, u32[]{:S(2)}) async-start(bf16[64,24,2880]{2,1,0:T(8,128)(2,1)} %bitcast.66), calls=%async_computation.2 | async-start | bytes 18087936 | tf_op jit(solution)/shard_map/all_to_all | solution.py:376
  247.9 3.5 spread.1
  251.4 132.3 %all-to-all-done.2 = bf16[64,24,2880]{2,1,0:T(8,128)(2,1)} async-done(((bf16[64,24,2880]{2,1,0:T(8,128)(2,1)}), bf16[64,24,2880]{2,1,0:T(8,128)(2,1)}, u32[]{:S(2)}, u32[]{:S(2)}) %all-to-all-start.2) | async-done | bytes 8847392 | tf_op jit(solution)/shard_map/all_to_all | solution.py:376
  383.6 7.7 %combine.1 = (f32[2880,128]{1,0:T(8,128)S(1)}, bf16[2880,128]{1,0:T(8,128)(2,1)S(1)}) custom-call(s32[5]{0:T(128)S(1)} %copy-done.7, bf16[2,768,2880]{2,1,0:T(8,128)(2,1)} %bitcast.29.y_ref, bf16[16,128]{1,0:T(8,128)(2,1)S(1)} %slice.41.own_tail_ref, bf16[16,128]{1,0:T(8,128)(2,1)S(1)} %slice.42.sib_tail_ref, f32[2880,512]{1,0:T(8,128)} %bitcast.68), custom_call_target="tpu_custom_call" | custom-call | flops 2264924160 | bytes 12000000 | tf_op jit(solution)/shard_map/combine/pallas_call | solution.py:245
  391.3 3.0 collective-permute-start.21
  (80 shorter events, 49.8 us)
Async XLA Ops:
  4.8 5.2 %collective-permute-start.7 = (bf16[2896,128]{1,0:T(8,128)(2,1)S(1)}, bf16[2896,128]{1,0:T(8,128)(2,1)S(1)}, u32[]{:S(2)}, u32[]{:S(2)}) collective-permute-start(bf16[2896,128]{1,0:T(8,128)(2,1)S(1)} %place.1.own_ref), channel_id=1, source_target_pairs={{0,8},{8,0},{1,9},{9,1},{2,10},{10,2},{3,11},{11,3},{4,12},{12,4},... | collective-permute-start | bytes 2224136 | tf_op jit(solution)/shard_map/ppermute | solution.py:340
  5.6 21.2 %collective-permute-start = (bf16[2896,128]{1,0:T(8,128)(2,1)S(1)}, bf16[2896,128]{1,0:T(8,128)(2,1)S(1)}, u32[]{:S(2)}, u32[]{:S(2)}) collective-permute-start(bf16[2896,128]{1,0:T(8,128)(2,1)S(1)} %place.1.own_ref), channel_id=1, source_target_pairs={{0,6},{2,0},{4,2},{6,4},{1,7},{3,1},{5,3},{7,5},{8,14},{10,8},{12,... | collective-permute-start | bytes 2224136 | tf_op jit(solution)/shard_map/ppermute | solution.py:323
  8.4 19.0 %collective-permute-start.4 = (bf16[2896,128]{1,0:T(8,128)(2,1)S(1)}, bf16[2896,128]{1,0:T(8,128)(2,1)S(1)}, u32[]{:S(2)}, u32[]{:S(2)}) collective-permute-start(bf16[2896,128]{1,0:T(8,128)(2,1)S(1)} %place.1.own_ref), channel_id=1, source_target_pairs={{0,2},{2,4},{4,6},{6,0},{1,3},{3,5},{5,7},{7,1},{8,10},{10,12},{12... | collective-permute-start | bytes 2224136 | tf_op jit(solution)/shard_map/ppermute | solution.py:323
  8.4 18.4 %collective-permute-start.6 = (bf16[2880,128]{1,0:T(8,128)(2,1)}, bf16[2880,128]{1,0:T(8,128)(2,1)}, u32[]{:S(2)}, u32[]{:S(2)}) collective-permute-start(bf16[2880,128]{1,0:T(8,128)(2,1)} %bitcast.9), channel_id=1, source_target_pairs={{0,1},{1,0},{2,3},{3,2},{4,5},{5,4},{6,7},{7,6},{8,9},{9,8},{10,11... | collective-permute-start | bytes 2211848 | tf_op jit(solution)/shard_map/ppermute | solution.py:339
  27.4 42.0 %all-to-all-start = ((bf16[16,24,2880]{2,1,0:T(8,128)(2,1)}), bf16[16,24,2880]{2,1,0:T(8,128)(2,1)}, u32[]{:S(2)}, u32[]{:S(2)}) async-start(bf16[16,24,2880]{2,1,0:T(8,128)(2,1)} %bitcast.12), calls=%async_computation | async-start | bytes 4521984 | tf_op jit(solution)/shard_map/all_to_all | solution.py:343
  35.1 18.0 %collective-permute-start.2 = (bf16[2896,128]{1,0:T(8,128)(2,1)S(1)}, bf16[2896,128]{1,0:T(8,128)(2,1)S(1)}, u32[]{:S(2)}, u32[]{:S(2)}) collective-permute-start(bf16[2896,128]{1,0:T(8,128)(2,1)S(1)} %place.1.own_ref), channel_id=1, source_target_pairs={{0,4},{2,6},{4,0},{6,2},{1,5},{3,7},{5,1},{7,3},{8,12},{10,14},{12... | collective-permute-start | bytes 2224136 | tf_op jit(solution)/shard_map/ppermute | solution.py:323
  35.5 21.6 %collective-permute-start.1 = (bf16[2896,128]{1,0:T(8,128)(2,1)S(1)}, bf16[2896,128]{1,0:T(8,128)(2,1)S(1)}, u32[]{:S(2)}, u32[]{:S(2)}) collective-permute-start(bf16[2896,128]{1,0:T(8,128)(2,1)S(1)} %collective-permute-done.refs_0_), channel_id=1, source_target_pairs={{0,8},{8,0},{1,9},{9,1},{2,10},{10,2},{3,11},{11,3},{4,12},{12,4},... | collective-permute-start | bytes 2224136 | tf_op jit(solution)/shard_map/ppermute | solution.py:346
  53.1 4.4 %collective-permute-start.3 = (bf16[2896,128]{1,0:T(8,128)(2,1)S(1)}, bf16[2896,128]{1,0:T(8,128)(2,1)S(1)}, u32[]{:S(2)}, u32[]{:S(2)}) collective-permute-start(bf16[2896,128]{1,0:T(8,128)(2,1)S(1)} %collective-permute-done.2.refs_2_), channel_id=1, source_target_pairs={{0,8},{8,0},{1,9},{9,1},{2,10},{10,2},{3,11},{11,3},{4,12},{12,4},... | collective-permute-start | bytes 2224136 | tf_op jit(solution)/shard_map/ppermute | solution.py:346
  69.4 104.5 %all-to-all-start.1 = ((bf16[16,72,2880]{2,1,0:T(8,128)(2,1)}), bf16[16,72,2880]{2,1,0:T(8,128)(2,1)}, u32[]{:S(2)}, u32[]{:S(2)}) async-start(bf16[16,72,2880]{2,1,0:T(8,128)(2,1)} %bitcast.67), calls=%async_computation.1 | async-start | bytes 13565952 | tf_op jit(solution)/shard_map/all_to_all | solution.py:349
  74.2 31.0 %collective-permute-start.8 = (bf16[2,2880,128]{2,1,0:T(8,128)(2,1)S(1)}, bf16[2,2880,128]{2,1,0:T(8,128)(2,1)S(1)}, u32[]{:S(2)}, u32[]{:S(2)}) collective-permute-start(bf16[2,2880,128]{2,1,0:T(8,128)(2,1)S(1)} %pad_maximum_fusion.p0_ref), channel_id=1, source_target_pairs={{0,6},{2,0},{4,2},{6,4},{1,7},{3,1},{5,3},{7,5},{8,14},{10,8},{12,... | collective-permute-start | bytes 4423688 | tf_op jit(solution)/shard_map/ppermute | solution.py:323
  75.3 32.3 %collective-permute-start.9 = (bf16[2,2880,128]{2,1,0:T(8,128)(2,1)S(1)}, bf16[2,2880,128]{2,1,0:T(8,128)(2,1)}, u32[]{:S(2)}, u32[]{:S(2)}) collective-permute-start(bf16[2,2880,128]{2,1,0:T(8,128)(2,1)S(1)} %pad_maximum_fusion.p0_ref), channel_id=1, source_target_pairs={{0,4},{2,6},{4,0},{6,2},{1,5},{3,7},{5,1},{7,3},{8,12},{10,14},{12... | collective-permute-start | bytes 4423688 | tf_op jit(solution)/shard_map/ppermute | solution.py:323
  75.5 67.0 %collective-permute-start.10 = (bf16[2,2880,128]{2,1,0:T(8,128)(2,1)S(1)}, bf16[2,2880,128]{2,1,0:T(8,128)(2,1)}, u32[]{:S(2)}, u32[]{:S(2)}) collective-permute-start(bf16[2,2880,128]{2,1,0:T(8,128)(2,1)S(1)} %pad_maximum_fusion.p0_ref), channel_id=1, source_target_pairs={{0,2},{2,4},{4,6},{6,0},{1,3},{3,5},{5,7},{7,1},{8,10},{10,12},{12... | collective-permute-start | bytes 4423688 | tf_op jit(solution)/shard_map/ppermute | solution.py:323
  153.7 3.8 collective-permute-start.11
  160.9 26.1 %collective-permute-start.12 = (bf16[1440,128]{1,0:T(8,128)(2,1)S(1)}, bf16[1440,128]{1,0:T(8,128)(2,1)S(1)}, u32[]{:S(2)}, u32[]{:S(2)}) collective-permute-start(bf16[1440,128]{1,0:T(8,128)(2,1)S(1)} %get-tuple-element.40), channel_id=1, source_target_pairs={{0,32},{32,64},{64,96},{96,0},{1,33},{33,65},{65,97},{97,1},{2,34}... | collective-permute-start | bytes 1105928 | tf_op jit(solution)/shard_map/ppermute | solution.py:357
  161.9 27.2 %collective-permute-start.13 = (bf16[1440,128]{1,0:T(8,128)(2,1)S(1)}, bf16[1440,128]{1,0:T(8,128)(2,1)S(1)}, u32[]{:S(2)}, u32[]{:S(2)}) collective-permute-start(bf16[1440,128]{1,0:T(8,128)(2,1)S(1)} %get-tuple-element.39), channel_id=1, source_target_pairs={{0,64},{32,96},{64,0},{96,32},{1,65},{33,97},{65,1},{97,33},{2,66}... | collective-permute-start | bytes 1105928 | tf_op jit(solution)/shard_map/ppermute | solution.py:357
  162.8 26.2 %collective-permute-start.14 = (bf16[1440,128]{1,0:T(8,128)(2,1)S(1)}, bf16[1440,128]{1,0:T(8,128)(2,1)S(1)}, u32[]{:S(2)}, u32[]{:S(2)}) collective-permute-start(bf16[1440,128]{1,0:T(8,128)(2,1)S(1)} %get-tuple-element.38), channel_id=1, source_target_pairs={{0,96},{32,0},{64,32},{96,64},{1,97},{33,1},{65,33},{97,65},{2,98}... | collective-permute-start | bytes 1105928 | tf_op jit(solution)/shard_map/ppermute | solution.py:357
  190.4 10.6 %collective-permute-start.15 = (bf16[720,128]{1,0:T(8,128)(2,1)S(1)}, bf16[720,128]{1,0:T(8,128)(2,1)S(1)}, u32[]{:S(2)}, u32[]{:S(2)}) collective-permute-start(bf16[720,128]{1,0:T(8,128)(2,1)S(1)} %fusion.5), channel_id=1, source_target_pairs={{0,16},{16,0},{1,17},{17,1},{2,18},{18,2},{3,19},{19,3},{4,20},{20... | collective-permute-start | bytes 552968 | tf_op jit(solution)/shard_map/ppermute | solution.py:364
  201.0 11.4 %collective-permute-start.16 = (bf16[720,128]{1,0:T(8,128)(2,1)S(1)}, bf16[720,128]{1,0:T(8,128)(2,1)S(1)}, u32[]{:S(2)}, u32[]{:S(2)}) collective-permute-start(bf16[720,128]{1,0:T(8,128)(2,1)S(1)} %fusion.4), channel_id=1, source_target_pairs={{0,16},{16,0},{1,17},{17,1},{2,18},{18,2},{3,19},{19,3},{4,20},{20... | collective-permute-start | bytes 552968 | tf_op jit(solution)/shard_map/ppermute | solution.py:367
  212.5 10.7 %collective-permute-start.17 = (bf16[1440,128]{1,0:T(8,128)(2,1)S(1)}, bf16[1440,128]{1,0:T(8,128)(2,1)S(1)}, u32[]{:S(2)}, u32[]{:S(2)}) collective-permute-start(bf16[1440,128]{1,0:T(8,128)(2,1)S(1)} %get-tuple-element.42), channel_id=1, source_target_pairs={{0,96},{32,0},{64,32},{96,64},{1,97},{33,1},{65,33},{97,65},{2,98}... | collective-permute-start | bytes 1105928 | tf_op jit(solution)/shard_map/ppermute | solution.py:323
  213.6 11.1 %collective-permute-start.18 = (bf16[1440,128]{1,0:T(8,128)(2,1)S(1)}, bf16[1440,128]{1,0:T(8,128)(2,1)S(1)}, u32[]{:S(2)}, u32[]{:S(2)}) collective-permute-start(bf16[1440,128]{1,0:T(8,128)(2,1)S(1)} %get-tuple-element.42), channel_id=1, source_target_pairs={{0,64},{32,96},{64,0},{96,32},{1,65},{33,97},{65,1},{97,33},{2,66}... | collective-permute-start | bytes 1105928 | tf_op jit(solution)/shard_map/ppermute | solution.py:323
  219.1 16.3 %collective-permute-start.19 = (bf16[1440,128]{1,0:T(8,128)(2,1)S(1)}, bf16[1440,128]{1,0:T(8,128)(2,1)S(1)}, u32[]{:S(2)}, u32[]{:S(2)}) collective-permute-start(bf16[1440,128]{1,0:T(8,128)(2,1)S(1)} %get-tuple-element.42), channel_id=1, source_target_pairs={{0,32},{32,64},{64,96},{96,0},{1,33},{33,65},{65,97},{97,1},{2,34}... | collective-permute-start | bytes 1105928 | tf_op jit(solution)/shard_map/ppermute | solution.py:323
  235.5 148.2 %all-to-all-start.2 = ((bf16[64,24,2880]{2,1,0:T(8,128)(2,1)}), bf16[64,24,2880]{2,1,0:T(8,128)(2,1)}, u32[]{:S(2)}, u32[]{:S(2)}) async-start(bf16[64,24,2880]{2,1,0:T(8,128)(2,1)} %bitcast.66), calls=%async_computation.2 | async-start | bytes 18087936 | tf_op jit(solution)/shard_map/all_to_all | solution.py:376
  243.8 4.1 %collective-permute-start.20 = (bf16[4,1440,128]{2,1,0:T(8,128)(2,1)S(1)}, bf16[4,1440,128]{2,1,0:T(8,128)(2,1)S(1)}, u32[]{:S(2)}, u32[]{:S(2)}) collective-permute-start(bf16[4,1440,128]{2,1,0:T(8,128)(2,1)S(1)} %pad_maximum_fusion.1.own_ref), channel_id=1, source_target_pairs={{0,8},{8,0},{1,9},{9,1},{2,10},{10,2},{3,11},{11,3},{4,12},{12,4},... | collective-permute-start | bytes 4423688 | tf_op jit(solution)/shard_map/ppermute | solution.py:373
  391.3 4.8 %collective-permute-start.21 = (bf16[2880,128]{1,0:T(8,128)(2,1)S(1)}, bf16[2880,128]{1,0:T(8,128)(2,1)S(1)}, u32[]{:S(2)}, u32[]{:S(2)}) collective-permute-start(bf16[2880,128]{1,0:T(8,128)(2,1)S(1)} %get-tuple-element.35), channel_id=1, source_target_pairs={{0,8},{8,0},{1,9},{9,1},{2,10},{10,2},{3,11},{11,3},{4,12},{12,4},... | collective-permute-start | bytes 2211848 | tf_op jit(solution)/shard_map/ppermute | solution.py:378
  (15 other events, 180.1 us)

commit v10 on v8

--- a/solution.py
+++ b/solution.py
@@ -365,11 +365,12 @@
     (out,) = ffn_part(at, 2, far, *weights, after(out, gone))
     total = (kept + after(came, out).astype(F32)).astype(BF)
     full = lax.all_gather(after(total, out), ("x", "zh"), axis=0, tiled=True).reshape(4, 1440, 128)
-    grad = spread(at, full, core_swap(full)).reshape(2880, 512)
 
     out = after(out, total).reshape(64, 24, 2880)
     out = lax.all_to_all(out, over + ("y",), split_axis=0, concat_axis=0, tiled=True)
-    own, sib = combine(at, out.reshape(2, 768, 2880), mine[2880:], sibling[2880:], grad)
+    own, sib = combine(at, out.reshape(2, 768, 2880), mine[2880:], sibling[2880:], mine)
+    full = after(full, own, sib)
+    grad = spread(at, full, core_swap(full)).reshape(2880, 512)
     mixed = (own + core_swap(sib).astype(F32)).astype(BF)
     return mixed.T, grad.T
 

time: 399 us -> 399 us (level)
  waiting for transfers between devices: 252 us -> 244 us
  starting transfers between devices: 42.9 us -> 50.2 us
    all_gather x1, waiting for transfers between devices: 143 us -> 0.01 us  [local(): lax.all_gather(after(total, out), ('x', 'zh'), axis=0, tiled=True)]
    all_to_all x1, waiting for transfers between devices: 0.01 us -> 138 us  [local(): lax.all_to_all(out, over + ('y',), split_axis=0, concat_axis=0, tiled=True)]
    ppermute x1, starting transfers between devices: 0.45 us -> 6.69 us  [local(): mixed = (own + core_swap(sib).astype(F32)).astype(BF)]
    unnamed x30 -> x26, local copies, waits for them, and re-layouts: 9.64 us -> 10.5 us
  transfers between devices with their start and end apart: 22 -> 22, of which waited for: 15 -> 14; matrix products, arithmetic and copies ran while one was open for 2% -> 2% of each run, Pallas kernels for 15% -> 16%
where the time goes in v10:
time: 399 us; the launch traced here: 397 us
  waiting for transfers between devices  244 us (61%)
  Pallas kernels  67.4 us (17%)
  starting transfers between devices  50.2 us (13%)
  between operations  14.2 us (4%)
  local copies, waits for them, and re-layouts  12.7 us (3%)
  other arithmetic  8.64 us (2%)
    all_to_all x1, waiting for transfers between devices, local(): lax.all_to_all(out, over + ('y',), split_axis=0, concat_axis=0, tiled=True)  138 us
    ppermute x6, waiting for transfers between devices, from_others(): return [shift(axis, -o, 4)(block) for o in (1, 2, 3)]  68.1 us
    pallas_call x3, Pallas kernels, ffn_part(): pl.pallas_call(kernel, grid_spec=pltpu.PrefetchScalarGridSpec(num_scalar_...  41.8 us
    ppermute x1, waiting for transfers between devices, local(): og_other = zl_swap(og)  14.1 us
    all_to_all x1, starting transfers between devices, local(): lax.all_to_all(out, over + ('y',), split_axis=0, concat_axis=0, tiled=True)  13.2 us
    unnamed x26, local copies, waits for them, and re-layouts  10.5 us
    all_to_all x1, waiting for transfers between devices, local(): far = lax.all_to_all(far, over, split_axis=0, concat_axis=0, tiled=True)  10.5 us
  transfers between devices with their start and end apart: 22, of which 14 were waited for; matrix products, arithmetic and copies ran while one was open for 2% of the time, Pallas kernels for 16%

profile of v10, /device:TPU:5, one launch (start us, length us, event | category | flops | bytes accessed | tf_op | source)
XLA Modules:
  0.0 397.1 jit_solution(17567287149672487191)
XLA Ops:
  12.1 2.7 collective-permute-start
  16.6 2.6 near_rows.1
  19.2 14.1 %collective-permute-done.6 = bf16[2880,128]{1,0:T(8,128)(2,1)S(1)} collective-permute-done((bf16[2880,128]{1,0:T(8,128)(2,1)}, bf16[2880,128]{1,0:T(8,128)(2,1)S(1)}, u32[]{:S(2)}, u32[]{:S(2)}) %collective-permute-start.6) | collective-permute-done | bytes 737312 | tf_op jit(solution)/shard_map/ppermute | solution.py:339
  34.2 7.6 %all-to-all-start = ((bf16[16,24,2880]{2,1,0:T(8,128)(2,1)}), bf16[16,24,2880]{2,1,0:T(8,128)(2,1)}, u32[]{:S(2)}, u32[]{:S(2)}) async-start(bf16[16,24,2880]{2,1,0:T(8,128)(2,1)} %bitcast.12), calls=%async_computation | async-start | bytes 4521984 | tf_op jit(solution)/shard_map/all_to_all | solution.py:343
  45.1 14.6 %collective-permute-done.2.refs_2_ = bf16[2896,128]{1,0:T(8,128)(2,1)S(1)} collective-permute-done((bf16[2896,128]{1,0:T(8,128)(2,1)S(1)}, bf16[2896,128]{1,0:T(8,128)(2,1)S(1)}, u32[]{:S(2)}, u32[]{:S(2)}) %collective-permute-start.2) | collective-permute-done | bytes 741408 | tf_op jit(solution)/shard_map/ppermute | solution.py:323
  59.7 2.6 collective-permute-start.3
  65.4 5.4 %far_rows.1 = bf16[2,8,3,24,2880]{4,3,2,1,0:T(8,128)(2,1)} custom-call(s32[5]{0:T(128)S(1)} %stack.32.at_ref, bf16[2896,128]{1,0:T(8,128)(2,1)} %collective-permute-done.refs_0_, bf16[2896,128]{1,0:T(8,128)(2,1)S(1)} %collective-permute-done.1.refs_1_, bf16[2896,128]{1,0:T(8,128)(2,1)S(1)} %collective-permute-done.2.refs_2_, ...), custom_call_target="tpu_custom_call" | custom-call | flops 849346560 | bytes 11000000 | tf_op jit(solution)/shard_map/far_rows/pallas_call | solution.py:128
  70.8 5.2 %all-to-all-done = bf16[16,24,2880]{2,1,0:T(8,128)(2,1)} async-done(((bf16[16,24,2880]{2,1,0:T(8,128)(2,1)}), bf16[16,24,2880]{2,1,0:T(8,128)(2,1)}, u32[]{:S(2)}, u32[]{:S(2)}) %all-to-all-start) | async-done | bytes 2211872 | tf_op jit(solution)/shard_map/all_to_all | solution.py:343
  76.0 4.9 %all-to-all-start.1 = ((bf16[16,72,2880]{2,1,0:T(8,128)(2,1)}), bf16[16,72,2880]{2,1,0:T(8,128)(2,1)}, u32[]{:S(2)}, u32[]{:S(2)}) async-start(bf16[16,72,2880]{2,1,0:T(8,128)(2,1)} %bitcast.65), calls=%async_computation.1 | async-start | bytes 13565952 | tf_op jit(solution)/shard_map/all_to_all | solution.py:349
  83.2 13.3 %ffn_part0.1.into_ref = bf16[16,4,24,2880]{3,2,1,0:T(8,128)(2,1)} custom-call(s32[5]{0:T(128)} %copy-done.5, bf16[384,2880]{1,0:T(8,128)(2,1)} %bitcast.17.x_ref, bf16[1,2880,768]{2,1,0:T(8,128)(2,1)} %g_hbm.3, bf16[1,2880,768]{2,1,0:T(8,128)(2,1)} %u_hbm.3, bf16[2880,768]{1,0:T(8,128)(2,1)} %bitcast.66), custom_call_target="tpu_custom_call" | custom-call | flops 5096079360 | bytes 18000000 | tf_op jit(solution)/shard_map/ffn_part0/pallas_call | solution.py:191
  96.5 15.3 %collective-permute-done.8.p1_ref = bf16[2,2880,128]{2,1,0:T(8,128)(2,1)} collective-permute-done((bf16[2,2880,128]{2,1,0:T(8,128)(2,1)S(1)}, bf16[2,2880,128]{2,1,0:T(8,128)(2,1)}, u32[]{:S(2)}, u32[]{:S(2)}) %collective-permute-start.8) | collective-permute-done | bytes 1474592 | tf_op jit(solution)/shard_map/ppermute | solution.py:323
  111.8 3.0 collective-permute-done.9.p2_ref
  114.8 34.5 %collective-permute-done.10.p3_ref = bf16[2,2880,128]{2,1,0:T(8,128)(2,1)} collective-permute-done((bf16[2,2880,128]{2,1,0:T(8,128)(2,1)S(1)}, bf16[2,2880,128]{2,1,0:T(8,128)(2,1)}, u32[]{:S(2)}, u32[]{:S(2)}) %collective-permute-start.10) | collective-permute-done | bytes 1474592 | tf_op jit(solution)/shard_map/ppermute | solution.py:323
  150.5 6.1 %local_grad.1 = bf16[2,4,1440,128]{3,2,1,0:T(8,128)(2,1)S(1)} custom-call(s32[5]{0:T(128)S(1)} %copy-done.6, bf16[2,2880,128]{2,1,0:T(8,128)(2,1)S(1)} %pad_maximum_fusion.p0_ref, bf16[2,2880,128]{2,1,0:T(8,128)(2,1)} %collective-permute-done.8.p1_ref, bf16[2,2880,128]{2,1,0:T(8,128)(2,1)} %collective-permute-done.9.p2_ref, ...), custom_call_target="tpu_custom_call" | custom-call | flops 3019898880 | bytes 10000000 | tf_op jit(solution)/shard_map/local_grad/pallas_call | solution.py:279
  160.3 3.1 collective-permute-done.11
  163.4 3.5 fusion.6
  170.0 10.5 %all-to-all-done.1 = bf16[16,72,2880]{2,1,0:T(8,128)(2,1)} async-done(((bf16[16,72,2880]{2,1,0:T(8,128)(2,1)}), bf16[16,72,2880]{2,1,0:T(8,128)(2,1)}, u32[]{:S(2)}, u32[]{:S(2)}) %all-to-all-start.1) | async-done | bytes 6635552 | tf_op jit(solution)/shard_map/all_to_all | solution.py:349
  180.4 13.3 %ffn_part1.1 = (bf16[16,4,24,2880]{3,2,1,0:T(8,128)(2,1)}, bf16[2880,768]{1,0:T(8,128)(2,1)S(1)}, bf16[2880,768]{1,0:T(8,128)(2,1)S(1)}, bf16[2880,768]{1,0:T(8,128)(2,1)S(1)}) custom-call(s32[5]{0:T(128)} %copy-done.5, bf16[16,3,24,2880]{3,2,1,0:T(8,128)(2,1)} %bitcast.14.x_ref, bf16[1,2880,768]{2,1,0:T(8,128)(2,1)} %g_hbm.3, ...), custom_call_target="tpu_custom_call", output_to_operand_aliasing={{0}: (5, {})} | custom-call | flops 5096079360 | bytes 18000000 | tf_op jit(solution)/shard_map/ffn_part1/pallas_call | solution.py:191
  200.6 15.2 %ffn_part2.1 = bf16[16,4,24,2880]{3,2,1,0:T(8,128)(2,1)} custom-call(s32[5]{0:T(128)S(1)} %copy-done.7, bf16[16,3,24,2880]{3,2,1,0:T(8,128)(2,1)} %bitcast.14.x_ref, bf16[2880,768]{1,0:T(8,128)(2,1)S(1)} %copy-done.1, bf16[2880,768]{1,0:T(8,128)(2,1)S(1)} %get-tuple-element.22.u_ref, ...), custom_call_target="tpu_custom_call", output_to_operand_aliasing={{}: (5, {})} | custom-call | flops 5096079360 | bytes 18000000 | tf_op jit(solution)/shard_map/ffn_part2/pallas_call | solution.py:191
  216.4 13.2 %all-to-all-start.2 = ((bf16[64,24,2880]{2,1,0:T(8,128)(2,1)}), bf16[64,24,2880]{2,1,0:T(8,128)(2,1)}, u32[]{:S(2)}, u32[]{:S(2)}) async-start(bf16[64,24,2880]{2,1,0:T(8,128)(2,1)} %bitcast.64), calls=%async_computation.2 | async-start | bytes 18087936 | tf_op jit(solution)/shard_map/all_to_all | solution.py:370
  230.4 137.7 %all-to-all-done.2 = bf16[64,24,2880]{2,1,0:T(8,128)(2,1)} async-done(((bf16[64,24,2880]{2,1,0:T(8,128)(2,1)}), bf16[64,24,2880]{2,1,0:T(8,128)(2,1)}, u32[]{:S(2)}, u32[]{:S(2)}) %all-to-all-start.2) | async-done | bytes 8847392 | tf_op jit(solution)/shard_map/all_to_all | solution.py:370
  368.1 7.8 %combine.1 = (f32[2880,128]{1,0:T(8,128)S(1)}, bf16[2880,128]{1,0:T(8,128)(2,1)S(1)}) custom-call(s32[5]{0:T(128)S(1)} %copy-done.7, bf16[2,768,2880]{2,1,0:T(8,128)(2,1)} %bitcast.29.y_ref, bf16[16,128]{1,0:T(8,128)(2,1)S(1)} %slice.41.own_tail_ref, bf16[16,128]{1,0:T(8,128)(2,1)S(1)} %slice.42.sib_tail_ref, bf16[2896,128]{1,0:T(8,128)(2,1)S(1)} %place.1.own_ref.ahead_ref), custom_call_target="tpu_custom_call" | custom-call | flops 2264924160 | bytes 12000000 | tf_op jit(solution)/shard_map/combine/pallas_call | solution.py:245
  375.9 6.7 %collective-permute-start.16 = (bf16[2880,128]{1,0:T(8,128)(2,1)S(1)}, bf16[2880,128]{1,0:T(8,128)(2,1)S(1)}, u32[]{:S(2)}, u32[]{:S(2)}) collective-permute-start(bf16[2880,128]{1,0:T(8,128)(2,1)S(1)} %get-tuple-element.33), channel_id=1, source_target_pairs={{0,8},{8,0},{1,9},{9,1},{2,10},{10,2},{3,11},{11,3},{4,12},{12,4},... | collective-permute-start | bytes 2211848 | tf_op jit(solution)/shard_map/ppermute | solution.py:374
  386.8 3.5 spread.1
  (69 shorter events, 36.7 us)
Async XLA Ops:
  11.4 5.2 %collective-permute-start.7 = (bf16[2896,128]{1,0:T(8,128)(2,1)S(1)}, bf16[2896,128]{1,0:T(8,128)(2,1)S(1)}, u32[]{:S(2)}, u32[]{:S(2)}) collective-permute-start(bf16[2896,128]{1,0:T(8,128)(2,1)S(1)} %place.1.own_ref.ahead_ref), channel_id=1, source_target_pairs={{0,8},{8,0},{1,9},{9,1},{2,10},{10,2},{3,11},{11,3},{4,12},{12,4},... | collective-permute-start | bytes 2224136 | tf_op jit(solution)/shard_map/ppermute | solution.py:340
  12.1 21.2 %collective-permute-start = (bf16[2896,128]{1,0:T(8,128)(2,1)S(1)}, bf16[2896,128]{1,0:T(8,128)(2,1)}, u32[]{:S(2)}, u32[]{:S(2)}) collective-permute-start(bf16[2896,128]{1,0:T(8,128)(2,1)S(1)} %place.1.own_ref.ahead_ref), channel_id=1, source_target_pairs={{0,6},{2,0},{4,2},{6,4},{1,7},{3,1},{5,3},{7,5},{8,14},{10,8},{12,... | collective-permute-start | bytes 2224136 | tf_op jit(solution)/shard_map/ppermute | solution.py:323
  14.9 19.1 %collective-permute-start.4 = (bf16[2896,128]{1,0:T(8,128)(2,1)S(1)}, bf16[2896,128]{1,0:T(8,128)(2,1)}, u32[]{:S(2)}, u32[]{:S(2)}) collective-permute-start(bf16[2896,128]{1,0:T(8,128)(2,1)S(1)} %place.1.own_ref.ahead_ref), channel_id=1, source_target_pairs={{0,2},{2,4},{4,6},{6,0},{1,3},{3,5},{5,7},{7,1},{8,10},{10,12},{12... | collective-permute-start | bytes 2224136 | tf_op jit(solution)/shard_map/ppermute | solution.py:323
  14.9 18.4 %collective-permute-start.6 = (bf16[2880,128]{1,0:T(8,128)(2,1)}, bf16[2880,128]{1,0:T(8,128)(2,1)S(1)}, u32[]{:S(2)}, u32[]{:S(2)}) collective-permute-start(bf16[2880,128]{1,0:T(8,128)(2,1)} %bitcast.71), channel_id=1, source_target_pairs={{0,1},{1,0},{2,3},{3,2},{4,5},{5,4},{6,7},{7,6},{8,9},{9,8},{10,11... | collective-permute-start | bytes 2211848 | tf_op jit(solution)/shard_map/ppermute | solution.py:339
  16.6 48.8 %copy-start.5 = (s32[5]{0:T(128)}, s32[5]{0:T(128)S(1)}, u32[]{:S(2)}) copy-start(s32[5]{0:T(128)S(1)} %stack.32.at_ref) | copy-start | bytes 64
  34.2 41.8 %all-to-all-start = ((bf16[16,24,2880]{2,1,0:T(8,128)(2,1)}), bf16[16,24,2880]{2,1,0:T(8,128)(2,1)}, u32[]{:S(2)}, u32[]{:S(2)}) async-start(bf16[16,24,2880]{2,1,0:T(8,128)(2,1)} %bitcast.12), calls=%async_computation | async-start | bytes 4521984 | tf_op jit(solution)/shard_map/all_to_all | solution.py:343
  41.7 17.9 %collective-permute-start.2 = (bf16[2896,128]{1,0:T(8,128)(2,1)S(1)}, bf16[2896,128]{1,0:T(8,128)(2,1)S(1)}, u32[]{:S(2)}, u32[]{:S(2)}) collective-permute-start(bf16[2896,128]{1,0:T(8,128)(2,1)S(1)} %place.1.own_ref.ahead_ref), channel_id=1, source_target_pairs={{0,4},{2,6},{4,0},{6,2},{1,5},{3,7},{5,1},{7,3},{8,12},{10,14},{12... | collective-permute-start | bytes 2224136 | tf_op jit(solution)/shard_map/ppermute | solution.py:323
  42.7 21.0 %collective-permute-start.1 = (bf16[2896,128]{1,0:T(8,128)(2,1)}, bf16[2896,128]{1,0:T(8,128)(2,1)S(1)}, u32[]{:S(2)}, u32[]{:S(2)}) collective-permute-start(bf16[2896,128]{1,0:T(8,128)(2,1)} %collective-permute-done.refs_0_), channel_id=1, source_target_pairs={{0,8},{8,0},{1,9},{9,1},{2,10},{10,2},{3,11},{11,3},{4,12},{12,4},... | collective-permute-start | bytes 2224136 | tf_op jit(solution)/shard_map/ppermute | solution.py:346
  59.7 5.4 %collective-permute-start.3 = (bf16[2896,128]{1,0:T(8,128)(2,1)S(1)}, bf16[2896,128]{1,0:T(8,128)(2,1)S(1)}, u32[]{:S(2)}, u32[]{:S(2)}) collective-permute-start(bf16[2896,128]{1,0:T(8,128)(2,1)S(1)} %collective-permute-done.2.refs_2_), channel_id=1, source_target_pairs={{0,8},{8,0},{1,9},{9,1},{2,10},{10,2},{3,11},{11,3},{4,12},{12,4},... | collective-permute-start | bytes 2224136 | tf_op jit(solution)/shard_map/ppermute | solution.py:346
  62.2 3.1 collective-permute-start.5
  76.0 104.5 %all-to-all-start.1 = ((bf16[16,72,2880]{2,1,0:T(8,128)(2,1)}), bf16[16,72,2880]{2,1,0:T(8,128)(2,1)}, u32[]{:S(2)}, u32[]{:S(2)}) async-start(bf16[16,72,2880]{2,1,0:T(8,128)(2,1)} %bitcast.65), calls=%async_computation.1 | async-start | bytes 13565952 | tf_op jit(solution)/shard_map/all_to_all | solution.py:349
  80.9 31.0 %collective-permute-start.8 = (bf16[2,2880,128]{2,1,0:T(8,128)(2,1)S(1)}, bf16[2,2880,128]{2,1,0:T(8,128)(2,1)}, u32[]{:S(2)}, u32[]{:S(2)}) collective-permute-start(bf16[2,2880,128]{2,1,0:T(8,128)(2,1)S(1)} %pad_maximum_fusion.p0_ref), channel_id=1, source_target_pairs={{0,6},{2,0},{4,2},{6,4},{1,7},{3,1},{5,3},{7,5},{8,14},{10,8},{12,... | collective-permute-start | bytes 4423688 | tf_op jit(solution)/shard_map/ppermute | solution.py:323
  82.5 32.3 %collective-permute-start.9 = (bf16[2,2880,128]{2,1,0:T(8,128)(2,1)S(1)}, bf16[2,2880,128]{2,1,0:T(8,128)(2,1)}, u32[]{:S(2)}, u32[]{:S(2)}) collective-permute-start(bf16[2,2880,128]{2,1,0:T(8,128)(2,1)S(1)} %pad_maximum_fusion.p0_ref), channel_id=1, source_target_pairs={{0,4},{2,6},{4,0},{6,2},{1,5},{3,7},{5,1},{7,3},{8,12},{10,14},{12... | collective-permute-start | bytes 4423688 | tf_op jit(solution)/shard_map/ppermute | solution.py:323
  82.5 66.8 %collective-permute-start.10 = (bf16[2,2880,128]{2,1,0:T(8,128)(2,1)S(1)}, bf16[2,2880,128]{2,1,0:T(8,128)(2,1)}, u32[]{:S(2)}, u32[]{:S(2)}) collective-permute-start(bf16[2,2880,128]{2,1,0:T(8,128)(2,1)S(1)} %pad_maximum_fusion.p0_ref), channel_id=1, source_target_pairs={{0,2},{2,4},{4,6},{6,0},{1,3},{3,5},{5,7},{7,1},{8,10},{10,12},{12... | collective-permute-start | bytes 4423688 | tf_op jit(solution)/shard_map/ppermute | solution.py:323
  83.2 66.1 %copy-start.6 = (s32[5]{0:T(128)S(1)}, s32[5]{0:T(128)}, u32[]{:S(2)}) copy-start(s32[5]{0:T(128)} %copy-done.5) | copy-start | bytes 64
  159.5 4.0 collective-permute-start.11
  167.7 28.1 %collective-permute-start.12 = (bf16[1440,128]{1,0:T(8,128)(2,1)}, bf16[1440,128]{1,0:T(8,128)(2,1)S(1)}, u32[]{:S(2)}, u32[]{:S(2)}) collective-permute-start(bf16[1440,128]{1,0:T(8,128)(2,1)} %get-tuple-element.40), channel_id=1, source_target_pairs={{0,32},{32,64},{64,96},{96,0},{1,33},{33,65},{65,97},{97,1},{2,34}... | collective-permute-start | bytes 1105928 | tf_op jit(solution)/shard_map/ppermute | solution.py:357
  168.6 27.2 %collective-permute-start.13 = (bf16[1440,128]{1,0:T(8,128)(2,1)S(1)}, bf16[1440,128]{1,0:T(8,128)(2,1)S(1)}, u32[]{:S(2)}, u32[]{:S(2)}) collective-permute-start(bf16[1440,128]{1,0:T(8,128)(2,1)S(1)} %get-tuple-element.39), channel_id=1, source_target_pairs={{0,64},{32,96},{64,0},{96,32},{1,65},{33,97},{65,1},{97,33},{2,66}... | collective-permute-start | bytes 1105928 | tf_op jit(solution)/shard_map/ppermute | solution.py:357
  169.7 26.1 %collective-permute-start.14 = (bf16[1440,128]{1,0:T(8,128)(2,1)S(1)}, bf16[1440,128]{1,0:T(8,128)(2,1)S(1)}, u32[]{:S(2)}, u32[]{:S(2)}) collective-permute-start(bf16[1440,128]{1,0:T(8,128)(2,1)S(1)} %get-tuple-element.38), channel_id=1, source_target_pairs={{0,96},{32,0},{64,32},{96,64},{1,97},{33,1},{65,33},{97,65},{2,98}... | collective-permute-start | bytes 1105928 | tf_op jit(solution)/shard_map/ppermute | solution.py:357
  197.2 18.5 %collective-permute-start.15 = (bf16[720,128]{1,0:T(8,128)(2,1)S(1)}, bf16[720,128]{1,0:T(8,128)(2,1)S(1)}, u32[]{:S(2)}, u32[]{:S(2)}) collective-permute-start(bf16[720,128]{1,0:T(8,128)(2,1)S(1)} %fusion.5), channel_id=1, source_target_pairs={{0,16},{16,0},{1,17},{17,1},{2,18},{18,2},{3,19},{19,3},{4,20},{20... | collective-permute-start | bytes 552968 | tf_op jit(solution)/shard_map/ppermute | solution.py:364
  216.4 151.7 %all-to-all-start.2 = ((bf16[64,24,2880]{2,1,0:T(8,128)(2,1)}), bf16[64,24,2880]{2,1,0:T(8,128)(2,1)}, u32[]{:S(2)}, u32[]{:S(2)}) async-start(bf16[64,24,2880]{2,1,0:T(8,128)(2,1)} %bitcast.64), calls=%async_computation.2 | async-start | bytes 18087936 | tf_op jit(solution)/shard_map/all_to_all | solution.py:370
  229.7 153.0 %all-gather.2.cloned.1.call-start = ((), (), s32[]{:S(2)}) async-start(), calls=%async_computation.3 | async-start | bytes 1658880 | tf_op jit(solution)/shard_map/all_gather | solution.py:367
  375.9 8.5 %collective-permute-start.16 = (bf16[2880,128]{1,0:T(8,128)(2,1)S(1)}, bf16[2880,128]{1,0:T(8,128)(2,1)S(1)}, u32[]{:S(2)}, u32[]{:S(2)}) collective-permute-start(bf16[2880,128]{1,0:T(8,128)(2,1)S(1)} %get-tuple-element.33), channel_id=1, source_target_pairs={{0,8},{8,0},{1,9},{9,1},{2,10},{10,2},{3,11},{11,3},{4,12},{12,4},... | collective-permute-start | bytes 2211848 | tf_op jit(solution)/shard_map/ppermute | solution.py:374
  382.6 4.2 %collective-permute-start.17 = (bf16[4,1440,128]{2,1,0:T(8,128)(2,1)}, bf16[4,1440,128]{2,1,0:T(8,128)(2,1)S(1)}, u32[]{:S(2)}, u32[]{:S(2)}) collective-permute-start(bf16[4,1440,128]{2,1,0:T(8,128)(2,1)} %bitcast.58), channel_id=1, source_target_pairs={{0,8},{8,0},{1,9},{9,1},{2,10},{10,2},{3,11},{11,3},{4,12},{12,4},... | collective-permute-start | bytes 4423688 | tf_op jit(solution)/shard_map/ppermute | solution.py:373
  (11 other events, 17.8 us)
Sparse Core Ops, SparseCore 0:
  233.4 140.5 all-gather.1
